TPU v7x, 512 devices: a whole 4x4x16 slice. The times are simulated.
512 devices in a mesh: section: 32 (over z, core), tensor: 16 (over x, y).
Axes of the slice: x: 4, y: 4, z: 16, core: 2. Of those that a mesh axis runs over, the one named last changes fastest.
Arguments:
- patches: bfloat16 [64, 128, 3200], P('section', 'tensor')
- plan: int32 [64], replicated, may hold values from 0 to 63, as said below
- norm_gain: float32 [3200], replicated, may hold values from 0.5 to 2
- proj_in: bfloat16 [3200, 6400], P('section', 'tensor'), may hold values from -0.109375 to 0.109375
- proj_out: bfloat16 [6400, 3200], P('tensor', 'section'), may hold values from -0.078125 to 0.078125
- layer_scale: float32 [3200], replicated, may hold values from 0.3 to 1.5
Outputs:
- delivered: bfloat16 [64, 128, 3200], P('section', 'tensor')
Inputs may be any that keep to these rules, and one draw needn't show every extreme that they name: `plan`: a permutation of the 64 block numbers; position p lies on section p // 2, block b starts on section b // 2; the 2 blocks that start on one section go to 2 different sections.
All inputs are finite; a program needn't handle non-finite values.
Results may differ from a plain program's by a relative error of at most 0.009.
Values may be sent and summed in bfloat16 or wider, within the bound.
No kernel may reach another device: no remote copies, remote signals or barrier semaphores. Data moves between devices by JAX's collectives and lax.ppermute only.
A program may use at most 64 MiB of HBM per device.

v0:
```python
import jax
import jax.numpy as jnp
from jax import lax
from jax.sharding import PartitionSpec as P


def local(patches, plan, norm_gain, proj_in, proj_out, layer_scale):
    per_section = patches.shape[0]
    width = patches.shape[2]
    values = patches.astype(jnp.float32)
    mean_square = jnp.mean(values * values, axis=-1, keepdims=True)
    normed = (values * lax.rsqrt(mean_square + 1e-06) * norm_gain).astype(jnp.bfloat16)
    gathered = lax.all_gather(normed, "tensor", axis=1, tiled=True)
    block_rows = gathered.shape[1]
    flat_rows = gathered.reshape(per_section * block_rows, width)
    summed = jnp.dot(
        flat_rows,
        lax.all_gather(proj_in, "section", axis=0, tiled=True),
        preferred_element_type=jnp.float32,
    )
    hidden = jax.nn.gelu(summed, approximate=False).astype(jnp.bfloat16)
    partial_sum = jnp.dot(
        hidden,
        lax.all_gather(proj_out, "section", axis=1, tiled=True),
        preferred_element_type=jnp.float32,
    )
    partial_sum = partial_sum.reshape(per_section, block_rows, width)
    branch = lax.psum_scatter(
        partial_sum.astype(jnp.bfloat16), "tensor", scatter_dimension=1, tiled=True
    ).astype(jnp.float32)
    encoded = (values + layer_scale * branch).astype(jnp.bfloat16)
    own_section = lax.axis_index("section")
    wanted = lax.dynamic_slice_in_dim(plan, own_section * per_section, per_section)
    everything = lax.all_gather(encoded, "section", axis=0, tiled=True)
    delivered = everything[wanted]
    return delivered


def solution(mesh):
    return jax.shard_map(
        local,
        mesh=mesh,
        in_specs=(
            P("section", "tensor", None),
            P(),
            P(),
            P("section", "tensor"),
            P("tensor", "section"),
            P(),
        ),
        out_specs=P("section", "tensor", None),
        check_vma=False,
    )
```

profile of v0, /device:TPU:6, one launch (start us, length us, event | category | flops | bytes accessed | tf_op | source)
XLA Modules:
  0.0 430.3 jit_solution(8934727876784055996)
XLA Ops:
  6.5 0.0 all-gather.11.cloned.1.call-start
  6.5 0.7 all-gather.11.cloned.1.call-update
  7.3 0.0 all-gather.13.cloned.1.call-start
  7.3 0.7 all-gather.13.cloned.1.call-update
  8.0 0.0 all-gather.7.cloned.1.call-start
  8.1 1.0 fusion.11
  9.1 1.6 fusion.13
  10.7 0.0 all-gather.7.cloned.1.call-update
  10.7 0.0 all-reduce.3.cloned.1.call-start
  10.8 76.2 %all-gather.11.cloned.1.call-done = bf16[32,100,400]{1,2,0:T(8,128)(2,1)} async-done(((bf16[1,100,400]{1,2,0:T(8,128)(2,1)}), bf16[32,100,400]{1,2,0:T(8,128)(2,1)}) %all-gather.11.cloned.1.call-update) | async-done | bytes 2560016 | tf_op jit(solution)/shard_map/all_gather | solution.py:18
  87.0 2.8 copy.9
  89.8 6.0 %reshape.26 = bf16[3200,400]{0,1:T(8,128)(2,1)} reshape(bf16[32,100,400]{1,0,2:T(8,128)(2,1)S(1)} %copy.9) | data formatting | bytes 5120000
  95.8 63.4 %all-gather.13.cloned.1.call-done = bf16[32,100,400]{1,2,0:T(8,128)(2,1)} async-done(((bf16[1,100,400]{1,2,0:T(8,128)(2,1)}), bf16[32,100,400]{1,2,0:T(8,128)(2,1)}) %all-gather.13.cloned.1.call-update) | async-done | bytes 2560016 | tf_op jit(solution)/shard_map/all_gather | solution.py:24
  159.3 2.8 copy.10
  162.0 6.0 %reshape.28 = bf16[3200,400]{0,1:T(8,128)(2,1)} reshape(bf16[32,100,400]{1,0,2:T(8,128)(2,1)S(1)} %copy.10) | data formatting | bytes 5120000
  168.1 50.3 %all-gather.7.cloned.1.call-done = bf16[2,128,3200]{2,1,0:T(8,128)(2,1)} async-done(((bf16[2,8,3200]{2,1,0:T(8,128)(2,1)}), bf16[2,128,3200]{2,1,0:T(8,128)(2,1)}) %all-gather.7.cloned.1.call-update) | async-done | bytes 1638416 | tf_op jit(solution)/shard_map/all_gather | solution.py:13
  218.4 0.0 copy-start
  218.4 0.0 copy-start.1
  218.4 0.0 copy-start.2
  218.4 8.4 %convolution_convert_fusion = bf16[256,3200]{1,0:T(8,128)(2,1)} fusion(bf16[3200,400]{0,1:T(8,128)(2,1)} %reshape.28, bf16[256,3200]{1,0:T(8,128)(2,1)} %bitcast.19, bf16[3200,400]{0,1:T(8,128)(2,1)} %reshape.26), kind=kOutput, calls=%fused_computation.1 | convolution fusion | flops 1318195200 | bytes 8396800 | tf_op jit(solution)/shard_map/dot_general | solution.py:22
  226.7 0.0 all-reduce.3.cloned.1.call-update
  226.7 0.0 all-gather.9.cloned.1.call-start
  226.8 1.3 dynamic-slice
  228.7 117.0 %all-reduce.3.cloned.1.call-done = bf16[2,128,3200]{2,1,0:T(8,128)(2,1)} async-done(((bf16[2,128,3200]{2,1,0:T(8,128)(2,1)}), bf16[2,128,3200]{2,1,0:T(8,128)(2,1)}) %all-reduce.3.cloned.1.call-update) | async-done | bytes 1638416
  345.7 0.0 copy-done
  345.7 0.0 copy-done.1
  345.7 1.6 fusion.14
  347.3 0.0 all-gather.9.cloned.1.call-update
  347.3 0.0 copy-done.2
  347.3 0.1 compare_select_fusion
  347.4 73.2 %all-gather.9.cloned.1.call-done = bf16[64,8,3200]{2,1,0:T(8,128)(2,1)} async-done(((bf16[2,8,3200]{2,1,0:T(8,128)(2,1)}), bf16[64,8,3200]{2,1,0:T(8,128)(2,1)}) %all-gather.9.cloned.1.call-update) | async-done | bytes 3276816 | tf_op jit(solution)/shard_map/all_gather | solution.py:34
  420.6 3.1 gather_fusion
  (2 shorter events, 0.0 us)
Async XLA Ops:
  6.5 80.5 %all-gather.11.cloned.1.call-start = ((), (), s32[]{:S(2)}) async-start(), calls=%async_computation.2 | async-start | bytes 3379200 | tf_op jit(solution)/shard_map/all_gather | solution.py:18
  7.3 152.0 %all-gather.13.cloned.1.call-start = ((), (), s32[]{:S(2)}) async-start(), calls=%async_computation.3 | async-start | bytes 3379200 | tf_op jit(solution)/shard_map/all_gather | solution.py:24
  8.0 210.3 %all-gather.7.cloned.1.call-start = ((), (), s32[]{:S(2)}) async-start(), calls=%async_computation | async-start | bytes 1740800 | tf_op jit(solution)/shard_map/all_gather | solution.py:13
  10.7 335.0 %all-reduce.3.cloned.1.call-start = ((), (), s32[]{:S(2)}) async-start(), calls=%async_computation.4 | async-start | bytes 3276800
  218.4 127.4 %copy-start = (bf16[2,8,3200]{2,1,0:T(8,128)(2,1)S(1)}, bf16[2,8,3200]{2,1,0:T(8,128)(2,1)}, u32[]{:S(2)}) copy-start(bf16[2,8,3200]{2,1,0:T(8,128)(2,1)} %param.6) | copy-start | bytes 307204
  218.4 127.4 %copy-start.1 = (f32[3200]{0:T(1024)S(1)}, f32[3200]{0:T(1024)}, u32[]{:S(2)}) copy-start(f32[3200]{0:T(1024)} %param.11) | copy-start | bytes 38404
  218.4 129.0 %copy-start.2 = (s32[64]{0:T(128)S(1)}, s32[64]{0:T(128)}, u32[]{:S(2)}) copy-start(s32[64]{0:T(128)} %param.7) | copy-start | bytes 772
  226.7 193.8 %all-gather.9.cloned.1.call-start = ((), (), s32[]{:S(2)}) async-start(), calls=%async_computation.1 | async-start | bytes 3379200 | tf_op jit(solution)/shard_map/all_gather | solution.py:34
Sparse Core Ops, SparseCore 0:
  9.5 77.4 all-gather.10
  89.1 70.0 all-gather.12
  162.3 55.9 all-gather.6
  226.9 118.8 all-reduce.2
  347.7 72.8 all-gather.8
where the time goes:
time: 432 us; the launch traced here: 430 us
  waiting for transfers between devices  382 us (88%)
  local copies, waits for them, and re-layouts  22 us (5%)
  between operations  13.8 us (3%)
  matrix products  8.36 us (2%)
    unnamed x6, waiting for transfers between devices  118 us
    all_gather x1, waiting for transfers between devices, local(): lax.all_gather(proj_in, 'section', axis=0, tiled=True)  76.2 us
    all_gather x1, waiting for transfers between devices, local(): everything = lax.all_gather(encoded, 'section', axis=0, tiled=True)  73.2 us
    all_gather x1, waiting for transfers between devices, local(): lax.all_gather(proj_out, 'section', axis=1, tiled=True)  63.4 us
    all_gather x1, waiting for transfers between devices, local(): gathered = lax.all_gather(normed, 'tensor', axis=1, tiled=True)  50.3 us
    unnamed x9, local copies, waits for them, and re-layouts  13.4 us
  transfers between devices with their start and end apart: 5, of which 5 were waited for; matrix products, arithmetic and copies ran while one was open for 5% of the time, Pallas kernels for 0%

commit v1 on v0

v1 whole, which is shorter than its diff:
```python
import functools

import jax
import jax.numpy as jnp
from jax import lax
from jax.experimental import pallas as pl
from jax.experimental.pallas import tpu as pltpu
from jax.sharding import PartitionSpec as P

LANE = 128
VMEM = pl.BlockSpec(memory_space=pltpu.VMEM)
SMEM = pl.BlockSpec(memory_space=pltpu.SMEM)


def call(body, out_shape, in_specs, flops=0, moved=0, n_out=1, scratch=()):
    return pl.pallas_call(
        body,
        out_shape=out_shape,
        in_specs=in_specs,
        out_specs=VMEM if n_out == 1 else [VMEM] * n_out,
        scratch_shapes=list(scratch),
        compiler_params=pltpu.CompilerParams(vmem_limit_bytes=40 * 1024 * 1024),
        cost_estimate=pl.CostEstimate(flops=flops, bytes_accessed=moved, transcendentals=0),
    )


def split_body(x_ref, o_ref):
    blocks, rows, width = x_ref.shape
    for m in range(o_ref.shape[0] // blocks):
        if (m + 1) * LANE <= width:
            for b in range(blocks):
                o_ref[m * blocks + b] = x_ref[b, :, m * LANE : (m + 1) * LANE]
        else:
            for b in range(blocks):
                o_ref[m * blocks + b] = jnp.zeros((rows, LANE), o_ref.dtype)


def order_body(plan_ref, x_ref, o_ref):
    for p in range(o_ref.shape[0]):
        o_ref[p] = x_ref[plan_ref[p]]


def norm_body(x_ref, gain_ref, rows_ref, copies_ref):
    blocks, rows, width = rows_ref.shape
    tiles = width // LANE
    for b in range(blocks):
        whole = jnp.concatenate([x_ref[m * blocks + b] for m in range(tiles)], axis=-1)
        rows_ref[b] = whole
        values = whole.astype(jnp.float32)
        mean_square = jnp.sum(values * values, axis=-1, keepdims=True) * (1.0 / width)
        normed = values * lax.rsqrt(mean_square + 1e-06) * gain_ref[...]
        normed = normed.astype(jnp.bfloat16)
        for t in range(copies_ref.shape[0]):
            copies_ref[t, b] = normed


def mlp_body(x_ref, w_ref, o_ref):
    sections, both, part = w_ref.shape
    hidden_units = both // 2
    total = jnp.zeros((x_ref.shape[0], hidden_units), jnp.float32)
    for s in range(sections):
        total += lax.dot_general(
            x_ref[:, s * part : (s + 1) * part],
            w_ref[s, :hidden_units, :],
            (((1,), (1,)), ((), ())),
            preferred_element_type=jnp.float32,
        )
    hidden = 0.5 * total * (1.0 + lax.erf(total * (0.5**0.5)))
    hidden = hidden.astype(jnp.bfloat16)
    for s in range(sections):
        o_ref[:, s * part : (s + 1) * part] = jnp.dot(
            hidden, w_ref[s, hidden_units:, :], preferred_element_type=jnp.float32
        ).astype(jnp.bfloat16)


def sum_body(x_ref, rows_ref, scale_ref, o_ref):
    blocks = rows_ref.shape[0]
    for b in range(blocks):
        branch = x_ref[0, b].astype(jnp.float32)
        for t in range(1, x_ref.shape[0]):
            branch += x_ref[t, b].astype(jnp.float32)
        values = rows_ref[b].astype(jnp.float32)
        o_ref[b] = (values + scale_ref[...] * branch).astype(o_ref.dtype)


def local(sections, groups, patches, plan, norm_gain, proj_in, proj_out, layer_scale):
    blocks, rows, width = patches.shape
    bf16 = jnp.bfloat16
    weights = jnp.concatenate([proj_in.T, proj_out], axis=0)
    weights = lax.all_gather(weights, "section", axis=0, tiled=False)

    shape = jax.ShapeDtypeStruct((sections * blocks, rows, LANE), bf16)
    tiles = call(split_body, shape, [VMEM])(patches)
    tiles = lax.all_to_all(tiles, "section", 0, 0, tiled=True)
    tiles = call(order_body, shape, [SMEM, VMEM])(plan, tiles)
    tiles = lax.all_to_all(tiles, "section", 0, 0, tiled=True)
    own, copies = call(
        norm_body,
        (
            jax.ShapeDtypeStruct((blocks, rows, width), bf16),
            jax.ShapeDtypeStruct((groups, blocks, rows, width), bf16),
        ),
        [VMEM, VMEM],
        n_out=2,
    )(tiles, norm_gain.reshape(1, width))

    all_rows = groups * blocks * rows
    normed = lax.all_to_all(copies, "tensor", 0, 0, tiled=True)
    partial_sum = call(
        mlp_body,
        jax.ShapeDtypeStruct((all_rows, width), bf16),
        [VMEM, VMEM],
        flops=4 * all_rows * width * proj_in.shape[1],
        moved=10 * 1024 * 1024,
    )(normed.reshape(all_rows, width), weights)
    terms = lax.all_to_all(
        partial_sum.reshape(groups, blocks, rows, width), "tensor", 0, 0, tiled=True
    )
    return call(
        sum_body, jax.ShapeDtypeStruct((blocks, rows, width), bf16), [VMEM, VMEM, VMEM]
    )(terms, own, layer_scale.reshape(1, width))


def solution(mesh):
    return jax.shard_map(
        functools.partial(local, mesh.shape["section"], mesh.shape["tensor"]),
        mesh=mesh,
        in_specs=(
            P("section", "tensor", None),
            P(),
            P(),
            P("section", "tensor"),
            P("tensor", "section"),
            P(),
        ),
        out_specs=P("section", "tensor", None),
        check_vma=False,
    )
```

time: 432 us -> 155 us (0.36)
  waiting for transfers between devices: 382 us -> 61.6 us
  blocking collectives: 0 us -> 32.8 us
  starting transfers between devices: 0.16 us -> 18.9 us
  Pallas kernels: 0 us -> 9.5 us
  matrix products: 8.36 us -> 0 us
  local copies, waits for them, and re-layouts: 22 us -> 15.2 us
    all_gather x4 -> x1, waiting for transfers between devices: 263 us -> 20.7 us  [local(): weights = lax.all_gather(weights, 'section', axis=0, tiled=False)]
    unnamed x6 -> x1, waiting for transfers between devices: 118 us -> 0.02 us
    all_to_all x0 -> x3, waiting for transfers between devices: none -> 40.9 us  [the longest x1 22.7 us: local(): lax.all_to_all(partial_sum.reshape(groups, blocks, rows, width), 'tensor'...]
    all_to_all x0 -> x1, blocking collectives: none -> 32.8 us  [local(): tiles = lax.all_to_all(tiles, 'section', 0, 0, tiled=True)]
    all_to_all x0 -> x3, starting transfers between devices: none -> 18.8 us  [the longest x1 7.53 us: local(): lax.all_to_all(partial_sum.reshape(groups, blocks, rows, width), 'tensor'...]
    pallas_call x0 -> x5, Pallas kernels: none -> 9.5 us  [the longest x1 5.93 us: local(): call(mlp_body, jax.ShapeDtypeStruct((all_rows, width), bf16), [VMEM, VMEM...]
    dot_general x1 -> x0, matrix products: 8.36 us -> none  [local(): jnp.dot(hidden, lax.all_gather(proj_out, 'section', axis=1, tiled=True),...]
    unnamed x9 -> x12, local copies, waits for them, and re-layouts: 13.4 us -> 6.46 us
  transfers between devices with their start and end apart: 5 -> 4, of which waited for: 5 -> 3; matrix products, arithmetic and copies ran while one was open for 5% -> 6% of each run, Pallas kernels for 0% -> 2%
where the time goes in v1:
time: 155 us; the launch traced here: 152 us
  waiting for transfers between devices  61.6 us (40%)
  blocking collectives  32.8 us (21%)
  starting transfers between devices  18.9 us (12%)
  local copies, waits for them, and re-layouts  15.2 us (10%)
  between operations  13.4 us (9%)
  Pallas kernels  9.5 us (6%)
    all_to_all x1, blocking collectives, local(): tiles = lax.all_to_all(tiles, 'section', 0, 0, tiled=True)  32.8 us
    all_to_all x1, waiting for transfers between devices, local(): lax.all_to_all(partial_sum.reshape(groups, blocks, rows, width), 'tensor'...  22.7 us
    all_gather x1, waiting for transfers between devices, local(): weights = lax.all_gather(weights, 'section', axis=0, tiled=False)  20.7 us
    all_to_all x1, waiting for transfers between devices, local(): tiles = lax.all_to_all(tiles, 'section', 0, 0, tiled=True)  18.2 us
    all_gather x1, local copies, waits for them, and re-layouts, local(): weights = lax.all_gather(weights, 'section', axis=0, tiled=False)  8.75 us
    all_to_all x1, starting transfers between devices, local(): lax.all_to_all(partial_sum.reshape(groups, blocks, rows, width), 'tensor'...  7.53 us
    all_to_all x1, starting transfers between devices, local(): normed = lax.all_to_all(copies, 'tensor', 0, 0, tiled=True)  7.46 us
    unnamed x12, local copies, waits for them, and re-layouts  6.46 us
  transfers between devices with their start and end apart: 4, of which 3 were waited for; matrix products, arithmetic and copies ran while one was open for 6% of the time, Pallas kernels for 2%

profile of v1, /device:TPU:6, one launch (start us, length us, event | category | flops | bytes accessed | tf_op | source)
XLA Modules:
  0.0 152.3 jit_solution(12783221807510938565)
XLA Ops:
  6.5 0.0 copy-start.3
  6.5 0.0 all-gather.4.cloned.1.call-start
  6.5 1.0 copy.7
  7.6 1.0 copy.8
  8.6 0.8 maximum_bitcast_fusion
  9.4 0.0 all-gather.4.cloned.1.call-update
  9.4 0.0 copy-start.1
  9.4 0.9 copy-done.1
  10.3 32.8 %all_to_all.20.x_ref = bf16[64,8,128]{2,1,0:T(8,128)(2,1)S(1)} all-to-all(bf16[64,8,128]{2,1,0:T(8,128)(2,1)S(1)} %shard_map.64), channel_id=1, replica_groups=mesh['section'=32,'tensor'=16] {'section'}, dimensions={0} | all-to-all | bytes 262144 | tf_op jit(solution)/shard_map/all_to_all | solution.py:94
  43.2 0.0 copy-start.2
  43.2 0.7 copy-done.2
  43.8 1.2 shard_map.65
  45.1 3.9 %all-to-all-start.1 = ((bf16[64,8,128]{2,1,0:T(8,128)(2,1)}), bf16[64,8,128]{2,1,0:T(8,128)(2,1)S(1)}, u32[]{:S(2)}, u32[]{:S(2)}) async-start(bf16[64,8,128]{2,1,0:T(8,128)(2,1)} %shard_map.65), calls=%async_computation.1 | async-start | bytes 262144 | tf_op jit(solution)/shard_map/all_to_all | solution.py:96
  48.9 0.0 copy-done.3
  49.0 18.2 %all-to-all-done.1.x_ref = bf16[64,8,128]{2,1,0:T(8,128)(2,1)S(1)} async-done(((bf16[64,8,128]{2,1,0:T(8,128)(2,1)}), bf16[64,8,128]{2,1,0:T(8,128)(2,1)S(1)}, u32[]{:S(2)}, u32[]{:S(2)}) %all-to-all-start.1) | async-done | bytes 131104 | tf_op jit(solution)/shard_map/all_to_all | solution.py:96
  67.2 1.4 shard_map.66
  68.6 7.5 %all-to-all-start.2 = ((bf16[16,2,8,3200]{3,2,1,0:T(8,128)(2,1)}), bf16[16,2,8,3200]{3,2,1,0:T(8,128)(2,1)S(1)}, u32[]{:S(2)}, u32[]{:S(2)}) async-start(bf16[16,2,8,3200]{3,2,1,0:T(8,128)(2,1)} %get-tuple-element.7), calls=%async_computation.2 | async-start | bytes 3276800 | tf_op jit(solution)/shard_map/all_to_all | solution.py:108
  76.0 20.7 %all-gather.4.cloned.1.call-done = bf16[32,800,100]{1,2,0:T(8,128)(2,1)} async-done(((bf16[1,800,100]{1,2,0:T(8,128)(2,1)}), bf16[32,800,100]{1,2,0:T(8,128)(2,1)}) %all-gather.4.cloned.1.call-update) | async-done | bytes 5120016 | tf_op jit(solution)/shard_map/all_gather | solution.py:90
  96.7 8.8 %copy.9.w_ref = bf16[32,800,100]{2,1,0:T(8,128)(2,1)} copy(bf16[32,800,100]{1,2,0:T(8,128)(2,1)} %all-gather.4.cloned.1.call-done) | data formatting | bytes 10240000 | tf_op jit(solution)/shard_map/all_gather | solution.py:90
  105.5 0.0 all-to-all-done.2
  105.5 0.0 copy-start
  105.5 2.9 %copy-done = bf16[32,800,100]{2,1,0:T(8,128)(2,1)S(1)} copy-done((bf16[32,800,100]{2,1,0:T(8,128)(2,1)S(1)}, bf16[32,800,100]{2,1,0:T(8,128)(2,1)}, u32[]{:S(2)}) %copy-start) | copy-done | bytes 5120024
  108.3 5.9 %shard_map.67 = bf16[256,3200]{1,0:T(8,128)(2,1)} custom-call(bf16[256,3200]{1,0:T(8,128)(2,1)S(1)} %bitcast.5, bf16[32,800,100]{2,1,0:T(8,128)(2,1)S(1)} %copy-done), custom_call_target="tpu_custom_call" | custom-call | flops 1310720000 | bytes 10485760 | tf_op jit(solution)/shard_map/pallas_call | solution.py:109
  114.3 0.0 copy-start.4
  114.3 7.5 %all-to-all-start.3 = ((bf16[16,2,8,3200]{3,2,1,0:T(8,128)(2,1)}), bf16[16,2,8,3200]{3,2,1,0:T(8,128)(2,1)S(1)}, u32[]{:S(2)}, u32[]{:S(2)}) async-start(bf16[16,2,8,3200]{3,2,1,0:T(8,128)(2,1)} %bitcast.3), calls=%async_computation.3 | async-start | bytes 3276800 | tf_op jit(solution)/shard_map/all_to_all | solution.py:116
  121.8 0.0 copy-done.4
  121.8 22.7 %all-to-all-done.3.x_ref = bf16[16,2,8,3200]{3,2,1,0:T(8,128)(2,1)S(1)} async-done(((bf16[16,2,8,3200]{3,2,1,0:T(8,128)(2,1)}), bf16[16,2,8,3200]{3,2,1,0:T(8,128)(2,1)S(1)}, u32[]{:S(2)}, u32[]{:S(2)}) %all-to-all-start.3) | async-done | bytes 1638432 | tf_op jit(solution)/shard_map/all_to_all | solution.py:116
  144.5 0.9 shard_map.68
  (3 shorter events, 0.0 us)
Async XLA Ops:
  6.5 42.4 %copy-start.3 = (f32[3200]{0:T(1024)S(1)}, f32[3200]{0:T(1024)}, u32[]{:S(2)}) copy-start(f32[3200]{0:T(1024)} %param.8) | copy-start | bytes 38404
  6.5 90.2 %all-gather.4.cloned.1.call-start = ((), (), s32[]{:S(2)}) async-start(), calls=%async_computation.4 | async-start | bytes 6150144 | tf_op jit(solution)/shard_map/all_gather | solution.py:90
  9.4 0.9 copy-start.1
  43.2 0.7 copy-start.2
  45.1 22.1 %all-to-all-start.1 = ((bf16[64,8,128]{2,1,0:T(8,128)(2,1)}), bf16[64,8,128]{2,1,0:T(8,128)(2,1)S(1)}, u32[]{:S(2)}, u32[]{:S(2)}) async-start(bf16[64,8,128]{2,1,0:T(8,128)(2,1)} %shard_map.65), calls=%async_computation.1 | async-start | bytes 262144 | tf_op jit(solution)/shard_map/all_to_all | solution.py:96
  68.6 36.9 %all-to-all-start.2 = ((bf16[16,2,8,3200]{3,2,1,0:T(8,128)(2,1)}), bf16[16,2,8,3200]{3,2,1,0:T(8,128)(2,1)S(1)}, u32[]{:S(2)}, u32[]{:S(2)}) async-start(bf16[16,2,8,3200]{3,2,1,0:T(8,128)(2,1)} %get-tuple-element.7), calls=%async_computation.2 | async-start | bytes 3276800 | tf_op jit(solution)/shard_map/all_to_all | solution.py:108
  105.5 2.9 %copy-start = (bf16[32,800,100]{2,1,0:T(8,128)(2,1)S(1)}, bf16[32,800,100]{2,1,0:T(8,128)(2,1)}, u32[]{:S(2)}) copy-start(bf16[32,800,100]{2,1,0:T(8,128)(2,1)} %copy.9.w_ref) | copy-start | bytes 15360004
  114.3 7.5 %copy-start.4 = (f32[3200]{0:T(1024)S(1)}, f32[3200]{0:T(1024)}, u32[]{:S(2)}) copy-start(f32[3200]{0:T(1024)} %param.11) | copy-start | bytes 38404
  114.3 30.3 %all-to-all-start.3 = ((bf16[16,2,8,3200]{3,2,1,0:T(8,128)(2,1)}), bf16[16,2,8,3200]{3,2,1,0:T(8,128)(2,1)S(1)}, u32[]{:S(2)}, u32[]{:S(2)}) async-start(bf16[16,2,8,3200]{3,2,1,0:T(8,128)(2,1)} %bitcast.3), calls=%async_computation.3 | async-start | bytes 3276800 | tf_op jit(solution)/shard_map/all_to_all | solution.py:116
Sparse Core Ops, SparseCore 0:
  9.5 87.1 all-gather.3

commit v2 on v1

--- a/solution.py
+++ b/solution.py
@@ -54,22 +54,41 @@
             copies_ref[t, b] = normed
 
 
-def mlp_body(x_ref, w_ref, o_ref):
-    sections, both, part = w_ref.shape
-    hidden_units = both // 2
-    total = jnp.zeros((x_ref.shape[0], hidden_units), jnp.float32)
+def pack_body(in_ref, out_ref, o_ref):
+    units, part = in_ref.shape
+    o_ref[:units, :part] = in_ref[...]
+    o_ref[units:, :part] = out_ref[...]
+    o_ref[:, part:] = jnp.zeros((2 * units, LANE - part), o_ref.dtype)
+
+
+def mlp_body(part, chunks, x_ref, w_ref, o_ref, held, sems):
+    sections, both, _ = w_ref.shape
+    units = both // 2
+    size = sections // chunks
+    copies = []
+    for half in range(2):
+        for c in range(chunks):
+            place = (pl.ds(c * size, size), pl.ds(half * units, units))
+            copy = pltpu.make_async_copy(w_ref.at[place], held.at[place], sems.at[half, c])
+            copy.start()
+            copies.append(copy)
+    total = jnp.zeros((x_ref.shape[0], units), jnp.float32)
     for s in range(sections):
+        if s % size == 0:
+            copies[s // size].wait()
         total += lax.dot_general(
             x_ref[:, s * part : (s + 1) * part],
-            w_ref[s, :hidden_units, :],
+            held[s, :units, :part],
             (((1,), (1,)), ((), ())),
             preferred_element_type=jnp.float32,
         )
     hidden = 0.5 * total * (1.0 + lax.erf(total * (0.5**0.5)))
     hidden = hidden.astype(jnp.bfloat16)
     for s in range(sections):
+        if s % size == 0:
+            copies[chunks + s // size].wait()
         o_ref[:, s * part : (s + 1) * part] = jnp.dot(
-            hidden, w_ref[s, hidden_units:, :], preferred_element_type=jnp.float32
+            hidden, held[s, units:, :part], preferred_element_type=jnp.float32
         ).astype(jnp.bfloat16)
 
 
@@ -86,7 +105,10 @@
 def local(sections, groups, patches, plan, norm_gain, proj_in, proj_out, layer_scale):
     blocks, rows, width = patches.shape
     bf16 = jnp.bfloat16
-    weights = jnp.concatenate([proj_in.T, proj_out], axis=0)
+    part, units = proj_in.shape
+    weights = call(pack_body, jax.ShapeDtypeStruct((2 * units, LANE), bf16), [VMEM, VMEM])(
+        proj_in.T, proj_out
+    )
     weights = lax.all_gather(weights, "section", axis=0, tiled=False)
 
     shape = jax.ShapeDtypeStruct((sections * blocks, rows, LANE), bf16)
@@ -105,20 +127,23 @@
     )(tiles, norm_gain.reshape(1, width))
 
     all_rows = groups * blocks * rows
-    normed = lax.all_to_all(copies, "tensor", 0, 0, tiled=True)
+    normed = lax.all_to_all(copies.reshape(all_rows, width), "tensor", 0, 0, tiled=True)
+    chunks = 4
     partial_sum = call(
-        mlp_body,
+        functools.partial(mlp_body, part, chunks),
         jax.ShapeDtypeStruct((all_rows, width), bf16),
-        [VMEM, VMEM],
-        flops=4 * all_rows * width * proj_in.shape[1],
+        [VMEM, pl.BlockSpec(memory_space=pltpu.HBM)],
+        flops=4 * all_rows * width * units,
         moved=10 * 1024 * 1024,
-    )(normed.reshape(all_rows, width), weights)
-    terms = lax.all_to_all(
-        partial_sum.reshape(groups, blocks, rows, width), "tensor", 0, 0, tiled=True
-    )
+        scratch=[
+            pltpu.VMEM((sections, 2 * units, LANE), bf16),
+            pltpu.SemaphoreType.DMA((2, chunks)),
+        ],
+    )(normed, weights)
+    terms = lax.all_to_all(partial_sum, "tensor", 0, 0, tiled=True)
     return call(
         sum_body, jax.ShapeDtypeStruct((blocks, rows, width), bf16), [VMEM, VMEM, VMEM]
-    )(terms, own, layer_scale.reshape(1, width))
+    )(terms.reshape(groups, blocks, rows, width), own, layer_scale.reshape(1, width))
 
 
 def solution(mesh):

time: 155 us -> 147 us (0.948)
  blocking collectives: 32.8 us -> 61.6 us
  waiting for transfers between devices: 61.6 us -> 41.9 us
  local copies, waits for them, and re-layouts: 15.2 us -> 6.22 us
  starting transfers between devices: 18.9 us -> 11.3 us
    all_to_all x0 -> x1, blocking collectives: none -> 28.7 us  [local(): lax.all_to_all(copies.reshape(all_rows, width), 'tensor', 0, 0, tiled=True)]
    all_gather x1, waiting for transfers between devices: 20.7 us -> 0.58 us  [local(): weights = lax.all_gather(weights, 'section', axis=0, tiled=False)]
    all_gather x1 -> x0, local copies, waits for them, and re-layouts: 8.75 us -> none  [local(): weights = lax.all_gather(weights, 'section', axis=0, tiled=False)]
    all_to_all x2 -> x1, starting transfers between devices: 15 us -> 7.49 us  [local(): terms = lax.all_to_all(partial_sum, 'tensor', 0, 0, tiled=True)]
    pallas_call x1 -> x2, Pallas kernels: 5.93 us -> 8.21 us  [the longest x1 7.46 us: local(): call(functools.partial(mlp_body, part, chunks), jax.ShapeDtypeStruct((all...]
    unnamed x12 -> x14, local copies, waits for them, and re-layouts: 6.46 us -> 6.2 us
    all_to_all x2 -> x1, waiting for transfers between devices: 22.7 us -> 22.7 us  [local(): terms = lax.all_to_all(partial_sum, 'tensor', 0, 0, tiled=True)]
  transfers between devices with their start and end apart: 4 -> 3, of which waited for: 3 -> 3; matrix products, arithmetic and copies ran while one was open for 6% -> 0% of each run, Pallas kernels for 2% -> 1%
where the time goes in v2:
time: 147 us; the launch traced here: 145 us
  blocking collectives  61.6 us (42%)
  waiting for transfers between devices  41.9 us (29%)
  between operations  13.5 us (9%)
  starting transfers between devices  11.3 us (8%)
  Pallas kernels  10.6 us (7%)
  local copies, waits for them, and re-layouts  6.22 us (4%)
    all_to_all x1, blocking collectives, local(): tiles = lax.all_to_all(tiles, 'section', 0, 0, tiled=True)  32.9 us
    all_to_all x1, blocking collectives, local(): lax.all_to_all(copies.reshape(all_rows, width), 'tensor', 0, 0, tiled=True)  28.7 us
    all_to_all x1, waiting for transfers between devices, local(): terms = lax.all_to_all(partial_sum, 'tensor', 0, 0, tiled=True)  22.7 us
    all_to_all x1, waiting for transfers between devices, local(): tiles = lax.all_to_all(tiles, 'section', 0, 0, tiled=True)  18.5 us
    all_to_all x1, starting transfers between devices, local(): terms = lax.all_to_all(partial_sum, 'tensor', 0, 0, tiled=True)  7.49 us
    pallas_call x1, Pallas kernels, local(): call(functools.partial(mlp_body, part, chunks), jax.ShapeDtypeStruct((all...  7.46 us
    unnamed x14, local copies, waits for them, and re-layouts  6.2 us
    all_to_all x1, starting transfers between devices, local(): tiles = lax.all_to_all(tiles, 'section', 0, 0, tiled=True)  3.85 us
  transfers between devices with their start and end apart: 3, of which 3 were waited for; matrix products, arithmetic and copies ran while one was open for 0% of the time, Pallas kernels for 1%

profile of v2, /device:TPU:6, one launch (start us, length us, event | category | flops | bytes accessed | tf_op | source)
XLA Modules:
  0.0 145.1 jit_solution(5466102342826530310)
XLA Ops:
  6.5 0.0 all-gather.3.cloned.1.call-start
  6.5 0.0 copy-start.2
  6.5 0.9 copy-done.2
  7.4 0.0 copy-start.3
  7.4 0.9 copy-done.3
  8.3 0.0 copy-start.5
  8.3 0.7 shard_map.67
  9.1 0.0 all-gather.3.cloned.1.call-update
  9.1 0.0 copy-start.1
  9.1 0.9 copy-done.1
  10.0 32.9 %all_to_all.30.x_ref = bf16[64,8,128]{2,1,0:T(8,128)(2,1)S(1)} all-to-all(bf16[64,8,128]{2,1,0:T(8,128)(2,1)S(1)} %shard_map.64), channel_id=1, replica_groups=mesh['section'=32,'tensor'=16] {'section'}, dimensions={0} | all-to-all | bytes 262144 | tf_op jit(solution)/shard_map/all_to_all | solution.py:116
  42.9 0.0 copy-start.4
  42.9 0.7 copy-done.4
  43.6 1.2 shard_map.65
  44.8 3.9 %all-to-all-start.1 = ((bf16[64,8,128]{2,1,0:T(8,128)(2,1)}), bf16[64,8,128]{2,1,0:T(8,128)(2,1)S(1)}, u32[]{:S(2)}, u32[]{:S(2)}) async-start(bf16[64,8,128]{2,1,0:T(8,128)(2,1)} %shard_map.65), calls=%async_computation.1 | async-start | bytes 262144 | tf_op jit(solution)/shard_map/all_to_all | solution.py:118
  48.6 0.0 copy-done.5
  48.7 18.5 %all-to-all-done.1.x_ref = bf16[64,8,128]{2,1,0:T(8,128)(2,1)S(1)} async-done(((bf16[64,8,128]{2,1,0:T(8,128)(2,1)}), bf16[64,8,128]{2,1,0:T(8,128)(2,1)S(1)}, u32[]{:S(2)}, u32[]{:S(2)}) %all-to-all-start.1) | async-done | bytes 131104 | tf_op jit(solution)/shard_map/all_to_all | solution.py:118
  67.2 0.2 shard_map.66
  67.4 28.7 %all_to_all.31 = bf16[16,16,3200]{2,1,0:T(8,128)(2,1)S(1)} all-to-all(bf16[16,16,3200]{2,1,0:T(8,128)(2,1)S(1)} %bitcast.9), channel_id=1, replica_groups=mesh['section'=32,'tensor'=16] {'tensor'}, dimensions={0} | all-to-all | bytes 3276800 | tf_op jit(solution)/shard_map/all_to_all | solution.py:130
  96.2 0.6 all-gather.3.cloned.1.call-done
  96.7 0.0 copy-start
  96.7 2.9 %copy-done = bf16[25600,128]{1,0:T(8,128)(2,1)S(1)} copy-done((bf16[25600,128]{1,0:T(8,128)(2,1)S(1)}, bf16[25600,128]{1,0:T(8,128)(2,1)}, u32[]{:S(2)}) %copy-start) | copy-done | bytes 6553624
  99.6 7.5 %shard_map.68 = bf16[256,3200]{1,0:T(8,128)(2,1)} custom-call(bf16[256,3200]{1,0:T(8,128)(2,1)S(1)} %bitcast.6, bf16[32,800,128]{2,1,0:T(8,128)(2,1)S(1)} %bitcast.7), custom_call_target="tpu_custom_call" | custom-call | flops 1310720000 | bytes 10485760 | tf_op jit(solution)/shard_map/pallas_call | solution.py:132
  107.1 0.0 copy-start.6
  107.1 7.5 %all-to-all-start.3 = ((bf16[16,16,3200]{2,1,0:T(8,128)(2,1)}), bf16[16,16,3200]{2,1,0:T(8,128)(2,1)S(1)}, u32[]{:S(2)}, u32[]{:S(2)}) async-start(bf16[16,16,3200]{2,1,0:T(8,128)(2,1)} %bitcast.4), calls=%async_computation.3 | async-start | bytes 3276800 | tf_op jit(solution)/shard_map/all_to_all | solution.py:143
  114.6 0.0 copy-done.6
  114.6 22.7 %all-to-all-done.3 = bf16[16,16,3200]{2,1,0:T(8,128)(2,1)S(1)} async-done(((bf16[16,16,3200]{2,1,0:T(8,128)(2,1)}), bf16[16,16,3200]{2,1,0:T(8,128)(2,1)S(1)}, u32[]{:S(2)}, u32[]{:S(2)}) %all-to-all-start.3) | async-done | bytes 1638432 | tf_op jit(solution)/shard_map/all_to_all | solution.py:143
  137.3 0.9 shard_map.69
  (3 shorter events, 0.0 us)
Async XLA Ops:
  6.5 90.2 %all-gather.3.cloned.1.call-start = ((), (), s32[]{:S(2)}) async-start(), calls=%async_computation.4 | async-start | bytes 6758400 | tf_op jit(solution)/shard_map/all_gather | solution.py:112
  6.5 0.9 copy-start.2
  7.4 0.9 copy-start.3
  8.3 40.3 %copy-start.5 = (f32[3200]{0:T(1024)S(1)}, f32[3200]{0:T(1024)}, u32[]{:S(2)}) copy-start(f32[3200]{0:T(1024)} %param.8) | copy-start | bytes 38404
  9.1 0.9 copy-start.1
  42.9 0.7 copy-start.4
  44.8 22.4 %all-to-all-start.1 = ((bf16[64,8,128]{2,1,0:T(8,128)(2,1)}), bf16[64,8,128]{2,1,0:T(8,128)(2,1)S(1)}, u32[]{:S(2)}, u32[]{:S(2)}) async-start(bf16[64,8,128]{2,1,0:T(8,128)(2,1)} %shard_map.65), calls=%async_computation.1 | async-start | bytes 262144 | tf_op jit(solution)/shard_map/all_to_all | solution.py:118
  96.7 2.9 %copy-start = (bf16[25600,128]{1,0:T(8,128)(2,1)S(1)}, bf16[25600,128]{1,0:T(8,128)(2,1)}, u32[]{:S(2)}) copy-start(bf16[25600,128]{1,0:T(8,128)(2,1)} %all-gather.3.cloned.1.call-done) | copy-start | bytes 19660804
  107.1 7.5 %copy-start.6 = (f32[3200]{0:T(1024)S(1)}, f32[3200]{0:T(1024)}, u32[]{:S(2)}) copy-start(f32[3200]{0:T(1024)} %param.11) | copy-start | bytes 38404
  107.1 30.3 %all-to-all-start.3 = ((bf16[16,16,3200]{2,1,0:T(8,128)(2,1)}), bf16[16,16,3200]{2,1,0:T(8,128)(2,1)S(1)}, u32[]{:S(2)}, u32[]{:S(2)}) async-start(bf16[16,16,3200]{2,1,0:T(8,128)(2,1)} %bitcast.4), calls=%async_computation.3 | async-start | bytes 3276800 | tf_op jit(solution)/shard_map/all_to_all | solution.py:143
Sparse Core Ops, SparseCore 0:
  9.5 87.2 all-gather.2

commit v3 on v2

--- a/solution.py
+++ b/solution.py
@@ -9,6 +9,7 @@
 
 LANE = 128
 VMEM = pl.BlockSpec(memory_space=pltpu.VMEM)
+ANY = pl.BlockSpec(memory_space=pl.ANY)
 SMEM = pl.BlockSpec(memory_space=pltpu.SMEM)
 
 
@@ -19,7 +20,7 @@
         in_specs=in_specs,
         out_specs=VMEM if n_out == 1 else [VMEM] * n_out,
         scratch_shapes=list(scratch),
-        compiler_params=pltpu.CompilerParams(vmem_limit_bytes=40 * 1024 * 1024),
+        compiler_params=pltpu.CompilerParams(vmem_limit_bytes=32 * 1024 * 1024),
         cost_estimate=pl.CostEstimate(flops=flops, bytes_accessed=moved, transcendentals=0),
     )
 
@@ -35,12 +36,14 @@
                 o_ref[m * blocks + b] = jnp.zeros((rows, LANE), o_ref.dtype)
 
 
-def order_body(plan_ref, x_ref, o_ref):
+def order_body(plan_ref, x_ref, *refs):
+    o_ref = refs[-1]
     for p in range(o_ref.shape[0]):
         o_ref[p] = x_ref[plan_ref[p]]
 
 
-def norm_body(x_ref, gain_ref, rows_ref, copies_ref):
+def norm_body(x_ref, gain_ref, *refs):
+    rows_ref, copies_ref = refs[-2:]
     blocks, rows, width = rows_ref.shape
     tiles = width // LANE
     for b in range(blocks):
@@ -61,21 +64,30 @@
     o_ref[:, part:] = jnp.zeros((2 * units, LANE - part), o_ref.dtype)
 
 
-def mlp_body(part, chunks, x_ref, w_ref, o_ref, held, sems):
-    sections, both, _ = w_ref.shape
+def mlp_body(part, offsets, sizes, x_ref, *refs):
+    n = len(offsets)
+    mine, others = refs[:n], refs[n : n + len(sizes)]
+    o_ref, held, sems = refs[n + len(sizes) :]
+    sections, both, _ = held.shape
     units = both // 2
-    size = sections // chunks
+    me = lax.axis_index("section")
+    core = lax.rem(me, 2)
+    shards = list(mine)
+    for ref, size in zip(others, sizes):
+        shards += [ref.at[k] for k in range(size)]
     copies = []
     for half in range(2):
-        for c in range(chunks):
-            place = (pl.ds(c * size, size), pl.ds(half * units, units))
-            copy = pltpu.make_async_copy(w_ref.at[place], held.at[place], sems.at[half, c])
+        rows = pl.ds(half * units, units)
+        for k, shard in enumerate(shards):
+            ring = lax.rem(me - core + 2 * offsets[k % n] + 2 * sections, sections)
+            place = ring + (core if k < n else 1 - core)
+            copy = pltpu.make_async_copy(shard.at[rows], held.at[place, rows], sems.at[half, k])
             copy.start()
             copies.append(copy)
+    for copy in copies[: 2 * n]:
+        copy.wait()
     total = jnp.zeros((x_ref.shape[0], units), jnp.float32)
     for s in range(sections):
-        if s % size == 0:
-            copies[s // size].wait()
         total += lax.dot_general(
             x_ref[:, s * part : (s + 1) * part],
             held[s, :units, :part],
@@ -84,12 +96,39 @@
         )
     hidden = 0.5 * total * (1.0 + lax.erf(total * (0.5**0.5)))
     hidden = hidden.astype(jnp.bfloat16)
+    for copy in copies[2 * n :]:
+        copy.wait()
     for s in range(sections):
-        if s % size == 0:
-            copies[chunks + s // size].wait()
         o_ref[:, s * part : (s + 1) * part] = jnp.dot(
             hidden, held[s, units:, :part], preferred_element_type=jnp.float32
         ).astype(jnp.bfloat16)
+
+
+def shifted(x, sections, steps):
+    return lax.ppermute(x, "section", [(i, (i + 2 * steps) % sections) for i in range(sections)])
+
+
+def gather_weights(mine, sections):
+    chips = sections // 2
+    ahead, back = chips // 2, (chips - 1) // 2
+    swap = [(i, i ^ 1) for i in range(sections)]
+    shards, offsets, groups, sizes = [mine], [0], [], []
+    down, up = mine, mine
+    done = 0
+    for step in range(1, ahead + 1):
+        down = shifted(down, sections, 1)
+        shards.append(down)
+        offsets.append(-step)
+        if step <= back:
+            up = shifted(up, sections, -1)
+            shards.append(up)
+            offsets.append(step)
+        if step in (3, 6, ahead):
+            group = jnp.stack(shards[done:])
+            groups.append(lax.ppermute(group, "section", swap))
+            sizes.append(len(shards) - done)
+            done = len(shards)
+    return shards, offsets, groups, sizes
 
 
 def sum_body(x_ref, rows_ref, scale_ref, o_ref):
@@ -109,12 +148,13 @@
     weights = call(pack_body, jax.ShapeDtypeStruct((2 * units, LANE), bf16), [VMEM, VMEM])(
         proj_in.T, proj_out
     )
-    weights = lax.all_gather(weights, "section", axis=0, tiled=False)
+    shards, offsets, others, sizes = gather_weights(weights, sections)
 
     shape = jax.ShapeDtypeStruct((sections * blocks, rows, LANE), bf16)
     tiles = call(split_body, shape, [VMEM])(patches)
     tiles = lax.all_to_all(tiles, "section", 0, 0, tiled=True)
-    tiles = call(order_body, shape, [SMEM, VMEM])(plan, tiles)
+    first, second = shards[3:5], shards[9:11]
+    tiles = call(order_body, shape, [SMEM, VMEM, ANY, ANY])(plan, tiles, *first)
     tiles = lax.all_to_all(tiles, "section", 0, 0, tiled=True)
     own, copies = call(
         norm_body,
@@ -122,24 +162,23 @@
             jax.ShapeDtypeStruct((blocks, rows, width), bf16),
             jax.ShapeDtypeStruct((groups, blocks, rows, width), bf16),
         ),
-        [VMEM, VMEM],
+        [VMEM, VMEM, ANY, ANY],
         n_out=2,
-    )(tiles, norm_gain.reshape(1, width))
+    )(tiles, norm_gain.reshape(1, width), *second)
 
     all_rows = groups * blocks * rows
     normed = lax.all_to_all(copies.reshape(all_rows, width), "tensor", 0, 0, tiled=True)
-    chunks = 4
     partial_sum = call(
-        functools.partial(mlp_body, part, chunks),
+        functools.partial(mlp_body, part, offsets, sizes),
         jax.ShapeDtypeStruct((all_rows, width), bf16),
-        [VMEM, pl.BlockSpec(memory_space=pltpu.HBM)],
+        [VMEM] + [ANY] * (len(shards) + len(others)),
         flops=4 * all_rows * width * units,
         moved=10 * 1024 * 1024,
         scratch=[
             pltpu.VMEM((sections, 2 * units, LANE), bf16),
-            pltpu.SemaphoreType.DMA((2, chunks)),
+            pltpu.SemaphoreType.DMA((2, sections)),
         ],
-    )(normed, weights)
+    )(normed, *shards, *others)
     terms = lax.all_to_all(partial_sum, "tensor", 0, 0, tiled=True)
     return call(
         sum_body, jax.ShapeDtypeStruct((blocks, rows, width), bf16), [VMEM, VMEM, VMEM]

time: 147 us -> 192 us (1.31)
  starting transfers between devices: 11.3 us -> 98.3 us
  blocking collectives: 61.6 us -> 0 us
  local copies, waits for them, and re-layouts: 6.22 us -> 25.2 us
  between operations: 13.5 us -> 0.36 us
  Pallas kernels: 10.6 us -> 17.5 us
  waiting for transfers between devices: 41.9 us -> 47.7 us
    ppermute x0 -> x18, starting transfers between devices: none -> 64.5 us  [the longest x15 58.8 us: shifted(): lax.ppermute(x, 'section', [(i, (i + 2 * steps) % sections) for i in rang...]
    all_to_all x2 -> x0, blocking collectives: 61.6 us -> none  [the longest x1 32.9 us: local(): tiles = lax.all_to_all(tiles, 'section', 0, 0, tiled=True)]
    ppermute x0 -> x18, waiting for transfers between devices: none -> 25.1 us  [the longest x15 23.1 us: shifted(): lax.ppermute(x, 'section', [(i, (i + 2 * steps) % sections) for i in rang...]
    all_to_all x1 -> x2, waiting for transfers between devices: 18.5 us -> 0.01 us  [local(): tiles = lax.all_to_all(tiles, 'section', 0, 0, tiled=True)]
    unnamed x14 -> x63, local copies, waits for them, and re-layouts: 6.2 us -> 23.1 us
    all_to_all x1 -> x2, starting transfers between devices: 3.85 us -> 19 us  [local(): tiles = lax.all_to_all(tiles, 'section', 0, 0, tiled=True)]
    all_to_all x0 -> x1, starting transfers between devices: none -> 7.43 us  [local(): lax.all_to_all(copies.reshape(all_rows, width), 'tensor', 0, 0, tiled=True)]
    pallas_call x2, Pallas kernels: 8.69 us -> 15.7 us  [the longest x1 14.4 us: local(): call(functools.partial(mlp_body, part, offsets, sizes), jax.ShapeDtypeStr...]
  transfers between devices with their start and end apart: 3 -> 22, of which waited for: 3 -> 10; matrix products, arithmetic and copies ran while one was open for 0% -> 5% of each run, Pallas kernels for 1% -> 1%
where the time goes in v3:
time: 192 us; the launch traced here: 189 us
  starting transfers between devices  98.3 us (51%)
  waiting for transfers between devices  47.7 us (25%)
  local copies, waits for them, and re-layouts  25.2 us (13%)
  Pallas kernels  17.5 us (9%)
    ppermute x15, starting transfers between devices, shifted(): lax.ppermute(x, 'section', [(i, (i + 2 * steps) % sections) for i in rang...  58.8 us
    ppermute x15, waiting for transfers between devices, shifted(): lax.ppermute(x, 'section', [(i, (i + 2 * steps) % sections) for i in rang...  23.1 us
    unnamed x63, local copies, waits for them, and re-layouts  23.1 us
    all_to_all x1, waiting for transfers between devices, local(): terms = lax.all_to_all(partial_sum, 'tensor', 0, 0, tiled=True)  22.6 us
    all_to_all x2, starting transfers between devices, local(): tiles = lax.all_to_all(tiles, 'section', 0, 0, tiled=True)  19 us
    pallas_call x1, Pallas kernels, local(): call(functools.partial(mlp_body, part, offsets, sizes), jax.ShapeDtypeStr...  14.4 us
    all_to_all x1, starting transfers between devices, local(): lax.all_to_all(copies.reshape(all_rows, width), 'tensor', 0, 0, tiled=True)  7.43 us
    all_to_all x1, starting transfers between devices, local(): terms = lax.all_to_all(partial_sum, 'tensor', 0, 0, tiled=True)  7.37 us
  transfers between devices with their start and end apart: 22, of which 10 were waited for; matrix products, arithmetic and copies ran while one was open for 5% of the time, Pallas kernels for 1%

profile of v3, /device:TPU:6, one launch (start us, length us, event | category | flops | bytes accessed | tf_op | source)
XLA Modules:
  0.0 189.2 jit_solution(5011961268570917154)
XLA Ops:
  0.0 0.9 copy-done.20
  0.9 0.9 copy-done.21
  1.9 3.8 %collective-permute-start = (bf16[800,128]{1,0:T(8,128)(2,1)S(1)}, bf16[800,128]{1,0:T(8,128)(2,1)S(1)}, u32[]{:S(2)}, u32[]{:S(2)}) collective-permute-start(bf16[800,128]{1,0:T(8,128)(2,1)S(1)} %shard_map.65.refs_0_), channel_id=1, source_target_pairs={{0,32},{16,48},{32,64},{48,80},{64,96},{80,112},{96,128},{112,144}... | collective-permute-start | bytes 614408 | tf_op jit(solution)/shard_map/ppermute | solution.py:108
  5.7 9.5 %collective-permute-start.2 = (bf16[800,128]{1,0:T(8,128)(2,1)S(1)}, bf16[800,128]{1,0:T(8,128)(2,1)S(1)}, u32[]{:S(2)}, u32[]{:S(2)}) collective-permute-start(bf16[800,128]{1,0:T(8,128)(2,1)S(1)} %shard_map.65.refs_0_), channel_id=1, source_target_pairs={{0,480},{16,496},{32,0},{48,16},{64,32},{80,48},{96,64},{112,80},{... | collective-permute-start | bytes 614408 | tf_op jit(solution)/shard_map/ppermute | solution.py:108
  15.2 0.9 copy-done.19
  16.1 0.7 shard_map.64
  16.8 9.2 %all-to-all-start = ((bf16[64,8,128]{2,1,0:T(8,128)(2,1)}), bf16[64,8,128]{2,1,0:T(8,128)(2,1)S(1)}, u32[]{:S(2)}, u32[]{:S(2)}) async-start(bf16[64,8,128]{2,1,0:T(8,128)(2,1)} %shard_map.64), calls=%async_computation | async-start | bytes 262144 | tf_op jit(solution)/shard_map/all_to_all | solution.py:155
  26.0 0.7 reshape.16.gain_ref
  26.7 0.7 bitcast_dynamic-update-slice_fusion.12
  27.4 3.7 %collective-permute-start.1 = (bf16[800,128]{1,0:T(8,128)(2,1)S(1)}, bf16[800,128]{1,0:T(8,128)(2,1)S(1)}, u32[]{:S(2)}, u32[]{:S(2)}) collective-permute-start(bf16[800,128]{1,0:T(8,128)(2,1)S(1)} %collective-permute-done.refs_1_), channel_id=1, source_target_pairs={{0,32},{16,48},{32,64},{48,80},{64,96},{80,112},{96,128},{112,144}... | collective-permute-start | bytes 614408 | tf_op jit(solution)/shard_map/ppermute | solution.py:108
  31.2 3.4 %collective-permute-start.3 = (bf16[800,128]{1,0:T(8,128)(2,1)S(1)}, bf16[800,128]{1,0:T(8,128)(2,1)S(1)}, u32[]{:S(2)}, u32[]{:S(2)}) collective-permute-start(bf16[800,128]{1,0:T(8,128)(2,1)S(1)} %collective-permute-done.2.refs_2_), channel_id=1, source_target_pairs={{0,480},{16,496},{32,0},{48,16},{64,32},{80,48},{96,64},{112,80},{... | collective-permute-start | bytes 614408 | tf_op jit(solution)/shard_map/ppermute | solution.py:108
  34.5 0.7 bitcast_dynamic-update-slice_fusion.11
  35.2 0.7 bitcast_dynamic-update-slice_fusion.10
  35.9 4.2 %collective-permute-done.1.refs_0_.refs_3_ = bf16[800,128]{1,0:T(8,128)(2,1)S(1)} collective-permute-done((bf16[800,128]{1,0:T(8,128)(2,1)S(1)}, bf16[800,128]{1,0:T(8,128)(2,1)S(1)}, u32[]{:S(2)}, u32[]{:S(2)}) %collective-permute-start.1) | collective-permute-done | bytes 204832 | tf_op jit(solution)/shard_map/ppermute | solution.py:108
  40.1 2.3 %collective-permute-start.4 = (bf16[800,128]{1,0:T(8,128)(2,1)S(1)}, bf16[800,128]{1,0:T(8,128)(2,1)S(1)}, u32[]{:S(2)}, u32[]{:S(2)}) collective-permute-start(bf16[800,128]{1,0:T(8,128)(2,1)S(1)} %collective-permute-done.1.refs_0_.refs_3_), channel_id=1, source_target_pairs={{0,32},{16,48},{32,64},{48,80},{64,96},{80,112},{96,128},{112,144}... | collective-permute-start | bytes 614408 | tf_op jit(solution)/shard_map/ppermute | solution.py:108
  42.4 4.7 %collective-permute-start.7 = (bf16[800,128]{1,0:T(8,128)(2,1)S(1)}, bf16[800,128]{1,0:T(8,128)(2,1)S(1)}, u32[]{:S(2)}, u32[]{:S(2)}) collective-permute-start(bf16[800,128]{1,0:T(8,128)(2,1)S(1)} %collective-permute-done.3.refs_1_.refs_4_), channel_id=1, source_target_pairs={{0,480},{16,496},{32,0},{48,16},{64,32},{80,48},{96,64},{112,80},{... | collective-permute-start | bytes 614408 | tf_op jit(solution)/shard_map/ppermute | solution.py:108
  47.2 0.7 bitcast_dynamic-update-slice_fusion.9
  47.9 0.7 bitcast_dynamic-update-slice_fusion.8
  48.6 1.2 shard_map.66
  49.8 9.8 %all-to-all-start.1 = ((bf16[64,8,128]{2,1,0:T(8,128)(2,1)}), bf16[64,8,128]{2,1,0:T(8,128)(2,1)S(1)}, u32[]{:S(2)}, u32[]{:S(2)}) async-start(bf16[64,8,128]{2,1,0:T(8,128)(2,1)} %shard_map.66), calls=%async_computation.1 | async-start | bytes 262144 | tf_op jit(solution)/shard_map/all_to_all | solution.py:158
  59.6 3.7 %collective-permute-start.5 = (bf16[800,128]{1,0:T(8,128)(2,1)S(1)}, bf16[800,128]{1,0:T(8,128)(2,1)S(1)}, u32[]{:S(2)}, u32[]{:S(2)}) collective-permute-start(bf16[800,128]{1,0:T(8,128)(2,1)S(1)} %collective-permute-done.4.refs_5_), channel_id=1, source_target_pairs={{0,32},{16,48},{32,64},{48,80},{64,96},{80,112},{96,128},{112,144}... | collective-permute-start | bytes 614408 | tf_op jit(solution)/shard_map/ppermute | solution.py:108
  63.3 3.4 %collective-permute-start.8 = (bf16[800,128]{1,0:T(8,128)(2,1)S(1)}, bf16[800,128]{1,0:T(8,128)(2,1)S(1)}, u32[]{:S(2)}, u32[]{:S(2)}) collective-permute-start(bf16[800,128]{1,0:T(8,128)(2,1)S(1)} %collective-permute-done.7.refs_6_), channel_id=1, source_target_pairs={{0,480},{16,496},{32,0},{48,16},{64,32},{80,48},{96,64},{112,80},{... | collective-permute-start | bytes 614408 | tf_op jit(solution)/shard_map/ppermute | solution.py:108
  66.7 0.7 bitcast_dynamic-update-slice_fusion.7
  67.4 0.7 bitcast_dynamic-update-slice_fusion.6
  68.1 1.9 %collective-permute-start.15 = (bf16[7,800,128]{2,1,0:T(8,128)(2,1)}, bf16[7,800,128]{2,1,0:T(8,128)(2,1)}, u32[]{:S(2)}, u32[]{:S(2)}) collective-permute-start(bf16[7,800,128]{2,1,0:T(8,128)(2,1)} %bitcast_dynamic-update-slice_fusion.6), channel_id=1, source_target_pairs={{0,16},{16,0},{32,48},{48,32},{64,80},{80,64},{96,112},{112,96},{1... | collective-permute-start | bytes 4300808 | tf_op jit(solution)/shard_map/ppermute | solution.py:128
  70.0 3.7 %collective-permute-done.5.refs_7_ = bf16[800,128]{1,0:T(8,128)(2,1)S(1)} collective-permute-done((bf16[800,128]{1,0:T(8,128)(2,1)S(1)}, bf16[800,128]{1,0:T(8,128)(2,1)S(1)}, u32[]{:S(2)}, u32[]{:S(2)}) %collective-permute-start.5) | collective-permute-done | bytes 204832 | tf_op jit(solution)/shard_map/ppermute | solution.py:108
  73.7 2.1 %collective-permute-start.6 = (bf16[800,128]{1,0:T(8,128)(2,1)S(1)}, bf16[800,128]{1,0:T(8,128)(2,1)S(1)}, u32[]{:S(2)}, u32[]{:S(2)}) collective-permute-start(bf16[800,128]{1,0:T(8,128)(2,1)S(1)} %collective-permute-done.5.refs_7_), channel_id=1, source_target_pairs={{0,32},{16,48},{32,64},{48,80},{64,96},{80,112},{96,128},{112,144}... | collective-permute-start | bytes 614408 | tf_op jit(solution)/shard_map/ppermute | solution.py:108
  75.8 5.0 %collective-permute-start.9 = (bf16[800,128]{1,0:T(8,128)(2,1)S(1)}, bf16[800,128]{1,0:T(8,128)(2,1)S(1)}, u32[]{:S(2)}, u32[]{:S(2)}) collective-permute-start(bf16[800,128]{1,0:T(8,128)(2,1)S(1)} %collective-permute-done.8.refs_8_), channel_id=1, source_target_pairs={{0,480},{16,496},{32,0},{48,16},{64,32},{80,48},{96,64},{112,80},{... | collective-permute-start | bytes 614408 | tf_op jit(solution)/shard_map/ppermute | solution.py:108
  80.8 0.7 bitcast_dynamic-update-slice_fusion.5
  81.5 0.7 bitcast_dynamic-update-slice_fusion.4
  82.2 1.4 collective-permute-done.6.refs_0_.refs_9_
  83.6 1.2 collective-permute-done.9.refs_1_.refs_10_
  85.0 1.2 copy-done
  86.8 7.4 %all-to-all-start.2 = ((bf16[16,16,3200]{2,1,0:T(8,128)(2,1)}), bf16[16,16,3200]{2,1,0:T(8,128)(2,1)S(1)}, u32[]{:S(2)}, u32[]{:S(2)}) async-start(bf16[16,16,3200]{2,1,0:T(8,128)(2,1)} %bitcast.36), calls=%async_computation.2 | async-start | bytes 3276800 | tf_op jit(solution)/shard_map/all_to_all | solution.py:170
  94.3 1.9 %collective-permute-start.10 = (bf16[800,128]{1,0:T(8,128)(2,1)S(1)}, bf16[800,128]{1,0:T(8,128)(2,1)S(1)}, u32[]{:S(2)}, u32[]{:S(2)}) collective-permute-start(bf16[800,128]{1,0:T(8,128)(2,1)S(1)} %collective-permute-done.6.refs_0_.refs_9_), channel_id=1, source_target_pairs={{0,32},{16,48},{32,64},{48,80},{64,96},{80,112},{96,128},{112,144}... | collective-permute-start | bytes 614408 | tf_op jit(solution)/shard_map/ppermute | solution.py:108
  96.2 5.6 %collective-permute-start.11 = (bf16[800,128]{1,0:T(8,128)(2,1)S(1)}, bf16[800,128]{1,0:T(8,128)(2,1)S(1)}, u32[]{:S(2)}, u32[]{:S(2)}) collective-permute-start(bf16[800,128]{1,0:T(8,128)(2,1)S(1)} %collective-permute-done.9.refs_1_.refs_10_), channel_id=1, source_target_pairs={{0,480},{16,496},{32,0},{48,16},{64,32},{80,48},{96,64},{112,80},{... | collective-permute-start | bytes 614408 | tf_op jit(solution)/shard_map/ppermute | solution.py:108
  101.8 0.7 bitcast_dynamic-update-slice_fusion.3
  102.5 0.7 bitcast_dynamic-update-slice_fusion.2
  103.6 0.7 bitcast_dynamic-update-slice_fusion.1
  104.3 0.7 collective-permute-done.11.refs_12_
  105.1 0.7 bitcast_dynamic-update-slice_fusion
  105.8 1.9 %collective-permute-start.16 = (bf16[6,800,128]{2,1,0:T(8,128)(2,1)}, bf16[6,800,128]{2,1,0:T(8,128)(2,1)S(1)}, u32[]{:S(2)}, u32[]{:S(2)}) collective-permute-start(bf16[6,800,128]{2,1,0:T(8,128)(2,1)} %bitcast_dynamic-update-slice_fusion), channel_id=1, source_target_pairs={{0,16},{16,0},{32,48},{48,32},{64,80},{80,64},{96,112},{112,96},{1... | collective-permute-start | bytes 3686408 | tf_op jit(solution)/shard_map/ppermute | solution.py:128
  107.7 4.2 %collective-permute-start.12 = (bf16[800,128]{1,0:T(8,128)(2,1)S(1)}, bf16[800,128]{1,0:T(8,128)(2,1)S(1)}, u32[]{:S(2)}, u32[]{:S(2)}) collective-permute-start(bf16[800,128]{1,0:T(8,128)(2,1)S(1)} %collective-permute-done.10.refs_11_), channel_id=1, source_target_pairs={{0,32},{16,48},{32,64},{48,80},{64,96},{80,112},{96,128},{112,144}... | collective-permute-start | bytes 614408 | tf_op jit(solution)/shard_map/ppermute | solution.py:108
  111.9 3.3 %collective-permute-start.13 = (bf16[800,128]{1,0:T(8,128)(2,1)S(1)}, bf16[800,128]{1,0:T(8,128)(2,1)S(1)}, u32[]{:S(2)}, u32[]{:S(2)}) collective-permute-start(bf16[800,128]{1,0:T(8,128)(2,1)S(1)} %collective-permute-done.11.refs_12_), channel_id=1, source_target_pairs={{0,480},{16,496},{32,0},{48,16},{64,32},{80,48},{96,64},{112,80},{... | collective-permute-start | bytes 614408 | tf_op jit(solution)/shard_map/ppermute | solution.py:108
  115.3 3.8 %collective-permute-done.12.refs_13_ = bf16[800,128]{1,0:T(8,128)(2,1)S(1)} collective-permute-done((bf16[800,128]{1,0:T(8,128)(2,1)S(1)}, bf16[800,128]{1,0:T(8,128)(2,1)S(1)}, u32[]{:S(2)}, u32[]{:S(2)}) %collective-permute-start.12) | collective-permute-done | bytes 204832 | tf_op jit(solution)/shard_map/ppermute | solution.py:108
  119.0 2.2 %collective-permute-start.14 = (bf16[800,128]{1,0:T(8,128)(2,1)S(1)}, bf16[800,128]{1,0:T(8,128)(2,1)S(1)}, u32[]{:S(2)}, u32[]{:S(2)}) collective-permute-start(bf16[800,128]{1,0:T(8,128)(2,1)S(1)} %collective-permute-done.12.refs_13_), channel_id=1, source_target_pairs={{0,32},{16,48},{32,64},{48,80},{64,96},{80,112},{96,128},{112,144}... | collective-permute-start | bytes 614408 | tf_op jit(solution)/shard_map/ppermute | solution.py:108
  121.3 7.7 %collective-permute-done.14.refs_15_ = bf16[800,128]{1,0:T(8,128)(2,1)S(1)} collective-permute-done((bf16[800,128]{1,0:T(8,128)(2,1)S(1)}, bf16[800,128]{1,0:T(8,128)(2,1)S(1)}, u32[]{:S(2)}, u32[]{:S(2)}) %collective-permute-start.14) | collective-permute-done | bytes 204832 | tf_op jit(solution)/shard_map/ppermute | solution.py:108
  129.1 1.9 %collective-permute-start.17 = (bf16[3,800,128]{2,1,0:T(8,128)(2,1)S(1)}, bf16[3,800,128]{2,1,0:T(8,128)(2,1)S(1)}, u32[]{:S(2)}, u32[]{:S(2)}) collective-permute-start(bf16[3,800,128]{2,1,0:T(8,128)(2,1)S(1)} %pad_maximum_fusion), channel_id=1, source_target_pairs={{0,16},{16,0},{32,48},{48,32},{64,80},{80,64},{96,112},{112,96},{1... | collective-permute-start | bytes 1843208 | tf_op jit(solution)/shard_map/ppermute | solution.py:128
  131.1 2.0 %collective-permute-done.17.refs_18_ = bf16[3,800,128]{2,1,0:T(8,128)(2,1)S(1)} collective-permute-done((bf16[3,800,128]{2,1,0:T(8,128)(2,1)S(1)}, bf16[3,800,128]{2,1,0:T(8,128)(2,1)S(1)}, u32[]{:S(2)}, u32[]{:S(2)}) %collective-permute-start.17) | collective-permute-done | bytes 614432 | tf_op jit(solution)/shard_map/ppermute | solution.py:128
  133.1 0.8 copy-done.17
  133.9 1.1 copy-done.1
  135.0 1.3 copy-done.2
  136.3 0.9 copy-done.4
  137.2 0.9 copy-done.6
  138.1 0.9 copy-done.8
  139.0 0.9 copy-done.10
  140.0 0.9 copy-done.12
  140.9 0.9 copy-done.14
  141.8 0.9 copy-done.16
  142.8 1.1 copy-done.18
  143.8 14.4 %shard_map.68 = bf16[256,3200]{1,0:T(8,128)(2,1)} custom-call(bf16[256,3200]{1,0:T(8,128)(2,1)S(1)} %bitcast.34, bf16[800,128]{1,0:T(8,128)(2,1)S(1)} %shard_map.65.refs_0_, bf16[800,128]{1,0:T(8,128)(2,1)S(1)} %collective-permute-done.refs_1_, bf16[800,128]{1,0:T(8,128)(2,1)S(1)} %copy-done.4, bf16[800,128]{1,0:T(8,128)(2,1)S(1)} %collective-permute-done.1.refs_0_.refs_3_, ...), custom_call_target="tpu_custom_call" | custom-call | flops 1310720000 | bytes 10485760 | tf_op jit(solution)/shard_map/pallas_call | solution.py:171
  158.3 7.4 %all-to-all-start.3 = ((bf16[16,16,3200]{2,1,0:T(8,128)(2,1)}), bf16[16,16,3200]{2,1,0:T(8,128)(2,1)S(1)}, u32[]{:S(2)}, u32[]{:S(2)}) async-start(bf16[16,16,3200]{2,1,0:T(8,128)(2,1)} %bitcast.19), calls=%async_computation.3 | async-start | bytes 3276800 | tf_op jit(solution)/shard_map/all_to_all | solution.py:182
  165.7 22.6 %all-to-all-done.3 = bf16[16,16,3200]{2,1,0:T(8,128)(2,1)S(1)} async-done(((bf16[16,16,3200]{2,1,0:T(8,128)(2,1)}), bf16[16,16,3200]{2,1,0:T(8,128)(2,1)S(1)}, u32[]{:S(2)}, u32[]{:S(2)}) %all-to-all-start.3) | async-done | bytes 1638432 | tf_op jit(solution)/shard_map/all_to_all | solution.py:182
  188.3 0.9 shard_map.69
  (54 shorter events, 1.5 us)
Async XLA Ops:
  0.0 0.9 copy-start.20
  0.9 0.9 copy-start.21
  1.8 46.8 %copy-start.24 = (s32[64]{0:T(128)S(1)}, s32[64]{0:T(128)}, u32[]{:S(2)}) copy-start(s32[64]{0:T(128)} %plan_ref.1) | copy-start | bytes 772
  1.9 25.6 %collective-permute-start = (bf16[800,128]{1,0:T(8,128)(2,1)S(1)}, bf16[800,128]{1,0:T(8,128)(2,1)S(1)}, u32[]{:S(2)}, u32[]{:S(2)}) collective-permute-start(bf16[800,128]{1,0:T(8,128)(2,1)S(1)} %shard_map.65.refs_0_), channel_id=1, source_target_pairs={{0,32},{16,48},{32,64},{48,80},{64,96},{80,112},{96,128},{112,144}... | collective-permute-start | bytes 614408 | tf_op jit(solution)/shard_map/ppermute | solution.py:108
  5.7 25.5 %collective-permute-start.2 = (bf16[800,128]{1,0:T(8,128)(2,1)S(1)}, bf16[800,128]{1,0:T(8,128)(2,1)S(1)}, u32[]{:S(2)}, u32[]{:S(2)}) collective-permute-start(bf16[800,128]{1,0:T(8,128)(2,1)S(1)} %shard_map.65.refs_0_), channel_id=1, source_target_pairs={{0,480},{16,496},{32,0},{48,16},{64,32},{80,48},{96,64},{112,80},{... | collective-permute-start | bytes 614408 | tf_op jit(solution)/shard_map/ppermute | solution.py:108
  15.2 0.9 copy-start.19
  16.8 31.8 %all-to-all-start = ((bf16[64,8,128]{2,1,0:T(8,128)(2,1)}), bf16[64,8,128]{2,1,0:T(8,128)(2,1)S(1)}, u32[]{:S(2)}, u32[]{:S(2)}) async-start(bf16[64,8,128]{2,1,0:T(8,128)(2,1)} %shard_map.64), calls=%async_computation | async-start | bytes 262144 | tf_op jit(solution)/shard_map/all_to_all | solution.py:155
  27.4 12.6 %collective-permute-start.1 = (bf16[800,128]{1,0:T(8,128)(2,1)S(1)}, bf16[800,128]{1,0:T(8,128)(2,1)S(1)}, u32[]{:S(2)}, u32[]{:S(2)}) collective-permute-start(bf16[800,128]{1,0:T(8,128)(2,1)S(1)} %collective-permute-done.refs_1_), channel_id=1, source_target_pairs={{0,32},{16,48},{32,64},{48,80},{64,96},{80,112},{96,128},{112,144}... | collective-permute-start | bytes 614408 | tf_op jit(solution)/shard_map/ppermute | solution.py:108
  31.1 36.3 %copy-start.3 = (bf16[800,128]{1,0:T(8,128)(2,1)}, bf16[800,128]{1,0:T(8,128)(2,1)S(1)}, u32[]{:S(2)}) copy-start(bf16[800,128]{1,0:T(8,128)(2,1)S(1)} %collective-permute-done.2.refs_2_) | copy-start | bytes 614404
  31.2 11.2 %collective-permute-start.3 = (bf16[800,128]{1,0:T(8,128)(2,1)S(1)}, bf16[800,128]{1,0:T(8,128)(2,1)S(1)}, u32[]{:S(2)}, u32[]{:S(2)}) collective-permute-start(bf16[800,128]{1,0:T(8,128)(2,1)S(1)} %collective-permute-done.2.refs_2_), channel_id=1, source_target_pairs={{0,480},{16,496},{32,0},{48,16},{64,32},{80,48},{96,64},{112,80},{... | collective-permute-start | bytes 614408 | tf_op jit(solution)/shard_map/ppermute | solution.py:108
  40.1 19.5 %collective-permute-start.4 = (bf16[800,128]{1,0:T(8,128)(2,1)S(1)}, bf16[800,128]{1,0:T(8,128)(2,1)S(1)}, u32[]{:S(2)}, u32[]{:S(2)}) collective-permute-start(bf16[800,128]{1,0:T(8,128)(2,1)S(1)} %collective-permute-done.1.refs_0_.refs_3_), channel_id=1, source_target_pairs={{0,32},{16,48},{32,64},{48,80},{64,96},{80,112},{96,128},{112,144}... | collective-permute-start | bytes 614408 | tf_op jit(solution)/shard_map/ppermute | solution.py:108
  42.4 20.9 %collective-permute-start.7 = (bf16[800,128]{1,0:T(8,128)(2,1)S(1)}, bf16[800,128]{1,0:T(8,128)(2,1)S(1)}, u32[]{:S(2)}, u32[]{:S(2)}) collective-permute-start(bf16[800,128]{1,0:T(8,128)(2,1)S(1)} %collective-permute-done.3.refs_1_.refs_4_), channel_id=1, source_target_pairs={{0,480},{16,496},{32,0},{48,16},{64,32},{80,48},{96,64},{112,80},{... | collective-permute-start | bytes 614408 | tf_op jit(solution)/shard_map/ppermute | solution.py:108
  49.8 32.4 %all-to-all-start.1 = ((bf16[64,8,128]{2,1,0:T(8,128)(2,1)}), bf16[64,8,128]{2,1,0:T(8,128)(2,1)S(1)}, u32[]{:S(2)}, u32[]{:S(2)}) async-start(bf16[64,8,128]{2,1,0:T(8,128)(2,1)} %shard_map.66), calls=%async_computation.1 | async-start | bytes 262144 | tf_op jit(solution)/shard_map/all_to_all | solution.py:158
  59.6 16.2 %copy-start.5 = (bf16[800,128]{1,0:T(8,128)(2,1)}, bf16[800,128]{1,0:T(8,128)(2,1)S(1)}, u32[]{:S(2)}) copy-start(bf16[800,128]{1,0:T(8,128)(2,1)S(1)} %collective-permute-done.4.refs_5_) | copy-start | bytes 614404
  59.6 14.1 %collective-permute-start.5 = (bf16[800,128]{1,0:T(8,128)(2,1)S(1)}, bf16[800,128]{1,0:T(8,128)(2,1)S(1)}, u32[]{:S(2)}, u32[]{:S(2)}) collective-permute-start(bf16[800,128]{1,0:T(8,128)(2,1)S(1)} %collective-permute-done.4.refs_5_), channel_id=1, source_target_pairs={{0,32},{16,48},{32,64},{48,80},{64,96},{80,112},{96,128},{112,144}... | collective-permute-start | bytes 614408 | tf_op jit(solution)/shard_map/ppermute | solution.py:108
  63.3 23.5 %copy-start.7 = (bf16[800,128]{1,0:T(8,128)(2,1)}, bf16[800,128]{1,0:T(8,128)(2,1)S(1)}, u32[]{:S(2)}) copy-start(bf16[800,128]{1,0:T(8,128)(2,1)S(1)} %collective-permute-done.7.refs_6_) | copy-start | bytes 614404
  63.3 12.5 %collective-permute-start.8 = (bf16[800,128]{1,0:T(8,128)(2,1)S(1)}, bf16[800,128]{1,0:T(8,128)(2,1)S(1)}, u32[]{:S(2)}, u32[]{:S(2)}) collective-permute-start(bf16[800,128]{1,0:T(8,128)(2,1)S(1)} %collective-permute-done.7.refs_6_), channel_id=1, source_target_pairs={{0,480},{16,496},{32,0},{48,16},{64,32},{80,48},{96,64},{112,80},{... | collective-permute-start | bytes 614408 | tf_op jit(solution)/shard_map/ppermute | solution.py:108
  68.1 62.9 %collective-permute-start.15 = (bf16[7,800,128]{2,1,0:T(8,128)(2,1)}, bf16[7,800,128]{2,1,0:T(8,128)(2,1)}, u32[]{:S(2)}, u32[]{:S(2)}) collective-permute-start(bf16[7,800,128]{2,1,0:T(8,128)(2,1)} %bitcast_dynamic-update-slice_fusion.6), channel_id=1, source_target_pairs={{0,16},{16,0},{32,48},{48,32},{64,80},{80,64},{96,112},{112,96},{1... | collective-permute-start | bytes 4300808 | tf_op jit(solution)/shard_map/ppermute | solution.py:128
  73.7 13.1 %copy-start.9 = (bf16[800,128]{1,0:T(8,128)(2,1)}, bf16[800,128]{1,0:T(8,128)(2,1)S(1)}, u32[]{:S(2)}) copy-start(bf16[800,128]{1,0:T(8,128)(2,1)S(1)} %collective-permute-done.5.refs_7_) | copy-start | bytes 614404
  73.7 9.9 %collective-permute-start.6 = (bf16[800,128]{1,0:T(8,128)(2,1)S(1)}, bf16[800,128]{1,0:T(8,128)(2,1)S(1)}, u32[]{:S(2)}, u32[]{:S(2)}) collective-permute-start(bf16[800,128]{1,0:T(8,128)(2,1)S(1)} %collective-permute-done.5.refs_7_), channel_id=1, source_target_pairs={{0,32},{16,48},{32,64},{48,80},{64,96},{80,112},{96,128},{112,144}... | collective-permute-start | bytes 614408 | tf_op jit(solution)/shard_map/ppermute | solution.py:108
  75.8 11.0 %copy-start.11 = (bf16[800,128]{1,0:T(8,128)(2,1)}, bf16[800,128]{1,0:T(8,128)(2,1)S(1)}, u32[]{:S(2)}) copy-start(bf16[800,128]{1,0:T(8,128)(2,1)S(1)} %collective-permute-done.8.refs_8_) | copy-start | bytes 614404
  75.8 9.0 %collective-permute-start.9 = (bf16[800,128]{1,0:T(8,128)(2,1)S(1)}, bf16[800,128]{1,0:T(8,128)(2,1)S(1)}, u32[]{:S(2)}, u32[]{:S(2)}) collective-permute-start(bf16[800,128]{1,0:T(8,128)(2,1)S(1)} %collective-permute-done.8.refs_8_), channel_id=1, source_target_pairs={{0,480},{16,496},{32,0},{48,16},{64,32},{80,48},{96,64},{112,80},{... | collective-permute-start | bytes 614408 | tf_op jit(solution)/shard_map/ppermute | solution.py:108
  85.0 1.2 copy-start
  86.2 0.6 copy-start.22
  86.8 48.1 %all-to-all-start.2 = ((bf16[16,16,3200]{2,1,0:T(8,128)(2,1)}), bf16[16,16,3200]{2,1,0:T(8,128)(2,1)S(1)}, u32[]{:S(2)}, u32[]{:S(2)}) async-start(bf16[16,16,3200]{2,1,0:T(8,128)(2,1)} %bitcast.36), calls=%async_computation.2 | async-start | bytes 3276800 | tf_op jit(solution)/shard_map/all_to_all | solution.py:170
  94.3 9.3 %collective-permute-start.10 = (bf16[800,128]{1,0:T(8,128)(2,1)S(1)}, bf16[800,128]{1,0:T(8,128)(2,1)S(1)}, u32[]{:S(2)}, u32[]{:S(2)}) collective-permute-start(bf16[800,128]{1,0:T(8,128)(2,1)S(1)} %collective-permute-done.6.refs_0_.refs_9_), channel_id=1, source_target_pairs={{0,32},{16,48},{32,64},{48,80},{64,96},{80,112},{96,128},{112,144}... | collective-permute-start | bytes 614408 | tf_op jit(solution)/shard_map/ppermute | solution.py:108
  96.2 8.9 %collective-permute-start.11 = (bf16[800,128]{1,0:T(8,128)(2,1)S(1)}, bf16[800,128]{1,0:T(8,128)(2,1)S(1)}, u32[]{:S(2)}, u32[]{:S(2)}) collective-permute-start(bf16[800,128]{1,0:T(8,128)(2,1)S(1)} %collective-permute-done.9.refs_1_.refs_10_), channel_id=1, source_target_pairs={{0,480},{16,496},{32,0},{48,16},{64,32},{80,48},{96,64},{112,80},{... | collective-permute-start | bytes 614408 | tf_op jit(solution)/shard_map/ppermute | solution.py:108
  103.6 11.7 %copy-start.13 = (bf16[800,128]{1,0:T(8,128)(2,1)}, bf16[800,128]{1,0:T(8,128)(2,1)S(1)}, u32[]{:S(2)}) copy-start(bf16[800,128]{1,0:T(8,128)(2,1)S(1)} %collective-permute-done.10.refs_11_) | copy-start | bytes 614404
  105.1 24.0 %copy-start.15 = (bf16[800,128]{1,0:T(8,128)(2,1)}, bf16[800,128]{1,0:T(8,128)(2,1)S(1)}, u32[]{:S(2)}) copy-start(bf16[800,128]{1,0:T(8,128)(2,1)S(1)} %collective-permute-done.11.refs_12_) | copy-start | bytes 614404
  105.8 28.1 %collective-permute-start.16 = (bf16[6,800,128]{2,1,0:T(8,128)(2,1)}, bf16[6,800,128]{2,1,0:T(8,128)(2,1)S(1)}, u32[]{:S(2)}, u32[]{:S(2)}) collective-permute-start(bf16[6,800,128]{2,1,0:T(8,128)(2,1)} %bitcast_dynamic-update-slice_fusion), channel_id=1, source_target_pairs={{0,16},{16,0},{32,48},{48,32},{64,80},{80,64},{96,112},{112,96},{1... | collective-permute-start | bytes 3686408 | tf_op jit(solution)/shard_map/ppermute | solution.py:128
  107.7 11.3 %collective-permute-start.12 = (bf16[800,128]{1,0:T(8,128)(2,1)S(1)}, bf16[800,128]{1,0:T(8,128)(2,1)S(1)}, u32[]{:S(2)}, u32[]{:S(2)}) collective-permute-start(bf16[800,128]{1,0:T(8,128)(2,1)S(1)} %collective-permute-done.10.refs_11_), channel_id=1, source_target_pairs={{0,32},{16,48},{32,64},{48,80},{64,96},{80,112},{96,128},{112,144}... | collective-permute-start | bytes 614408 | tf_op jit(solution)/shard_map/ppermute | solution.py:108
  111.9 9.4 %collective-permute-start.13 = (bf16[800,128]{1,0:T(8,128)(2,1)S(1)}, bf16[800,128]{1,0:T(8,128)(2,1)S(1)}, u32[]{:S(2)}, u32[]{:S(2)}) collective-permute-start(bf16[800,128]{1,0:T(8,128)(2,1)S(1)} %collective-permute-done.11.refs_12_), channel_id=1, source_target_pairs={{0,480},{16,496},{32,0},{48,16},{64,32},{80,48},{96,64},{112,80},{... | collective-permute-start | bytes 614408 | tf_op jit(solution)/shard_map/ppermute | solution.py:108
  119.0 10.0 %collective-permute-start.14 = (bf16[800,128]{1,0:T(8,128)(2,1)S(1)}, bf16[800,128]{1,0:T(8,128)(2,1)S(1)}, u32[]{:S(2)}, u32[]{:S(2)}) collective-permute-start(bf16[800,128]{1,0:T(8,128)(2,1)S(1)} %collective-permute-done.12.refs_13_), channel_id=1, source_target_pairs={{0,32},{16,48},{32,64},{48,80},{64,96},{80,112},{96,128},{112,144}... | collective-permute-start | bytes 614408 | tf_op jit(solution)/shard_map/ppermute | solution.py:108
  129.1 3.9 %collective-permute-start.17 = (bf16[3,800,128]{2,1,0:T(8,128)(2,1)S(1)}, bf16[3,800,128]{2,1,0:T(8,128)(2,1)S(1)}, u32[]{:S(2)}, u32[]{:S(2)}) collective-permute-start(bf16[3,800,128]{2,1,0:T(8,128)(2,1)S(1)} %pad_maximum_fusion), channel_id=1, source_target_pairs={{0,16},{16,0},{32,48},{48,32},{64,80},{80,64},{96,112},{112,96},{1... | collective-permute-start | bytes 1843208 | tf_op jit(solution)/shard_map/ppermute | solution.py:128
  133.1 0.8 copy-start.17
  133.9 1.1 copy-start.1
  135.0 1.3 copy-start.2
  136.3 0.9 copy-start.4
  137.2 0.9 copy-start.6
  138.1 0.9 copy-start.8
  139.0 0.9 copy-start.10
  140.0 0.9 copy-start.12
  140.9 0.9 copy-start.14
  141.8 0.9 copy-start.16
  142.8 1.1 copy-start.18
  158.3 7.4 %copy-start.25 = (f32[3200]{0:T(1024)S(1)}, f32[3200]{0:T(1024)}, u32[]{:S(2)}) copy-start(f32[3200]{0:T(1024)} %param.11) | copy-start | bytes 38404
  158.3 30.0 %copy-start.23 = (bf16[2,8,3200]{2,1,0:T(8,128)(2,1)S(1)}, bf16[2,8,3200]{2,1,0:T(8,128)(2,1)}, u32[]{:S(2)}) copy-start(bf16[2,8,3200]{2,1,0:T(8,128)(2,1)} %copy-done.22) | copy-start | bytes 307204
  158.3 30.0 %all-to-all-start.3 = ((bf16[16,16,3200]{2,1,0:T(8,128)(2,1)}), bf16[16,16,3200]{2,1,0:T(8,128)(2,1)S(1)}, u32[]{:S(2)}, u32[]{:S(2)}) async-start(bf16[16,16,3200]{2,1,0:T(8,128)(2,1)} %bitcast.19), calls=%async_computation.3 | async-start | bytes 3276800 | tf_op jit(solution)/shard_map/all_to_all | solution.py:182

commit v4 on v2

--- a/solution.py
+++ b/solution.py
@@ -9,17 +9,18 @@
 
 LANE = 128
 VMEM = pl.BlockSpec(memory_space=pltpu.VMEM)
+ANY = pl.BlockSpec(memory_space=pl.ANY)
 SMEM = pl.BlockSpec(memory_space=pltpu.SMEM)
 
 
-def call(body, out_shape, in_specs, flops=0, moved=0, n_out=1, scratch=()):
+def call(body, out_shape, in_specs, flops=0, moved=0, n_out=1, scratch=(), limit=32):
     return pl.pallas_call(
         body,
         out_shape=out_shape,
         in_specs=in_specs,
         out_specs=VMEM if n_out == 1 else [VMEM] * n_out,
         scratch_shapes=list(scratch),
-        compiler_params=pltpu.CompilerParams(vmem_limit_bytes=40 * 1024 * 1024),
+        compiler_params=pltpu.CompilerParams(vmem_limit_bytes=limit * 1024 * 1024),
         cost_estimate=pl.CostEstimate(flops=flops, bytes_accessed=moved, transcendentals=0),
     )
 
@@ -55,30 +56,46 @@
 
 
 def pack_body(in_ref, out_ref, o_ref):
-    units, part = in_ref.shape
-    o_ref[:units, :part] = in_ref[...]
-    o_ref[units:, :part] = out_ref[...]
-    o_ref[:, part:] = jnp.zeros((2 * units, LANE - part), o_ref.dtype)
+    part = in_ref.shape[1]
+    kept = o_ref.shape[0] // 2
+    fold, chunk = kept // 4, part // 4
+    for k, ref in enumerate((in_ref, out_ref)):
+        at = k * kept
+        o_ref[at : at + kept, :part] = ref[:kept, :]
+        for j in range(4):
+            o_ref[at + j * fold : at + (j + 1) * fold, part : part + chunk] = ref[
+                kept:, j * chunk : (j + 1) * chunk
+            ]
+        o_ref[at : at + kept, part + chunk :] = jnp.zeros((kept, LANE - part - chunk), o_ref.dtype)
 
 
-def mlp_body(part, chunks, x_ref, w_ref, o_ref, held, sems):
-    sections, both, _ = w_ref.shape
-    units = both // 2
+def unpacked(packed, part):
+    fold, chunk = packed.shape[0] // 4, part // 4
+    rest = [packed[j * fold : (j + 1) * fold, part : part + chunk] for j in range(4)]
+    return jnp.concatenate([packed[:, :part], jnp.concatenate(rest, axis=1)], axis=0)
+
+
+def mlp_body(part, units, chunks, x_hbm, w_hbm, o_ref, x_ref, held, x_sem, sems):
+    sections, both, _ = held.shape
+    kept = both // 2
     size = sections // chunks
+    x_copy = pltpu.make_async_copy(x_hbm, x_ref, x_sem)
+    x_copy.start()
     copies = []
     for half in range(2):
         for c in range(chunks):
-            place = (pl.ds(c * size, size), pl.ds(half * units, units))
-            copy = pltpu.make_async_copy(w_ref.at[place], held.at[place], sems.at[half, c])
+            place = (pl.ds(c * size, size), pl.ds(half * kept, kept))
+            copy = pltpu.make_async_copy(w_hbm.at[place], held.at[place], sems.at[half, c])
             copy.start()
             copies.append(copy)
+    x_copy.wait()
     total = jnp.zeros((x_ref.shape[0], units), jnp.float32)
     for s in range(sections):
         if s % size == 0:
             copies[s // size].wait()
         total += lax.dot_general(
             x_ref[:, s * part : (s + 1) * part],
-            held[s, :units, :part],
+            unpacked(held[s, :kept, :], part),
             (((1,), (1,)), ((), ())),
             preferred_element_type=jnp.float32,
         )
@@ -88,7 +105,7 @@
         if s % size == 0:
             copies[chunks + s // size].wait()
         o_ref[:, s * part : (s + 1) * part] = jnp.dot(
-            hidden, held[s, units:, :part], preferred_element_type=jnp.float32
+            hidden, unpacked(held[s, kept:, :], part), preferred_element_type=jnp.float32
         ).astype(jnp.bfloat16)
 
 
@@ -106,9 +123,10 @@
     blocks, rows, width = patches.shape
     bf16 = jnp.bfloat16
     part, units = proj_in.shape
-    weights = call(pack_body, jax.ShapeDtypeStruct((2 * units, LANE), bf16), [VMEM, VMEM])(
-        proj_in.T, proj_out
-    )
+    kept = units * 4 // 5
+    weights = call(
+        pack_body, jax.ShapeDtypeStruct((2 * kept, LANE), bf16), [VMEM, VMEM], limit=60
+    )(proj_in.T, proj_out)
     weights = lax.all_gather(weights, "section", axis=0, tiled=False)
 
     shape = jax.ShapeDtypeStruct((sections * blocks, rows, LANE), bf16)
@@ -130,15 +148,18 @@
     normed = lax.all_to_all(copies.reshape(all_rows, width), "tensor", 0, 0, tiled=True)
     chunks = 4
     partial_sum = call(
-        functools.partial(mlp_body, part, chunks),
+        functools.partial(mlp_body, part, units, chunks),
         jax.ShapeDtypeStruct((all_rows, width), bf16),
-        [VMEM, pl.BlockSpec(memory_space=pltpu.HBM)],
+        [ANY, ANY],
         flops=4 * all_rows * width * units,
         moved=10 * 1024 * 1024,
         scratch=[
-            pltpu.VMEM((sections, 2 * units, LANE), bf16),
+            pltpu.VMEM((all_rows, width), bf16),
+            pltpu.VMEM((sections, 2 * kept, LANE), bf16),
+            pltpu.SemaphoreType.DMA(()),
             pltpu.SemaphoreType.DMA((2, chunks)),
         ],
+        limit=60,
     )(normed, weights)
     terms = lax.all_to_all(partial_sum, "tensor", 0, 0, tiled=True)
     return call(

time: 147 us -> 144 us (0.980)
  local copies, waits for them, and re-layouts: 6.22 us -> 2.29 us
  Pallas kernels: 10.6 us -> 14.3 us
    unnamed x14 -> x6, local copies, waits for them, and re-layouts: 6.2 us -> 1.55 us
    pallas_call x2, Pallas kernels: 8.21 us -> 12 us  [the longest x1 10.2 us: local(): call(functools.partial(mlp_body, part, units, chunks), jax.ShapeDtypeStru...]
  transfers between devices with their start and end apart: 3 -> 3, of which waited for: 3 -> 2; matrix products, arithmetic and copies ran while one was open for 0% -> 1% of each run, Pallas kernels for 1% -> 1%
where the time goes in v4:
time: 144 us; the launch traced here: 142 us
  blocking collectives  61.4 us (43%)
  waiting for transfers between devices  40.6 us (28%)
  Pallas kernels  14.3 us (10%)
  between operations  13.5 us (9%)
  starting transfers between devices  10.1 us (7%)
  local copies, waits for them, and re-layouts  2.29 us (2%)
    all_to_all x1, blocking collectives, local(): tiles = lax.all_to_all(tiles, 'section', 0, 0, tiled=True)  32.5 us
    all_to_all x1, blocking collectives, local(): lax.all_to_all(copies.reshape(all_rows, width), 'tensor', 0, 0, tiled=True)  29 us
    all_to_all x1, waiting for transfers between devices, local(): terms = lax.all_to_all(partial_sum, 'tensor', 0, 0, tiled=True)  22.7 us
    all_to_all x1, waiting for transfers between devices, local(): tiles = lax.all_to_all(tiles, 'section', 0, 0, tiled=True)  17.8 us
    pallas_call x1, Pallas kernels, local(): call(functools.partial(mlp_body, part, units, chunks), jax.ShapeDtypeStru...  10.2 us
    all_to_all x1, starting transfers between devices, local(): terms = lax.all_to_all(partial_sum, 'tensor', 0, 0, tiled=True)  6.22 us
    all_to_all x1, starting transfers between devices, local(): tiles = lax.all_to_all(tiles, 'section', 0, 0, tiled=True)  3.85 us
  transfers between devices with their start and end apart: 3, of which 2 were waited for; matrix products, arithmetic and copies ran while one was open for 1% of the time, Pallas kernels for 1%

profile of v4, /device:TPU:6, one launch (start us, length us, event | category | flops | bytes accessed | tf_op | source)
XLA Modules:
  0.0 142.1 jit_solution(5790471751539309297)
XLA Ops:
  6.5 0.0 all-gather.3.cloned.1.call-start
  6.5 1.8 %shard_map.67 = bf16[640,128]{1,0:T(8,128)(2,1)} custom-call(bf16[400,100]{1,0:T(8,128)(2,1)} %bitcast.11, bf16[400,100]{1,0:T(8,128)(2,1)} %out_ref.1), custom_call_target="tpu_custom_call" | custom-call | tf_op jit(solution)/shard_map/pallas_call | solution.py:127
  8.3 0.0 all-gather.3.cloned.1.call-update
  8.3 0.0 copy-start
  8.3 0.9 copy-done
  9.2 32.5 %all_to_all.30.x_ref = bf16[64,8,128]{2,1,0:T(8,128)(2,1)S(1)} all-to-all(bf16[64,8,128]{2,1,0:T(8,128)(2,1)S(1)} %shard_map.64), channel_id=1, replica_groups=mesh['section'=32,'tensor'=16] {'section'}, dimensions={0} | all-to-all | bytes 262144 | tf_op jit(solution)/shard_map/all_to_all | solution.py:134
  41.7 0.0 copy-start.1
  41.7 0.7 copy-done.1
  42.4 1.2 shard_map.65
  43.6 3.8 %all-to-all-start.1 = ((bf16[64,8,128]{2,1,0:T(8,128)(2,1)}), bf16[64,8,128]{2,1,0:T(8,128)(2,1)S(1)}, u32[]{:S(2)}, u32[]{:S(2)}) async-start(bf16[64,8,128]{2,1,0:T(8,128)(2,1)} %shard_map.65), calls=%async_computation.1 | async-start | bytes 262144 | tf_op jit(solution)/shard_map/all_to_all | solution.py:136
  47.5 0.7 reshape.16.gain_ref
  48.2 17.8 %all-to-all-done.1.x_ref = bf16[64,8,128]{2,1,0:T(8,128)(2,1)S(1)} async-done(((bf16[64,8,128]{2,1,0:T(8,128)(2,1)}), bf16[64,8,128]{2,1,0:T(8,128)(2,1)S(1)}, u32[]{:S(2)}, u32[]{:S(2)}) %all-to-all-start.1) | async-done | bytes 131104 | tf_op jit(solution)/shard_map/all_to_all | solution.py:136
  66.0 0.2 shard_map.66
  66.3 29.0 %all_to_all.31 = bf16[16,16,3200]{2,1,0:T(8,128)(2,1)} all-to-all(bf16[16,16,3200]{2,1,0:T(8,128)(2,1)S(1)} %bitcast.7), channel_id=1, replica_groups=mesh['section'=32,'tensor'=16] {'tensor'}, dimensions={0} | all-to-all | bytes 3276800 | tf_op jit(solution)/shard_map/all_to_all | solution.py:148
  95.2 0.0 all-gather.3.cloned.1.call-done
  95.2 10.2 %shard_map.68 = bf16[256,3200]{1,0:T(8,128)(2,1)} custom-call(bf16[256,3200]{1,0:T(8,128)(2,1)} %bitcast.9, bf16[32,640,128]{2,1,0:T(8,128)(2,1)} %bitcast.10), custom_call_target="tpu_custom_call" | custom-call | flops 1310720000 | bytes 10485760 | tf_op jit(solution)/shard_map/pallas_call | solution.py:150
  105.5 0.0 copy-start.2
  105.5 6.2 %all-to-all-start.3 = ((bf16[16,16,3200]{2,1,0:T(8,128)(2,1)}), bf16[16,16,3200]{2,1,0:T(8,128)(2,1)S(1)}, u32[]{:S(2)}, u32[]{:S(2)}) async-start(bf16[16,16,3200]{2,1,0:T(8,128)(2,1)} %bitcast.8), calls=%async_computation.3 | async-start | bytes 3276800 | tf_op jit(solution)/shard_map/all_to_all | solution.py:164
  111.7 0.0 copy-done.2
  111.7 22.7 %all-to-all-done.3 = bf16[16,16,3200]{2,1,0:T(8,128)(2,1)S(1)} async-done(((bf16[16,16,3200]{2,1,0:T(8,128)(2,1)}), bf16[16,16,3200]{2,1,0:T(8,128)(2,1)S(1)}, u32[]{:S(2)}, u32[]{:S(2)}) %all-to-all-start.3) | async-done | bytes 1638432 | tf_op jit(solution)/shard_map/all_to_all | solution.py:164
  134.4 0.9 shard_map.69
  (2 shorter events, 0.0 us)
Async XLA Ops:
  6.5 88.7 %all-gather.3.cloned.1.call-start = ((), (), s32[]{:S(2)}) async-start(), calls=%async_computation.4 | async-start | bytes 5406720 | tf_op jit(solution)/shard_map/all_gather | solution.py:130
  8.3 0.9 copy-start
  41.7 0.7 copy-start.1
  43.6 22.4 %all-to-all-start.1 = ((bf16[64,8,128]{2,1,0:T(8,128)(2,1)}), bf16[64,8,128]{2,1,0:T(8,128)(2,1)S(1)}, u32[]{:S(2)}, u32[]{:S(2)}) async-start(bf16[64,8,128]{2,1,0:T(8,128)(2,1)} %shard_map.65), calls=%async_computation.1 | async-start | bytes 262144 | tf_op jit(solution)/shard_map/all_to_all | solution.py:136
  105.5 6.2 %copy-start.2 = (f32[3200]{0:T(1024)S(1)}, f32[3200]{0:T(1024)}, u32[]{:S(2)}) copy-start(f32[3200]{0:T(1024)} %param.11) | copy-start | bytes 38404
  105.5 29.0 %all-to-all-start.3 = ((bf16[16,16,3200]{2,1,0:T(8,128)(2,1)}), bf16[16,16,3200]{2,1,0:T(8,128)(2,1)S(1)}, u32[]{:S(2)}, u32[]{:S(2)}) async-start(bf16[16,16,3200]{2,1,0:T(8,128)(2,1)} %bitcast.8), calls=%async_computation.3 | async-start | bytes 3276800 | tf_op jit(solution)/shard_map/all_to_all | solution.py:164
Sparse Core Ops, SparseCore 0:
  9.5 84.8 all-gather.2

commit v5 on v2

--- a/solution.py
+++ b/solution.py
@@ -9,17 +9,18 @@
 
 LANE = 128
 VMEM = pl.BlockSpec(memory_space=pltpu.VMEM)
+ANY = pl.BlockSpec(memory_space=pl.ANY)
 SMEM = pl.BlockSpec(memory_space=pltpu.SMEM)
 
 
-def call(body, out_shape, in_specs, flops=0, moved=0, n_out=1, scratch=()):
+def call(body, out_shape, in_specs, flops=0, moved=0, n_out=1, scratch=(), limit=32):
     return pl.pallas_call(
         body,
         out_shape=out_shape,
         in_specs=in_specs,
         out_specs=VMEM if n_out == 1 else [VMEM] * n_out,
         scratch_shapes=list(scratch),
-        compiler_params=pltpu.CompilerParams(vmem_limit_bytes=40 * 1024 * 1024),
+        compiler_params=pltpu.CompilerParams(vmem_limit_bytes=limit * 1024 * 1024),
         cost_estimate=pl.CostEstimate(flops=flops, bytes_accessed=moved, transcendentals=0),
     )
 
@@ -61,35 +62,43 @@
     o_ref[:, part:] = jnp.zeros((2 * units, LANE - part), o_ref.dtype)
 
 
-def mlp_body(part, chunks, x_ref, w_ref, o_ref, held, sems):
-    sections, both, _ = w_ref.shape
+def mlp_body(part, x_hbm, w_hbm, o_ref, x_ref, spread, held, x_sem, in_sem, out_sem):
+    sections, both, _ = held.shape
     units = both // 2
-    size = sections // chunks
-    copies = []
-    for half in range(2):
-        for c in range(chunks):
-            place = (pl.ds(c * size, size), pl.ds(half * units, units))
-            copy = pltpu.make_async_copy(w_ref.at[place], held.at[place], sems.at[half, c])
-            copy.start()
-            copies.append(copy)
-    total = jnp.zeros((x_ref.shape[0], units), jnp.float32)
+    rows = x_ref.shape[0]
+    x_copy = pltpu.make_async_copy(x_hbm, x_ref, x_sem)
+    x_copy.start()
+    first, second = pl.ds(0, units), pl.ds(units, units)
+    in_copy = pltpu.make_async_copy(w_hbm.at[:, first], held.at[:, first], in_sem)
+    in_copy.start()
+    out_copy = pltpu.make_async_copy(w_hbm.at[:, second], held.at[:, second], out_sem)
+    out_copy.start()
+    x_copy.wait()
+    blank = jnp.zeros((rows, LANE - part), x_ref.dtype)
     for s in range(sections):
-        if s % size == 0:
-            copies[s // size].wait()
+        spread[:, s * LANE : (s + 1) * LANE] = jnp.concatenate(
+            [x_ref[:, s * part : (s + 1) * part], blank], axis=1
+        )
+    in_copy.wait()
+    total = jnp.zeros((rows, units), jnp.float32)
+    for s in range(0, sections, 2):
         total += lax.dot_general(
-            x_ref[:, s * part : (s + 1) * part],
-            held[s, :units, :part],
+            spread[:, s * LANE : (s + 2) * LANE],
+            jnp.concatenate([held[s, :units, :], held[s + 1, :units, :]], axis=1),
             (((1,), (1,)), ((), ())),
             preferred_element_type=jnp.float32,
         )
     hidden = 0.5 * total * (1.0 + lax.erf(total * (0.5**0.5)))
     hidden = hidden.astype(jnp.bfloat16)
-    for s in range(sections):
-        if s % size == 0:
-            copies[chunks + s // size].wait()
-        o_ref[:, s * part : (s + 1) * part] = jnp.dot(
-            hidden, held[s, units:, :part], preferred_element_type=jnp.float32
+    out_copy.wait()
+    for s in range(0, sections, 2):
+        product = jnp.dot(
+            hidden,
+            jnp.concatenate([held[s, units:, :], held[s + 1, units:, :]], axis=1),
+            preferred_element_type=jnp.float32,
         ).astype(jnp.bfloat16)
+        for i in range(2):
+            o_ref[:, (s + i) * part : (s + i + 1) * part] = product[:, i * LANE : i * LANE + part]
 
 
 def sum_body(x_ref, rows_ref, scale_ref, o_ref):
@@ -106,9 +115,9 @@
     blocks, rows, width = patches.shape
     bf16 = jnp.bfloat16
     part, units = proj_in.shape
-    weights = call(pack_body, jax.ShapeDtypeStruct((2 * units, LANE), bf16), [VMEM, VMEM])(
-        proj_in.T, proj_out
-    )
+    weights = call(
+        pack_body, jax.ShapeDtypeStruct((2 * units, LANE), bf16), [VMEM, VMEM], limit=60
+    )(proj_in.T, proj_out)
     weights = lax.all_gather(weights, "section", axis=0, tiled=False)
 
     shape = jax.ShapeDtypeStruct((sections * blocks, rows, LANE), bf16)
@@ -128,17 +137,21 @@
 
     all_rows = groups * blocks * rows
     normed = lax.all_to_all(copies.reshape(all_rows, width), "tensor", 0, 0, tiled=True)
-    chunks = 4
     partial_sum = call(
-        functools.partial(mlp_body, part, chunks),
+        functools.partial(mlp_body, part),
         jax.ShapeDtypeStruct((all_rows, width), bf16),
-        [VMEM, pl.BlockSpec(memory_space=pltpu.HBM)],
+        [ANY, ANY],
         flops=4 * all_rows * width * units,
         moved=10 * 1024 * 1024,
         scratch=[
+            pltpu.VMEM((all_rows, width), bf16),
+            pltpu.VMEM((all_rows, sections * LANE), bf16),
             pltpu.VMEM((sections, 2 * units, LANE), bf16),
-            pltpu.SemaphoreType.DMA((2, chunks)),
+            pltpu.SemaphoreType.DMA(()),
+            pltpu.SemaphoreType.DMA(()),
+            pltpu.SemaphoreType.DMA(()),
         ],
+        limit=60,
     )(normed, weights)
     terms = lax.all_to_all(partial_sum, "tensor", 0, 0, tiled=True)
     return call(

time: 147 us -> 143 us (0.973)
  local copies, waits for them, and re-layouts: 6.22 us -> 1.58 us
    unnamed x14 -> x8, local copies, waits for them, and re-layouts: 6.2 us -> 1.55 us
where the time goes in v5:
time: 143 us; the launch traced here: 142 us
  blocking collectives  61.6 us (43%)
  waiting for transfers between devices  42.2 us (30%)
  between operations  13.5 us (9%)
  Pallas kernels  11.5 us (8%)
  starting transfers between devices  11.3 us (8%)
  local copies, waits for them, and re-layouts  1.58 us (1%)
    all_to_all x1, blocking collectives, local(): tiles = lax.all_to_all(tiles, 'section', 0, 0, tiled=True)  32.5 us
    all_to_all x1, blocking collectives, local(): lax.all_to_all(copies.reshape(all_rows, width), 'tensor', 0, 0, tiled=True)  29 us
    all_to_all x1, waiting for transfers between devices, local(): terms = lax.all_to_all(partial_sum, 'tensor', 0, 0, tiled=True)  22.7 us
    all_to_all x1, waiting for transfers between devices, local(): tiles = lax.all_to_all(tiles, 'section', 0, 0, tiled=True)  18.3 us
    all_to_all x1, starting transfers between devices, local(): terms = lax.all_to_all(partial_sum, 'tensor', 0, 0, tiled=True)  7.43 us
    pallas_call x1, Pallas kernels, local(): call(functools.partial(mlp_body, part), jax.ShapeDtypeStruct((all_rows, w...  7.39 us
    all_to_all x1, starting transfers between devices, local(): tiles = lax.all_to_all(tiles, 'section', 0, 0, tiled=True)  3.84 us
  transfers between devices with their start and end apart: 3, of which 3 were waited for; matrix products, arithmetic and copies ran while one was open for 0% of the time, Pallas kernels for 1%

profile of v5, /device:TPU:6, one launch (start us, length us, event | category | flops | bytes accessed | tf_op | source)
XLA Modules:
  0.0 141.5 jit_solution(12922018543491154809)
XLA Ops:
  6.5 0.0 copy-start.2
  6.5 0.0 all-gather.3.cloned.1.call-start
  6.5 1.7 %shard_map.67 = bf16[800,128]{1,0:T(8,128)(2,1)} custom-call(bf16[400,100]{1,0:T(8,128)(2,1)} %bitcast.11, bf16[400,100]{1,0:T(8,128)(2,1)} %out_ref.1), custom_call_target="tpu_custom_call" | custom-call | tf_op jit(solution)/shard_map/pallas_call | solution.py:118
  8.2 0.0 all-gather.3.cloned.1.call-update
  8.3 0.0 copy-start
  8.3 0.9 copy-done
  9.2 32.5 %all_to_all.30.x_ref = bf16[64,8,128]{2,1,0:T(8,128)(2,1)S(1)} all-to-all(bf16[64,8,128]{2,1,0:T(8,128)(2,1)S(1)} %shard_map.64), channel_id=1, replica_groups=mesh['section'=32,'tensor'=16] {'section'}, dimensions={0} | all-to-all | bytes 262144 | tf_op jit(solution)/shard_map/all_to_all | solution.py:125
  41.7 0.0 copy-start.1
  41.7 0.7 copy-done.1
  42.4 1.2 shard_map.65
  43.6 3.8 %all-to-all-start.1 = ((bf16[64,8,128]{2,1,0:T(8,128)(2,1)}), bf16[64,8,128]{2,1,0:T(8,128)(2,1)S(1)}, u32[]{:S(2)}, u32[]{:S(2)}) async-start(bf16[64,8,128]{2,1,0:T(8,128)(2,1)} %shard_map.65), calls=%async_computation.1 | async-start | bytes 262144 | tf_op jit(solution)/shard_map/all_to_all | solution.py:127
  47.5 0.0 copy-done.2
  47.5 18.3 %all-to-all-done.1.x_ref = bf16[64,8,128]{2,1,0:T(8,128)(2,1)S(1)} async-done(((bf16[64,8,128]{2,1,0:T(8,128)(2,1)}), bf16[64,8,128]{2,1,0:T(8,128)(2,1)S(1)}, u32[]{:S(2)}, u32[]{:S(2)}) %all-to-all-start.1) | async-done | bytes 131104 | tf_op jit(solution)/shard_map/all_to_all | solution.py:127
  65.8 0.2 shard_map.66
  66.0 29.0 %all_to_all.31 = bf16[16,16,3200]{2,1,0:T(8,128)(2,1)} all-to-all(bf16[16,16,3200]{2,1,0:T(8,128)(2,1)S(1)} %bitcast.7), channel_id=1, replica_groups=mesh['section'=32,'tensor'=16] {'tensor'}, dimensions={0} | all-to-all | bytes 3276800 | tf_op jit(solution)/shard_map/all_to_all | solution.py:139
  95.0 1.2 all-gather.3.cloned.1.call-done
  96.2 7.4 %shard_map.68 = bf16[256,3200]{1,0:T(8,128)(2,1)} custom-call(bf16[256,3200]{1,0:T(8,128)(2,1)} %bitcast.9, bf16[32,800,128]{2,1,0:T(8,128)(2,1)} %bitcast.10), custom_call_target="tpu_custom_call" | custom-call | flops 1310720000 | bytes 10485760 | tf_op jit(solution)/shard_map/pallas_call | solution.py:140
  103.6 0.0 copy-start.3
  103.7 7.4 %all-to-all-start.3 = ((bf16[16,16,3200]{2,1,0:T(8,128)(2,1)}), bf16[16,16,3200]{2,1,0:T(8,128)(2,1)S(1)}, u32[]{:S(2)}, u32[]{:S(2)}) async-start(bf16[16,16,3200]{2,1,0:T(8,128)(2,1)} %bitcast.8), calls=%async_computation.3 | async-start | bytes 3276800 | tf_op jit(solution)/shard_map/all_to_all | solution.py:156
  111.1 0.0 copy-done.3
  111.1 22.7 %all-to-all-done.3 = bf16[16,16,3200]{2,1,0:T(8,128)(2,1)S(1)} async-done(((bf16[16,16,3200]{2,1,0:T(8,128)(2,1)}), bf16[16,16,3200]{2,1,0:T(8,128)(2,1)S(1)}, u32[]{:S(2)}, u32[]{:S(2)}) %all-to-all-start.3) | async-done | bytes 1638432 | tf_op jit(solution)/shard_map/all_to_all | solution.py:156
  133.8 0.9 shard_map.69
  (3 shorter events, 0.0 us)
Async XLA Ops:
  6.5 40.9 %copy-start.2 = (f32[3200]{0:T(1024)S(1)}, f32[3200]{0:T(1024)}, u32[]{:S(2)}) copy-start(f32[3200]{0:T(1024)} %param.8) | copy-start | bytes 38404
  6.5 89.7 %all-gather.3.cloned.1.call-start = ((), (), s32[]{:S(2)}) async-start(), calls=%async_computation.4 | async-start | bytes 6758400 | tf_op jit(solution)/shard_map/all_gather | solution.py:121
  8.3 0.9 copy-start
  41.7 0.7 copy-start.1
  43.6 22.2 %all-to-all-start.1 = ((bf16[64,8,128]{2,1,0:T(8,128)(2,1)}), bf16[64,8,128]{2,1,0:T(8,128)(2,1)S(1)}, u32[]{:S(2)}, u32[]{:S(2)}) async-start(bf16[64,8,128]{2,1,0:T(8,128)(2,1)} %shard_map.65), calls=%async_computation.1 | async-start | bytes 262144 | tf_op jit(solution)/shard_map/all_to_all | solution.py:127
  103.6 7.4 %copy-start.3 = (f32[3200]{0:T(1024)S(1)}, f32[3200]{0:T(1024)}, u32[]{:S(2)}) copy-start(f32[3200]{0:T(1024)} %param.11) | copy-start | bytes 38404
  103.7 30.1 %all-to-all-start.3 = ((bf16[16,16,3200]{2,1,0:T(8,128)(2,1)}), bf16[16,16,3200]{2,1,0:T(8,128)(2,1)S(1)}, u32[]{:S(2)}, u32[]{:S(2)}) async-start(bf16[16,16,3200]{2,1,0:T(8,128)(2,1)} %bitcast.8), calls=%async_computation.3 | async-start | bytes 3276800 | tf_op jit(solution)/shard_map/all_to_all | solution.py:156
Sparse Core Ops, SparseCore 0:
  9.5 86.7 all-gather.2

commit v6 on v5

--- a/solution.py
+++ b/solution.py
@@ -25,15 +25,18 @@
     )
 
 
-def split_body(x_ref, o_ref):
+def first_body(x_ref, in_ref, out_ref, weights_ref, tiles_ref):
+    units, part = in_ref.shape
+    weights_ref[:units, :part] = in_ref[...]
+    weights_ref[units:, :part] = out_ref[...]
+    weights_ref[:, part:] = jnp.zeros((2 * units, LANE - part), weights_ref.dtype)
     blocks, rows, width = x_ref.shape
-    for m in range(o_ref.shape[0] // blocks):
-        if (m + 1) * LANE <= width:
-            for b in range(blocks):
-                o_ref[m * blocks + b] = x_ref[b, :, m * LANE : (m + 1) * LANE]
-        else:
-            for b in range(blocks):
-                o_ref[m * blocks + b] = jnp.zeros((rows, LANE), o_ref.dtype)
+    for m in range(tiles_ref.shape[0] // blocks):
+        for b in range(blocks):
+            if (m + 1) * LANE <= width:
+                tiles_ref[m * blocks + b] = x_ref[b, :, m * LANE : (m + 1) * LANE]
+            else:
+                tiles_ref[m * blocks + b] = jnp.zeros((rows, LANE), tiles_ref.dtype)
 
 
 def order_body(plan_ref, x_ref, o_ref):
@@ -49,17 +52,10 @@
         rows_ref[b] = whole
         values = whole.astype(jnp.float32)
         mean_square = jnp.sum(values * values, axis=-1, keepdims=True) * (1.0 / width)
-        normed = values * lax.rsqrt(mean_square + 1e-06) * gain_ref[...]
+        normed = values * lax.rsqrt(mean_square + 1e-06) * gain_ref[...].reshape(1, width)
         normed = normed.astype(jnp.bfloat16)
         for t in range(copies_ref.shape[0]):
             copies_ref[t, b] = normed
-
-
-def pack_body(in_ref, out_ref, o_ref):
-    units, part = in_ref.shape
-    o_ref[:units, :part] = in_ref[...]
-    o_ref[units:, :part] = out_ref[...]
-    o_ref[:, part:] = jnp.zeros((2 * units, LANE - part), o_ref.dtype)
 
 
 def mlp_body(part, x_hbm, w_hbm, o_ref, x_ref, spread, held, x_sem, in_sem, out_sem):
@@ -108,22 +104,24 @@
         for t in range(1, x_ref.shape[0]):
             branch += x_ref[t, b].astype(jnp.float32)
         values = rows_ref[b].astype(jnp.float32)
-        o_ref[b] = (values + scale_ref[...] * branch).astype(o_ref.dtype)
+        o_ref[b] = (values + scale_ref[...].reshape(1, -1) * branch).astype(o_ref.dtype)
 
 
 def local(sections, groups, patches, plan, norm_gain, proj_in, proj_out, layer_scale):
     blocks, rows, width = patches.shape
     bf16 = jnp.bfloat16
     part, units = proj_in.shape
-    weights = call(
-        pack_body, jax.ShapeDtypeStruct((2 * units, LANE), bf16), [VMEM, VMEM], limit=60
-    )(proj_in.T, proj_out)
+    shape = jax.ShapeDtypeStruct((sections * blocks, rows, LANE), bf16)
+    weights, tiles = call(
+        first_body,
+        (jax.ShapeDtypeStruct((2 * units, LANE), bf16), shape),
+        [VMEM, VMEM, VMEM],
+        n_out=2,
+        limit=60,
+    )(patches, proj_in.T, proj_out)
     weights = lax.all_gather(weights, "section", axis=0, tiled=False)
-
-    shape = jax.ShapeDtypeStruct((sections * blocks, rows, LANE), bf16)
-    tiles = call(split_body, shape, [VMEM])(patches)
     tiles = lax.all_to_all(tiles, "section", 0, 0, tiled=True)
-    tiles = call(order_body, shape, [SMEM, VMEM])(plan, tiles)
+    tiles = call(order_body, shape, [SMEM, VMEM], limit=60)(plan, tiles)
     tiles = lax.all_to_all(tiles, "section", 0, 0, tiled=True)
     own, copies = call(
         norm_body,
@@ -133,7 +131,8 @@
         ),
         [VMEM, VMEM],
         n_out=2,
-    )(tiles, norm_gain.reshape(1, width))
+        limit=60,
+    )(tiles, norm_gain)
 
     all_rows = groups * blocks * rows
     normed = lax.all_to_all(copies.reshape(all_rows, width), "tensor", 0, 0, tiled=True)
@@ -155,8 +154,11 @@
     )(normed, weights)
     terms = lax.all_to_all(partial_sum, "tensor", 0, 0, tiled=True)
     return call(
-        sum_body, jax.ShapeDtypeStruct((blocks, rows, width), bf16), [VMEM, VMEM, VMEM]
-    )(terms.reshape(groups, blocks, rows, width), own, layer_scale.reshape(1, width))
+        sum_body,
+        jax.ShapeDtypeStruct((blocks, rows, width), bf16),
+        [VMEM, VMEM, VMEM],
+        limit=60,
+    )(terms.reshape(groups, blocks, rows, width), own, layer_scale)
 
 
 def solution(mesh):

time: 143 us -> 144 us (level)
  blocking collectives: 61.6 us -> 113 us
  waiting for transfers between devices: 42.2 us -> 0.02 us
  starting transfers between devices: 11.3 us -> 0.01 us
  Pallas kernels: 11.5 us -> 15.6 us
  local copies, waits for them, and re-layouts: 1.58 us -> 0 us
    all_to_all x2 -> x0, waiting for transfers between devices: 41 us -> none  [the longest x1 22.7 us: local(): terms = lax.all_to_all(partial_sum, 'tensor', 0, 0, tiled=True)]
    all_to_all x0 -> x1, blocking collectives: none -> 28.7 us  [local(): terms = lax.all_to_all(partial_sum, 'tensor', 0, 0, tiled=True)]
    all_to_all x1 -> x2, blocking collectives: 32.5 us -> 55.8 us  [local(): tiles = lax.all_to_all(tiles, 'section', 0, 0, tiled=True)]
    all_to_all x2 -> x0, starting transfers between devices: 11.3 us -> none  [the longest x1 7.43 us: local(): terms = lax.all_to_all(partial_sum, 'tensor', 0, 0, tiled=True)]
    pallas_call x1, Pallas kernels: 0.22 us -> 2.41 us  [local(): call(norm_body, (jax.ShapeDtypeStruct((blocks, rows, width), bf16), jax.S...]
    unnamed x8 -> x0, local copies, waits for them, and re-layouts: 1.55 us -> none
    pallas_call x1, Pallas kernels: 0.88 us -> 2.37 us  [local(): call(sum_body, jax.ShapeDtypeStruct((blocks, rows, width), bf16), [VMEM,...]
    pallas_call x3 -> x2, Pallas kernels: 2.96 us -> 3.44 us  [the longest x1 1.82 us: local(): call(first_body, (jax.ShapeDtypeStruct((2 * units, LANE), bf16), shape),...]
  transfers between devices with their start and end apart: 3 -> 1, of which waited for: 3 -> 0; matrix products, arithmetic and copies ran while one was open for 0% -> 0% of each run, Pallas kernels for 1% -> 3%
where the time goes in v6:
time: 144 us; the launch traced here: 142 us
  blocking collectives  113 us (78%)
  Pallas kernels  15.6 us (11%)
  between operations  13.4 us (9%)
    all_to_all x2, blocking collectives, local(): tiles = lax.all_to_all(tiles, 'section', 0, 0, tiled=True)  55.8 us
    all_to_all x1, blocking collectives, local(): lax.all_to_all(copies.reshape(all_rows, width), 'tensor', 0, 0, tiled=True)  28.8 us
    all_to_all x1, blocking collectives, local(): terms = lax.all_to_all(partial_sum, 'tensor', 0, 0, tiled=True)  28.7 us
    pallas_call x1, Pallas kernels, local(): call(functools.partial(mlp_body, part), jax.ShapeDtypeStruct((all_rows, w...  7.39 us
  transfers between devices with their start and end apart: 1, of which 0 were waited for; matrix products, arithmetic and copies ran while one was open for 0% of the time, Pallas kernels for 3%

profile of v6, /device:TPU:6, one launch (start us, length us, event | category | flops | bytes accessed | tf_op | source)
XLA Modules:
  0.0 142.2 jit_solution(7303509141362467350)
XLA Ops:
  6.5 0.0 all-gather.3.cloned.1.call-start
  6.5 1.8 %shard_map.64 = (bf16[800,128]{1,0:T(8,128)(2,1)}, bf16[64,8,128]{2,1,0:T(8,128)(2,1)}) custom-call(bf16[2,8,3200]{2,1,0:T(8,128)(2,1)} %x_ref.1, bf16[400,100]{1,0:T(8,128)(2,1)} %bitcast.11, bf16[400,100]{1,0:T(8,128)(2,1)} %out_ref.1), custom_call_target="tpu_custom_call" | custom-call | tf_op jit(solution)/shard_map/pallas_call | solution.py:115
  8.4 0.0 all-gather.3.cloned.1.call-update
  8.4 32.9 %all_to_all.30.x_ref = bf16[64,8,128]{2,1,0:T(8,128)(2,1)} all-to-all(bf16[64,8,128]{2,1,0:T(8,128)(2,1)} %get-tuple-element.9), channel_id=1, replica_groups=mesh['section'=32,'tensor'=16] {'section'}, dimensions={0} | all-to-all | bytes 262144 | tf_op jit(solution)/shard_map/all_to_all | solution.py:123
  41.3 1.6 %shard_map.65 = bf16[64,8,128]{2,1,0:T(8,128)(2,1)} custom-call(s32[64]{0:T(128)} %plan_ref.1, bf16[64,8,128]{2,1,0:T(8,128)(2,1)} %all_to_all.30.x_ref), custom_call_target="tpu_custom_call" | custom-call | tf_op jit(solution)/shard_map/pallas_call | solution.py:124
  42.9 22.8 %all_to_all.31.x_ref = bf16[64,8,128]{2,1,0:T(8,128)(2,1)} all-to-all(bf16[64,8,128]{2,1,0:T(8,128)(2,1)} %shard_map.65), channel_id=1, replica_groups=mesh['section'=32,'tensor'=16] {'section'}, dimensions={0} | all-to-all | bytes 262144 | tf_op jit(solution)/shard_map/all_to_all | solution.py:125
  65.8 2.4 %shard_map.66 = (bf16[2,8,3200]{2,1,0:T(8,128)(2,1)}, bf16[16,2,8,3200]{3,2,1,0:T(8,128)(2,1)}) custom-call(bf16[64,8,128]{2,1,0:T(8,128)(2,1)} %all_to_all.31.x_ref, f32[3200]{0:T(1024)} %gain_ref.1), custom_call_target="tpu_custom_call" | custom-call | tf_op jit(solution)/shard_map/pallas_call | solution.py:126
  68.2 28.8 %all_to_all.32 = bf16[16,16,3200]{2,1,0:T(8,128)(2,1)} all-to-all(bf16[16,16,3200]{2,1,0:T(8,128)(2,1)} %bitcast.10), channel_id=1, replica_groups=mesh['section'=32,'tensor'=16] {'tensor'}, dimensions={0} | all-to-all | bytes 3276800 | tf_op jit(solution)/shard_map/all_to_all | solution.py:138
  96.9 0.0 all-gather.3.cloned.1.call-done
  96.9 7.4 %shard_map.67 = bf16[256,3200]{1,0:T(8,128)(2,1)} custom-call(bf16[256,3200]{1,0:T(8,128)(2,1)} %bitcast.6, bf16[32,800,128]{2,1,0:T(8,128)(2,1)} %bitcast.8), custom_call_target="tpu_custom_call" | custom-call | flops 1310720000 | bytes 10485760 | tf_op jit(solution)/shard_map/pallas_call | solution.py:139
  104.3 28.7 %all_to_all.33 = bf16[16,16,3200]{2,1,0:T(8,128)(2,1)} all-to-all(bf16[16,16,3200]{2,1,0:T(8,128)(2,1)} %bitcast.7), channel_id=1, replica_groups=mesh['section'=32,'tensor'=16] {'tensor'}, dimensions={0} | all-to-all | bytes 3276800 | tf_op jit(solution)/shard_map/all_to_all | solution.py:155
  133.0 2.4 %shard_map.68 = bf16[2,8,3200]{2,1,0:T(8,128)(2,1)} custom-call(bf16[16,2,8,3200]{3,2,1,0:T(8,128)(2,1)} %bitcast.9, bf16[2,8,3200]{2,1,0:T(8,128)(2,1)} %get-tuple-element.12.rows_ref, f32[3200]{0:T(1024)} %scale_ref.1), custom_call_target="tpu_custom_call" | custom-call | tf_op jit(solution)/shard_map/pallas_call | solution.py:156
Async XLA Ops:
  6.5 90.4 %all-gather.3.cloned.1.call-start = ((), (), s32[]{:S(2)}) async-start(), calls=%async_computation.4 | async-start | bytes 6758400 | tf_op jit(solution)/shard_map/all_gather | solution.py:122
Sparse Core Ops, SparseCore 0:
  9.5 86.5 all-gather.2

commit v7 on v6

--- a/solution.py
+++ b/solution.py
@@ -58,7 +58,7 @@
             copies_ref[t, b] = normed
 
 
-def mlp_body(part, x_hbm, w_hbm, o_ref, x_ref, spread, held, x_sem, in_sem, out_sem):
+def mlp_body(part, x_hbm, w_hbm, scale_ref, o_ref, x_ref, spread, held, x_sem, in_sem, out_sem):
     sections, both, _ = held.shape
     units = both // 2
     rows = x_ref.shape[0]
@@ -86,25 +86,30 @@
         )
     hidden = 0.5 * total * (1.0 + lax.erf(total * (0.5**0.5)))
     hidden = hidden.astype(jnp.bfloat16)
+    scale = scale_ref[...].reshape(1, sections * part)
+    edge = jnp.zeros((1, LANE - part), scale.dtype)
     out_copy.wait()
     for s in range(0, sections, 2):
         product = jnp.dot(
             hidden,
             jnp.concatenate([held[s, units:, :], held[s + 1, units:, :]], axis=1),
             preferred_element_type=jnp.float32,
-        ).astype(jnp.bfloat16)
+        )
+        columns = [scale[:, (s + i) * part : (s + i + 1) * part] for i in range(2)]
+        product = product * jnp.concatenate([columns[0], edge, columns[1], edge], axis=1)
+        product = product.astype(jnp.bfloat16)
         for i in range(2):
             o_ref[:, (s + i) * part : (s + i + 1) * part] = product[:, i * LANE : i * LANE + part]
 
 
-def sum_body(x_ref, rows_ref, scale_ref, o_ref):
+def sum_body(x_ref, rows_ref, o_ref):
     blocks = rows_ref.shape[0]
     for b in range(blocks):
         branch = x_ref[0, b].astype(jnp.float32)
         for t in range(1, x_ref.shape[0]):
             branch += x_ref[t, b].astype(jnp.float32)
         values = rows_ref[b].astype(jnp.float32)
-        o_ref[b] = (values + scale_ref[...].reshape(1, -1) * branch).astype(o_ref.dtype)
+        o_ref[b] = (values + branch).astype(o_ref.dtype)
 
 
 def local(sections, groups, patches, plan, norm_gain, proj_in, proj_out, layer_scale):
@@ -131,7 +136,6 @@
         ),
         [VMEM, VMEM],
         n_out=2,
-        limit=60,
     )(tiles, norm_gain)
 
     all_rows = groups * blocks * rows
@@ -139,7 +143,7 @@
     partial_sum = call(
         functools.partial(mlp_body, part),
         jax.ShapeDtypeStruct((all_rows, width), bf16),
-        [ANY, ANY],
+        [ANY, ANY, VMEM],
         flops=4 * all_rows * width * units,
         moved=10 * 1024 * 1024,
         scratch=[
@@ -151,14 +155,13 @@
             pltpu.SemaphoreType.DMA(()),
         ],
         limit=60,
-    )(normed, weights)
+    )(normed, weights, layer_scale)
     terms = lax.all_to_all(partial_sum, "tensor", 0, 0, tiled=True)
     return call(
         sum_body,
         jax.ShapeDtypeStruct((blocks, rows, width), bf16),
-        [VMEM, VMEM, VMEM],
-        limit=60,
-    )(terms.reshape(groups, blocks, rows, width), own, layer_scale)
+        [VMEM, VMEM],
+    )(terms.reshape(groups, blocks, rows, width), own)
 
 
 def solution(mesh):

time: 144 us -> 143 us (level)
  Pallas kernels: 15.6 us -> 12.7 us
  waiting for transfers between devices: 0.02 us -> 1.96 us
    pallas_call x1, Pallas kernels: 2.41 us -> 0.22 us  [local(): call(norm_body, (jax.ShapeDtypeStruct((blocks, rows, width), bf16), jax.S...]
    all_gather x1, waiting for transfers between devices: 0.01 us -> 1.95 us  [local(): weights = lax.all_gather(weights, 'section', axis=0, tiled=False)]
    pallas_call x1, Pallas kernels: 2.37 us -> 0.87 us  [local(): call(sum_body, jax.ShapeDtypeStruct((blocks, rows, width), bf16), [VMEM,...]
  transfers between devices with their start and end apart: 1 -> 1, of which waited for: 0 -> 1; matrix products, arithmetic and copies ran while one was open for 0% -> 0% of each run, Pallas kernels for 3% -> 1%
where the time goes in v7:
time: 143 us; the launch traced here: 141 us
  blocking collectives  112 us (78%)
  between operations  13.4 us (9%)
  Pallas kernels  12.7 us (9%)
  waiting for transfers between devices  1.96 us (1%)
    all_to_all x2, blocking collectives, local(): tiles = lax.all_to_all(tiles, 'section', 0, 0, tiled=True)  55 us
    all_to_all x1, blocking collectives, local(): terms = lax.all_to_all(partial_sum, 'tensor', 0, 0, tiled=True)  28.9 us
    all_to_all x1, blocking collectives, local(): lax.all_to_all(copies.reshape(all_rows, width), 'tensor', 0, 0, tiled=True)  28.4 us
    pallas_call x1, Pallas kernels, local(): call(functools.partial(mlp_body, part), jax.ShapeDtypeStruct((all_rows, w...  8.09 us
  transfers between devices with their start and end apart: 1, of which 1 were waited for; matrix products, arithmetic and copies ran while one was open for 0% of the time, Pallas kernels for 1%

profile of v7, /device:TPU:6, one launch (start us, length us, event | category | flops | bytes accessed | tf_op | source)
XLA Modules:
  0.0 141.1 jit_solution(3325491768402966174)
XLA Ops:
  6.5 0.0 all-gather.3.cloned.1.call-start
  6.5 1.8 %shard_map.64 = (bf16[800,128]{1,0:T(8,128)(2,1)}, bf16[64,8,128]{2,1,0:T(8,128)(2,1)}) custom-call(bf16[2,8,3200]{2,1,0:T(8,128)(2,1)} %x_ref.1, bf16[400,100]{1,0:T(8,128)(2,1)} %bitcast.11, bf16[400,100]{1,0:T(8,128)(2,1)} %out_ref.1), custom_call_target="tpu_custom_call" | custom-call | tf_op jit(solution)/shard_map/pallas_call | solution.py:120
  8.4 0.0 all-gather.3.cloned.1.call-update
  8.4 32.9 %all_to_all.30.x_ref = bf16[64,8,128]{2,1,0:T(8,128)(2,1)} all-to-all(bf16[64,8,128]{2,1,0:T(8,128)(2,1)} %get-tuple-element.9), channel_id=1, replica_groups=mesh['section'=32,'tensor'=16] {'section'}, dimensions={0} | all-to-all | bytes 262144 | tf_op jit(solution)/shard_map/all_to_all | solution.py:128
  41.3 1.6 %shard_map.65 = bf16[64,8,128]{2,1,0:T(8,128)(2,1)} custom-call(s32[64]{0:T(128)} %plan_ref.1, bf16[64,8,128]{2,1,0:T(8,128)(2,1)} %all_to_all.30.x_ref), custom_call_target="tpu_custom_call" | custom-call | tf_op jit(solution)/shard_map/pallas_call | solution.py:129
  43.0 22.1 %all_to_all.31.x_ref = bf16[64,8,128]{2,1,0:T(8,128)(2,1)S(1)} all-to-all(bf16[64,8,128]{2,1,0:T(8,128)(2,1)} %shard_map.65), channel_id=1, replica_groups=mesh['section'=32,'tensor'=16] {'section'}, dimensions={0} | all-to-all | bytes 262144 | tf_op jit(solution)/shard_map/all_to_all | solution.py:130
  65.0 0.0 copy-start
  65.0 0.7 copy-done
  65.8 0.2 shard_map.66
  66.0 28.4 %all_to_all.32 = bf16[16,16,3200]{2,1,0:T(8,128)(2,1)} all-to-all(bf16[16,16,3200]{2,1,0:T(8,128)(2,1)S(1)} %bitcast.7), channel_id=1, replica_groups=mesh['section'=32,'tensor'=16] {'tensor'}, dimensions={0} | all-to-all | bytes 3276800 | tf_op jit(solution)/shard_map/all_to_all | solution.py:142
  94.4 1.9 %all-gather.3.cloned.1.call-done = bf16[25600,128]{1,0:T(8,128)(2,1)} async-done(((bf16[800,128]{1,0:T(8,128)(2,1)}), bf16[25600,128]{1,0:T(8,128)(2,1)}) %all-gather.3.cloned.1.call-update) | async-done | bytes 6553616 | tf_op jit(solution)/shard_map/all_gather | solution.py:127
  96.3 8.1 %shard_map.67 = bf16[256,3200]{1,0:T(8,128)(2,1)} custom-call(bf16[256,3200]{1,0:T(8,128)(2,1)} %bitcast.8, bf16[32,800,128]{2,1,0:T(8,128)(2,1)} %bitcast.10, f32[3200]{0:T(1024)} %scale_ref.1), custom_call_target="tpu_custom_call" | custom-call | flops 1310720000 | bytes 10485760 | tf_op jit(solution)/shard_map/pallas_call | solution.py:143
  104.4 28.9 %all_to_all.33 = bf16[16,16,3200]{2,1,0:T(8,128)(2,1)S(1)} all-to-all(bf16[16,16,3200]{2,1,0:T(8,128)(2,1)} %bitcast.9), channel_id=1, replica_groups=mesh['section'=32,'tensor'=16] {'tensor'}, dimensions={0} | all-to-all | bytes 3276800 | tf_op jit(solution)/shard_map/all_to_all | solution.py:159
  133.3 0.9 shard_map.68
Async XLA Ops:
  6.5 89.8 %all-gather.3.cloned.1.call-start = ((), (), s32[]{:S(2)}) async-start(), calls=%async_computation.4 | async-start | bytes 6758400 | tf_op jit(solution)/shard_map/all_gather | solution.py:127
  65.0 0.7 copy-start
Sparse Core Ops, SparseCore 0:
  9.5 86.8 all-gather.2

commit v8 on v7

v8 whole, which is shorter than its diff:
```python
import functools

import jax
import jax.numpy as jnp
from jax import lax
from jax.experimental import pallas as pl
from jax.experimental.pallas import tpu as pltpu
from jax.sharding import PartitionSpec as P

LANE = 128
VMEM = pl.BlockSpec(memory_space=pltpu.VMEM)
ANY = pl.BlockSpec(memory_space=pl.ANY)
SMEM = pl.BlockSpec(memory_space=pltpu.SMEM)


def call(body, out_shape, in_specs, flops=0, moved=0, n_out=1, scratch=(), limit=32):
    return pl.pallas_call(
        body,
        out_shape=out_shape,
        in_specs=in_specs,
        out_specs=VMEM if n_out == 1 else [VMEM] * n_out,
        scratch_shapes=list(scratch),
        compiler_params=pltpu.CompilerParams(vmem_limit_bytes=limit * 1024 * 1024),
        cost_estimate=pl.CostEstimate(flops=flops, bytes_accessed=moved, transcendentals=0),
    )


def first_body(x_ref, in_ref, out_ref, weights_ref, tiles_ref):
    part = in_ref.shape[1]
    kept = weights_ref.shape[0] // 2
    fold, chunk = kept // 4, part // 4
    for k, ref in enumerate((in_ref, out_ref)):
        at = k * kept
        weights_ref[at : at + kept, :part] = ref[:kept, :]
        for j in range(4):
            weights_ref[at + j * fold : at + (j + 1) * fold, part : part + chunk] = ref[
                kept:, j * chunk : (j + 1) * chunk
            ]
        edge = LANE - part - chunk
        weights_ref[at : at + kept, part + chunk :] = jnp.zeros((kept, edge), weights_ref.dtype)
    blocks, rows, width = x_ref.shape
    for m in range(tiles_ref.shape[0] // blocks):
        for b in range(blocks):
            if (m + 1) * LANE <= width:
                tiles_ref[m * blocks + b] = x_ref[b, :, m * LANE : (m + 1) * LANE]
            else:
                tiles_ref[m * blocks + b] = jnp.zeros((rows, LANE), tiles_ref.dtype)


def order_body(plan_ref, x_ref, _, o_ref):
    for p in range(o_ref.shape[0]):
        o_ref[p] = x_ref[plan_ref[p]]


def norm_body(x_ref, gain_ref, _, rows_ref, copies_ref):
    blocks, rows, width = rows_ref.shape
    tiles = width // LANE
    for b in range(blocks):
        whole = jnp.concatenate([x_ref[m * blocks + b] for m in range(tiles)], axis=-1)
        rows_ref[b] = whole
        values = whole.astype(jnp.float32)
        mean_square = jnp.sum(values * values, axis=-1, keepdims=True) * (1.0 / width)
        normed = values * lax.rsqrt(mean_square + 1e-06) * gain_ref[...].reshape(1, width)
        normed = normed.astype(jnp.bfloat16)
        for t in range(copies_ref.shape[0]):
            copies_ref[t, b] = normed


def pair_body(mine_ref, other_ref, o_ref):
    core = lax.rem(lax.axis_index("section"), 2)
    o_ref[core] = mine_ref[...]
    o_ref[1 - core] = other_ref[...]


def opened(ref, index, at, kept, part):
    fold, chunk = kept // 4, part // 4
    rest = [ref[index, at + j * fold : at + (j + 1) * fold, part : part + chunk] for j in range(4)]
    rest.append(jnp.zeros((fold, LANE - part), ref.dtype))
    return jnp.concatenate([ref[index, at : at + kept, :], jnp.concatenate(rest, axis=1)], axis=0)


def mlp_body(part, units, plan, x_ref, scale_ref, *refs):
    shard_refs = refs[:-4]
    o_ref, spread, scales, results = refs[-4:]
    chips, rows, _ = spread.shape
    kept = units * 4 // 5
    me = lax.axis_index("section")
    core = lax.rem(me, 2)
    here = lax.div(me, 2)
    blank = jnp.zeros((rows, LANE - part), x_ref.dtype)
    edge = jnp.zeros((1, LANE - part), scale_ref.dtype)
    scale = scale_ref[...].reshape(1, 2 * chips * part)
    for c in range(chips):
        tiles, factors = [], []
        for s in (2 * c, 2 * c + 1):
            tiles += [x_ref[:, s * part : (s + 1) * part], blank]
            factors += [scale[:, s * part : (s + 1) * part], edge]
        spread[c] = jnp.concatenate(tiles, axis=1)
        scales[c] = jnp.concatenate(factors, axis=1)
    places = [
        lax.rem(here + away * (1 - 2 * core) + 2 * chips, chips) for _, _, away in plan
    ]
    total = jnp.zeros((rows, units), jnp.float32)
    for (r, i, _), place in zip(plan, places):
        pair = [opened(shard_refs[r], 2 * i + k, 0, kept, part) for k in range(2)]
        total += lax.dot_general(
            spread[place],
            jnp.concatenate(pair, axis=1),
            (((1,), (1,)), ((), ())),
            preferred_element_type=jnp.float32,
        )
    hidden = 0.5 * total * (1.0 + lax.erf(total * (0.5**0.5)))
    hidden = hidden.astype(jnp.bfloat16)
    for (r, i, _), place in zip(plan, places):
        pair = [opened(shard_refs[r], 2 * i + k, kept, kept, part) for k in range(2)]
        product = jnp.dot(
            hidden, jnp.concatenate(pair, axis=1), preferred_element_type=jnp.float32
        )
        results[place] = (product * scales[place]).astype(jnp.bfloat16)
    for s in range(2 * chips):
        at = (s % 2) * LANE
        o_ref[:, s * part : (s + 1) * part] = results[s // 2, :, at : at + part]


def gather_weights(mine, sections):
    chips = sections // 2
    half = chips // 2
    swap = [(i, i ^ 1) for i in range(sections)]
    step = [(i, (i + (2 if i % 2 == 0 else -2)) % sections) for i in range(sections)]
    other = lax.ppermute(mine, "section", swap)
    now = call(pair_body, jax.ShapeDtypeStruct((2,) + mine.shape, mine.dtype), [VMEM, VMEM])(
        mine, other
    )
    arrays, plan, waiting = [now], [(0, 0, 0)], []
    for k in range(1, half + 1):
        now = lax.ppermute(now, "section", step)
        plan.append((len(arrays), 0, -k))
        arrays.append(now)
        if k < half:
            waiting.append((k, now))
        if k in (half // 2 - 1, half - 2, half - 1):
            group = [w for _, w in waiting]
            group = group[0] if len(group) == 1 else jnp.concatenate(group, axis=0)
            for i, (away, _) in enumerate(waiting):
                plan.append((len(arrays), i, away))
            arrays.append(lax.ppermute(group, "section", swap))
            waiting = []
    return arrays, plan


def sum_body(x_ref, rows_ref, o_ref):
    blocks = rows_ref.shape[0]
    for b in range(blocks):
        branch = x_ref[0, b].astype(jnp.float32)
        for t in range(1, x_ref.shape[0]):
            branch += x_ref[t, b].astype(jnp.float32)
        values = rows_ref[b].astype(jnp.float32)
        o_ref[b] = (values + branch).astype(o_ref.dtype)


def local(sections, groups, patches, plan, norm_gain, proj_in, proj_out, layer_scale):
    blocks, rows, width = patches.shape
    bf16 = jnp.bfloat16
    part, units = proj_in.shape
    shape = jax.ShapeDtypeStruct((sections * blocks, rows, LANE), bf16)
    weights, tiles = call(
        first_body,
        (jax.ShapeDtypeStruct((2 * (units * 4 // 5), LANE), bf16), shape),
        [VMEM, VMEM, VMEM],
        n_out=2,
        limit=60,
    )(patches, proj_in.T, proj_out)
    shards, where = gather_weights(weights, sections)
    steps = [shards[r] for r, i, away in where if away <= 0]
    tiles = lax.all_to_all(tiles, "section", 0, 0, tiled=True)
    tiles = call(order_body, shape, [SMEM, VMEM, ANY], limit=60)(plan, tiles, steps[2])
    tiles = lax.all_to_all(tiles, "section", 0, 0, tiled=True)
    own, copies = call(
        norm_body,
        (
            jax.ShapeDtypeStruct((blocks, rows, width), bf16),
            jax.ShapeDtypeStruct((groups, blocks, rows, width), bf16),
        ),
        [VMEM, VMEM, ANY],
        n_out=2,
    )(tiles, norm_gain, steps[min(5, len(steps) - 1)])

    all_rows = groups * blocks * rows
    normed = lax.all_to_all(copies.reshape(all_rows, width), "tensor", 0, 0, tiled=True)
    partial_sum = call(
        functools.partial(mlp_body, part, units, where),
        jax.ShapeDtypeStruct((all_rows, width), bf16),
        [VMEM] * (2 + len(shards)),
        flops=4 * all_rows * width * units,
        moved=10 * 1024 * 1024,
        scratch=[
            pltpu.VMEM((sections // 2, all_rows, 2 * LANE), bf16),
            pltpu.VMEM((sections // 2, 1, 2 * LANE), jnp.float32),
            pltpu.VMEM((sections // 2, all_rows, 2 * LANE), bf16),
        ],
        limit=60,
    )(normed, layer_scale, *shards)
    terms = lax.all_to_all(partial_sum, "tensor", 0, 0, tiled=True)
    return call(
        sum_body,
        jax.ShapeDtypeStruct((blocks, rows, width), bf16),
        [VMEM, VMEM],
    )(terms.reshape(groups, blocks, rows, width), own)


def solution(mesh):
    return jax.shard_map(
        functools.partial(local, mesh.shape["section"], mesh.shape["tensor"]),
        mesh=mesh,
        in_specs=(
            P("section", "tensor", None),
            P(),
            P(),
            P("section", "tensor"),
            P("tensor", "section"),
            P(),
        ),
        out_specs=P("section", "tensor", None),
        check_vma=False,
    )
```

time: 143 us -> 164 us (1.15)
  blocking collectives: 112 us -> 27.4 us
  waiting for transfers between devices: 1.96 us -> 60.9 us
  starting transfers between devices: 0.01 us -> 56.5 us
  between operations: 13.4 us -> 0.28 us
  local copies, waits for them, and re-layouts: 0.72 us -> 2.87 us
  Pallas kernels: 12.7 us -> 14.5 us
    all_to_all x3 -> x0, blocking collectives: 83.4 us -> none  [the longest x2 55 us: local(): tiles = lax.all_to_all(tiles, 'section', 0, 0, tiled=True)]
    ppermute x0 -> x12, waiting for transfers between devices: none -> 45.5 us  [the longest x8 43.9 us: gather_weights(): now = lax.ppermute(now, 'section', step)]
    ppermute x0 -> x12, starting transfers between devices: none -> 29.7 us  [the longest x8 22 us: gather_weights(): now = lax.ppermute(now, 'section', step)]
    all_to_all x0 -> x3, starting transfers between devices: none -> 26.8 us  [the longest x2 19.2 us: local(): tiles = lax.all_to_all(tiles, 'section', 0, 0, tiled=True)]
    all_to_all x0 -> x3, waiting for transfers between devices: none -> 15.4 us  [the longest x2 15.4 us: local(): tiles = lax.all_to_all(tiles, 'section', 0, 0, tiled=True)]
    unnamed x2 -> x34, local copies, waits for them, and re-layouts: 0.72 us -> 2.87 us
    all_gather x1 -> x0, waiting for transfers between devices: 1.95 us -> none  [local(): weights = lax.all_gather(weights, 'section', axis=0, tiled=False)]
    pallas_call x3 -> x4, Pallas kernels: 11.6 us -> 12.2 us  [the longest x1 8.74 us: local(): call(functools.partial(mlp_body, part, units, where), jax.ShapeDtypeStruc...]
  transfers between devices with their start and end apart: 1 -> 15, of which waited for: 1 -> 8; matrix products, arithmetic and copies ran while one was open for 0% -> 0% of each run, Pallas kernels for 1% -> 1%
where the time goes in v8:
time: 164 us; the launch traced here: 163 us
  waiting for transfers between devices  60.9 us (37%)
  starting transfers between devices  56.5 us (34%)
  blocking collectives  27.4 us (17%)
  Pallas kernels  14.5 us (9%)
  local copies, waits for them, and re-layouts  2.87 us (2%)
    ppermute x8, waiting for transfers between devices, gather_weights(): now = lax.ppermute(now, 'section', step)  43.9 us
    all_to_all x1, blocking collectives, local(): terms = lax.all_to_all(partial_sum, 'tensor', 0, 0, tiled=True)  27.4 us
    ppermute x8, starting transfers between devices, gather_weights(): now = lax.ppermute(now, 'section', step)  22 us
    all_to_all x2, starting transfers between devices, local(): tiles = lax.all_to_all(tiles, 'section', 0, 0, tiled=True)  19.2 us
    all_to_all x2, waiting for transfers between devices, local(): tiles = lax.all_to_all(tiles, 'section', 0, 0, tiled=True)  15.4 us
    pallas_call x1, Pallas kernels, local(): call(functools.partial(mlp_body, part, units, where), jax.ShapeDtypeStruc...  8.74 us
    all_to_all x1, starting transfers between devices, local(): lax.all_to_all(copies.reshape(all_rows, width), 'tensor', 0, 0, tiled=True)  7.56 us
    ppermute x3, starting transfers between devices, gather_weights(): arrays.append(lax.ppermute(group, 'section', swap))  5.75 us
  transfers between devices with their start and end apart: 15, of which 8 were waited for; matrix products, arithmetic and copies ran while one was open for 0% of the time, Pallas kernels for 1%

profile of v8, /device:TPU:6, one launch (start us, length us, event | category | flops | bytes accessed | tf_op | source)
XLA Modules:
  0.0 162.6 jit_solution(2612166912725599146)
XLA Ops:
  0.0 0.0 copy-start.3
  0.0 1.8 %shard_map.64 = (bf16[640,128]{1,0:T(8,128)(2,1)}, bf16[64,8,128]{2,1,0:T(8,128)(2,1)}) custom-call(bf16[2,8,3200]{2,1,0:T(8,128)(2,1)} %x_ref.1, bf16[400,100]{1,0:T(8,128)(2,1)} %bitcast.8, bf16[400,100]{1,0:T(8,128)(2,1)} %out_ref.1), custom_call_target="tpu_custom_call" | custom-call | tf_op jit(solution)/shard_map/pallas_call | solution.py:166
  1.8 1.9 %collective-permute-start = (bf16[640,128]{1,0:T(8,128)(2,1)}, bf16[640,128]{1,0:T(8,128)(2,1)S(1)}, u32[]{:S(2)}, u32[]{:S(2)}) collective-permute-start(bf16[640,128]{1,0:T(8,128)(2,1)} %get-tuple-element.10.mine_ref), channel_id=1, source_target_pairs={{0,16},{16,0},{32,48},{48,32},{64,80},{80,64},{96,112},{112,96},{1... | collective-permute-start | bytes 491528 | tf_op jit(solution)/shard_map/ppermute | solution.py:130
  3.8 1.6 collective-permute-done.other_ref
  5.3 0.0 copy-start.2
  5.3 0.9 copy-done.2
  6.3 0.0 copy-start.1
  6.3 3.8 %collective-permute-start.1 = (bf16[2,640,128]{2,1,0:T(8,128)(2,1)S(1)}, bf16[2,640,128]{2,1,0:T(8,128)(2,1)S(1)}, u32[]{:S(2)}, u32[]{:S(2)}) collective-permute-start(bf16[2,640,128]{2,1,0:T(8,128)(2,1)S(1)} %shard_map.65.refs_0_), channel_id=1, source_target_pairs={{0,32},{16,496},{32,64},{48,16},{64,96},{80,48},{96,128},{112,80},... | collective-permute-start | bytes 983048 | tf_op jit(solution)/shard_map/ppermute | solution.py:136
  10.1 12.6 %collective-permute-done.1.refs_1_ = bf16[2,640,128]{2,1,0:T(8,128)(2,1)S(1)} collective-permute-done((bf16[2,640,128]{2,1,0:T(8,128)(2,1)S(1)}, bf16[2,640,128]{2,1,0:T(8,128)(2,1)S(1)}, u32[]{:S(2)}, u32[]{:S(2)}) %collective-permute-start.1) | collective-permute-done | bytes 327712 | tf_op jit(solution)/shard_map/ppermute | solution.py:136
  22.7 0.0 copy-start.7
  22.7 1.9 %collective-permute-start.2 = (bf16[2,640,128]{2,1,0:T(8,128)(2,1)S(1)}, bf16[2,640,128]{2,1,0:T(8,128)(2,1)S(1)}, u32[]{:S(2)}, u32[]{:S(2)}) collective-permute-start(bf16[2,640,128]{2,1,0:T(8,128)(2,1)S(1)} %collective-permute-done.1.refs_1_), channel_id=1, source_target_pairs={{0,32},{16,496},{32,64},{48,16},{64,96},{80,48},{96,128},{112,80},... | collective-permute-start | bytes 983048 | tf_op jit(solution)/shard_map/ppermute | solution.py:136
  24.7 9.8 %all-to-all-start = ((bf16[64,8,128]{2,1,0:T(8,128)(2,1)}), bf16[64,8,128]{2,1,0:T(8,128)(2,1)S(1)}, u32[]{:S(2)}, u32[]{:S(2)}) async-start(bf16[64,8,128]{2,1,0:T(8,128)(2,1)} %get-tuple-element.9), calls=%async_computation | async-start | bytes 262144 | tf_op jit(solution)/shard_map/all_to_all | solution.py:175
  34.4 0.0 collective-permute-done.2._.refs_2_
  34.4 0.0 copy-start.5
  34.5 3.7 %collective-permute-start.3 = (bf16[2,640,128]{2,1,0:T(8,128)(2,1)S(1)}, bf16[2,640,128]{2,1,0:T(8,128)(2,1)S(1)}, u32[]{:S(2)}, u32[]{:S(2)}) collective-permute-start(bf16[2,640,128]{2,1,0:T(8,128)(2,1)S(1)} %collective-permute-done.2._.refs_2_), channel_id=1, source_target_pairs={{0,32},{16,496},{32,64},{48,16},{64,96},{80,48},{96,128},{112,80},... | collective-permute-start | bytes 983048 | tf_op jit(solution)/shard_map/ppermute | solution.py:136
  38.2 9.4 %collective-permute-done.3.refs_3_ = bf16[2,640,128]{2,1,0:T(8,128)(2,1)S(1)} collective-permute-done((bf16[2,640,128]{2,1,0:T(8,128)(2,1)S(1)}, bf16[2,640,128]{2,1,0:T(8,128)(2,1)S(1)}, u32[]{:S(2)}, u32[]{:S(2)}) %collective-permute-start.3) | collective-permute-done | bytes 327712 | tf_op jit(solution)/shard_map/ppermute | solution.py:136
  47.5 2.3 %collective-permute-start.4 = (bf16[2,640,128]{2,1,0:T(8,128)(2,1)S(1)}, bf16[2,640,128]{2,1,0:T(8,128)(2,1)S(1)}, u32[]{:S(2)}, u32[]{:S(2)}) collective-permute-start(bf16[2,640,128]{2,1,0:T(8,128)(2,1)S(1)} %collective-permute-done.3.refs_3_), channel_id=1, source_target_pairs={{0,32},{16,496},{32,64},{48,16},{64,96},{80,48},{96,128},{112,80},... | collective-permute-start | bytes 983048 | tf_op jit(solution)/shard_map/ppermute | solution.py:136
  49.8 1.9 %all-to-all-done.x_ref = bf16[64,8,128]{2,1,0:T(8,128)(2,1)S(1)} async-done(((bf16[64,8,128]{2,1,0:T(8,128)(2,1)}), bf16[64,8,128]{2,1,0:T(8,128)(2,1)S(1)}, u32[]{:S(2)}, u32[]{:S(2)}) %all-to-all-start) | async-done | bytes 131104 | tf_op jit(solution)/shard_map/all_to_all | solution.py:175
  51.7 0.0 copy-done.5
  51.7 0.7 copy-done.13
  52.3 1.6 shard_map.66
  54.0 9.5 %all-to-all-start.1 = ((bf16[64,8,128]{2,1,0:T(8,128)(2,1)}), bf16[64,8,128]{2,1,0:T(8,128)(2,1)S(1)}, u32[]{:S(2)}, u32[]{:S(2)}) async-start(bf16[64,8,128]{2,1,0:T(8,128)(2,1)} %shard_map.66), calls=%async_computation.1 | async-start | bytes 262144 | tf_op jit(solution)/shard_map/all_to_all | solution.py:177
  63.4 0.0 collective-permute-done.4.refs_5_
  63.4 0.0 copy-start.9
  63.4 3.7 %collective-permute-start.5 = (bf16[2,640,128]{2,1,0:T(8,128)(2,1)S(1)}, bf16[2,640,128]{2,1,0:T(8,128)(2,1)S(1)}, u32[]{:S(2)}, u32[]{:S(2)}) collective-permute-start(bf16[2,640,128]{2,1,0:T(8,128)(2,1)S(1)} %collective-permute-done.4.refs_5_), channel_id=1, source_target_pairs={{0,32},{16,496},{32,64},{48,16},{64,96},{80,48},{96,128},{112,80},... | collective-permute-start | bytes 983048 | tf_op jit(solution)/shard_map/ppermute | solution.py:136
  67.2 13.5 %all-to-all-done.1.x_ref = bf16[64,8,128]{2,1,0:T(8,128)(2,1)S(1)} async-done(((bf16[64,8,128]{2,1,0:T(8,128)(2,1)}), bf16[64,8,128]{2,1,0:T(8,128)(2,1)S(1)}, u32[]{:S(2)}, u32[]{:S(2)}) %all-to-all-start.1) | async-done | bytes 131104 | tf_op jit(solution)/shard_map/all_to_all | solution.py:177
  80.7 0.0 collective-permute-done.5._.refs_6_
  80.7 0.0 copy-done.3
  80.7 1.4 shard_map.67
  82.1 0.0 copy-done.9
  82.1 0.0 copy-done.1
  82.1 7.6 %all-to-all-start.2 = ((bf16[16,16,3200]{2,1,0:T(8,128)(2,1)}), bf16[16,16,3200]{2,1,0:T(8,128)(2,1)S(1)}, u32[]{:S(2)}, u32[]{:S(2)}) async-start(bf16[16,16,3200]{2,1,0:T(8,128)(2,1)} %bitcast.1), calls=%async_computation.2 | async-start | bytes 3276800 | tf_op jit(solution)/shard_map/all_to_all | solution.py:189
  89.7 2.8 %collective-permute-start.7 = (bf16[2,640,128]{2,1,0:T(8,128)(2,1)S(1)}, bf16[2,640,128]{2,1,0:T(8,128)(2,1)S(1)}, u32[]{:S(2)}, u32[]{:S(2)}) collective-permute-start(bf16[2,640,128]{2,1,0:T(8,128)(2,1)S(1)} %collective-permute-done.5._.refs_6_), channel_id=1, source_target_pairs={{0,32},{16,496},{32,64},{48,16},{64,96},{80,48},{96,128},{112,80},... | collective-permute-start | bytes 983048 | tf_op jit(solution)/shard_map/ppermute | solution.py:136
  92.5 0.0 copy-done.8
  92.5 0.0 copy-done.6
  92.5 0.1 pad_maximum_fusion
  92.6 1.9 %collective-permute-start.6 = (bf16[6,640,128]{2,1,0:T(8,128)(2,1)S(1)}, bf16[6,640,128]{2,1,0:T(8,128)(2,1)S(1)}, u32[]{:S(2)}, u32[]{:S(2)}) collective-permute-start(bf16[6,640,128]{2,1,0:T(8,128)(2,1)S(1)} %pad_maximum_fusion), channel_id=1, source_target_pairs={{0,16},{16,0},{32,48},{48,32},{64,80},{80,64},{96,112},{112,96},{1... | collective-permute-start | bytes 2949128 | tf_op jit(solution)/shard_map/ppermute | solution.py:146
  94.6 5.4 %collective-permute-done.7.refs_7_ = bf16[2,640,128]{2,1,0:T(8,128)(2,1)S(1)} collective-permute-done((bf16[2,640,128]{2,1,0:T(8,128)(2,1)S(1)}, bf16[2,640,128]{2,1,0:T(8,128)(2,1)S(1)}, u32[]{:S(2)}, u32[]{:S(2)}) %collective-permute-start.7) | collective-permute-done | bytes 327712 | tf_op jit(solution)/shard_map/ppermute | solution.py:136
  100.0 0.0 copy-done
  100.0 0.0 copy-done.10
  100.0 0.1 pad_maximum_fusion.1
  100.1 1.9 %collective-permute-start.8 = (bf16[6,640,128]{2,1,0:T(8,128)(2,1)S(1)}, bf16[6,640,128]{2,1,0:T(8,128)(2,1)}, u32[]{:S(2)}, u32[]{:S(2)}) collective-permute-start(bf16[6,640,128]{2,1,0:T(8,128)(2,1)S(1)} %pad_maximum_fusion.1), channel_id=1, source_target_pairs={{0,16},{16,0},{32,48},{48,32},{64,80},{80,64},{96,112},{112,96},{1... | collective-permute-start | bytes 2949128 | tf_op jit(solution)/shard_map/ppermute | solution.py:146
  102.0 1.9 %collective-permute-start.9 = (bf16[2,640,128]{2,1,0:T(8,128)(2,1)S(1)}, bf16[2,640,128]{2,1,0:T(8,128)(2,1)S(1)}, u32[]{:S(2)}, u32[]{:S(2)}) collective-permute-start(bf16[2,640,128]{2,1,0:T(8,128)(2,1)S(1)} %collective-permute-done.7.refs_7_), channel_id=1, source_target_pairs={{0,32},{16,496},{32,64},{48,16},{64,96},{80,48},{96,128},{112,80},... | collective-permute-start | bytes 983048 | tf_op jit(solution)/shard_map/ppermute | solution.py:136
  104.0 8.3 %collective-permute-done.9.refs_9_ = bf16[2,640,128]{2,1,0:T(8,128)(2,1)S(1)} collective-permute-done((bf16[2,640,128]{2,1,0:T(8,128)(2,1)S(1)}, bf16[2,640,128]{2,1,0:T(8,128)(2,1)S(1)}, u32[]{:S(2)}, u32[]{:S(2)}) %collective-permute-start.9) | collective-permute-done | bytes 327712 | tf_op jit(solution)/shard_map/ppermute | solution.py:136
  112.2 1.9 %collective-permute-start.10 = (bf16[2,640,128]{2,1,0:T(8,128)(2,1)S(1)}, bf16[2,640,128]{2,1,0:T(8,128)(2,1)S(1)}, u32[]{:S(2)}, u32[]{:S(2)}) collective-permute-start(bf16[2,640,128]{2,1,0:T(8,128)(2,1)S(1)} %collective-permute-done.9.refs_9_), channel_id=1, source_target_pairs={{0,16},{16,0},{32,48},{48,32},{64,80},{80,64},{96,112},{112,96},{1... | collective-permute-start | bytes 983048 | tf_op jit(solution)/shard_map/ppermute | solution.py:146
  114.1 1.9 %collective-permute-start.11 = (bf16[2,640,128]{2,1,0:T(8,128)(2,1)S(1)}, bf16[2,640,128]{2,1,0:T(8,128)(2,1)S(1)}, u32[]{:S(2)}, u32[]{:S(2)}) collective-permute-start(bf16[2,640,128]{2,1,0:T(8,128)(2,1)S(1)} %collective-permute-done.9.refs_9_), channel_id=1, source_target_pairs={{0,32},{16,496},{32,64},{48,16},{64,96},{80,48},{96,128},{112,80},... | collective-permute-start | bytes 983048 | tf_op jit(solution)/shard_map/ppermute | solution.py:136
  116.1 0.0 collective-permute-done.6.refs_4_
  116.1 0.0 copy-start.12
  116.1 0.0 collective-permute-done.10.refs_10_
  116.1 0.0 copy-start.15
  116.1 8.2 %collective-permute-done.11.refs_11_ = bf16[2,640,128]{2,1,0:T(8,128)(2,1)S(1)} collective-permute-done((bf16[2,640,128]{2,1,0:T(8,128)(2,1)S(1)}, bf16[2,640,128]{2,1,0:T(8,128)(2,1)S(1)}, u32[]{:S(2)}, u32[]{:S(2)}) %collective-permute-start.11) | collective-permute-done | bytes 327712 | tf_op jit(solution)/shard_map/ppermute | solution.py:136
  124.3 0.0 copy-done.11
  124.3 0.0 copy-done.12
  124.3 0.0 collective-permute-done.8.refs_8_
  124.3 0.0 all-to-all-done.2
  124.3 0.0 copy-start.4
  124.4 0.0 copy-done.7
  124.4 0.0 copy-done.14
  124.4 0.0 copy-done.15
  124.4 0.7 copy-done.16
  125.1 0.5 copy-done.4
  125.6 8.7 %shard_map.68 = bf16[256,3200]{1,0:T(8,128)(2,1)} custom-call(bf16[256,3200]{1,0:T(8,128)(2,1)} %bitcast.6, f32[3200]{0:T(1024)} %scale_ref.1, bf16[2,640,128]{2,1,0:T(8,128)(2,1)} %copy-done.1, bf16[2,640,128]{2,1,0:T(8,128)(2,1)} %copy-done.7, bf16[2,640,128]{2,1,0:T(8,128)(2,1)} %copy-done.5, bf16[2,640,128]{2,1,0:T(8,128)(2,1)} %copy-done.8, ...), custom_call_target="tpu_custom_call" | custom-call | flops 1310720000 | bytes 10485760 | tf_op jit(solution)/shard_map/pallas_call | solution.py:190
  134.4 27.4 %all_to_all.30 = bf16[16,16,3200]{2,1,0:T(8,128)(2,1)S(1)} all-to-all(bf16[16,16,3200]{2,1,0:T(8,128)(2,1)} %bitcast.7), channel_id=1, replica_groups=mesh['section'=32,'tensor'=16] {'tensor'}, dimensions={0} | all-to-all | bytes 3276800 | tf_op jit(solution)/shard_map/all_to_all | solution.py:203
  161.8 0.9 shard_map.69
  (9 shorter events, 0.1 us)
Async XLA Ops:
  0.0 80.7 %copy-start.3 = (f32[3200]{0:T(1024)S(1)}, f32[3200]{0:T(1024)}, u32[]{:S(2)}) copy-start(f32[3200]{0:T(1024)} %gain_ref.1) | copy-start | bytes 38404
  1.8 3.5 %collective-permute-start = (bf16[640,128]{1,0:T(8,128)(2,1)}, bf16[640,128]{1,0:T(8,128)(2,1)S(1)}, u32[]{:S(2)}, u32[]{:S(2)}) collective-permute-start(bf16[640,128]{1,0:T(8,128)(2,1)} %get-tuple-element.10.mine_ref), channel_id=1, source_target_pairs={{0,16},{16,0},{32,48},{48,32},{64,80},{80,64},{96,112},{112,96},{1... | collective-permute-start | bytes 491528 | tf_op jit(solution)/shard_map/ppermute | solution.py:130
  5.3 0.9 copy-start.2
  6.3 75.8 %copy-start.1 = (bf16[2,640,128]{2,1,0:T(8,128)(2,1)}, bf16[2,640,128]{2,1,0:T(8,128)(2,1)S(1)}, u32[]{:S(2)}) copy-start(bf16[2,640,128]{2,1,0:T(8,128)(2,1)S(1)} %shard_map.65.refs_0_) | copy-start | bytes 983044
  6.3 16.4 %collective-permute-start.1 = (bf16[2,640,128]{2,1,0:T(8,128)(2,1)S(1)}, bf16[2,640,128]{2,1,0:T(8,128)(2,1)S(1)}, u32[]{:S(2)}, u32[]{:S(2)}) collective-permute-start(bf16[2,640,128]{2,1,0:T(8,128)(2,1)S(1)} %shard_map.65.refs_0_), channel_id=1, source_target_pairs={{0,32},{16,496},{32,64},{48,16},{64,96},{80,48},{96,128},{112,80},... | collective-permute-start | bytes 983048 | tf_op jit(solution)/shard_map/ppermute | solution.py:136
  22.7 101.6 %copy-start.7 = (bf16[2,640,128]{2,1,0:T(8,128)(2,1)}, bf16[2,640,128]{2,1,0:T(8,128)(2,1)S(1)}, u32[]{:S(2)}) copy-start(bf16[2,640,128]{2,1,0:T(8,128)(2,1)S(1)} %collective-permute-done.1.refs_1_) | copy-start | bytes 983044
  22.7 11.7 %collective-permute-start.2 = (bf16[2,640,128]{2,1,0:T(8,128)(2,1)S(1)}, bf16[2,640,128]{2,1,0:T(8,128)(2,1)S(1)}, u32[]{:S(2)}, u32[]{:S(2)}) collective-permute-start(bf16[2,640,128]{2,1,0:T(8,128)(2,1)S(1)} %collective-permute-done.1.refs_1_), channel_id=1, source_target_pairs={{0,32},{16,496},{32,64},{48,16},{64,96},{80,48},{96,128},{112,80},... | collective-permute-start | bytes 983048 | tf_op jit(solution)/shard_map/ppermute | solution.py:136
  24.7 27.0 %all-to-all-start = ((bf16[64,8,128]{2,1,0:T(8,128)(2,1)}), bf16[64,8,128]{2,1,0:T(8,128)(2,1)S(1)}, u32[]{:S(2)}, u32[]{:S(2)}) async-start(bf16[64,8,128]{2,1,0:T(8,128)(2,1)} %get-tuple-element.9), calls=%async_computation | async-start | bytes 262144 | tf_op jit(solution)/shard_map/all_to_all | solution.py:175
  34.4 17.2 %copy-start.5 = (bf16[2,640,128]{2,1,0:T(8,128)(2,1)}, bf16[2,640,128]{2,1,0:T(8,128)(2,1)S(1)}, u32[]{:S(2)}) copy-start(bf16[2,640,128]{2,1,0:T(8,128)(2,1)S(1)} %collective-permute-done.2._.refs_2_) | copy-start | bytes 983044
  34.5 13.1 %collective-permute-start.3 = (bf16[2,640,128]{2,1,0:T(8,128)(2,1)S(1)}, bf16[2,640,128]{2,1,0:T(8,128)(2,1)S(1)}, u32[]{:S(2)}, u32[]{:S(2)}) collective-permute-start(bf16[2,640,128]{2,1,0:T(8,128)(2,1)S(1)} %collective-permute-done.2._.refs_2_), channel_id=1, source_target_pairs={{0,32},{16,496},{32,64},{48,16},{64,96},{80,48},{96,128},{112,80},... | collective-permute-start | bytes 983048 | tf_op jit(solution)/shard_map/ppermute | solution.py:136
  47.5 45.0 %copy-start.8 = (bf16[2,640,128]{2,1,0:T(8,128)(2,1)}, bf16[2,640,128]{2,1,0:T(8,128)(2,1)S(1)}, u32[]{:S(2)}) copy-start(bf16[2,640,128]{2,1,0:T(8,128)(2,1)S(1)} %collective-permute-done.3.refs_3_) | copy-start | bytes 983044
  47.5 15.9 %collective-permute-start.4 = (bf16[2,640,128]{2,1,0:T(8,128)(2,1)S(1)}, bf16[2,640,128]{2,1,0:T(8,128)(2,1)S(1)}, u32[]{:S(2)}, u32[]{:S(2)}) collective-permute-start(bf16[2,640,128]{2,1,0:T(8,128)(2,1)S(1)} %collective-permute-done.3.refs_3_), channel_id=1, source_target_pairs={{0,32},{16,496},{32,64},{48,16},{64,96},{80,48},{96,128},{112,80},... | collective-permute-start | bytes 983048 | tf_op jit(solution)/shard_map/ppermute | solution.py:136
  51.7 0.7 copy-start.13
  54.0 26.7 %all-to-all-start.1 = ((bf16[64,8,128]{2,1,0:T(8,128)(2,1)}), bf16[64,8,128]{2,1,0:T(8,128)(2,1)S(1)}, u32[]{:S(2)}, u32[]{:S(2)}) async-start(bf16[64,8,128]{2,1,0:T(8,128)(2,1)} %shard_map.66), calls=%async_computation.1 | async-start | bytes 262144 | tf_op jit(solution)/shard_map/all_to_all | solution.py:177
  63.4 18.7 %copy-start.9 = (bf16[2,640,128]{2,1,0:T(8,128)(2,1)}, bf16[2,640,128]{2,1,0:T(8,128)(2,1)S(1)}, u32[]{:S(2)}) copy-start(bf16[2,640,128]{2,1,0:T(8,128)(2,1)S(1)} %collective-permute-done.4.refs_5_) | copy-start | bytes 983044
  63.4 17.2 %collective-permute-start.5 = (bf16[2,640,128]{2,1,0:T(8,128)(2,1)S(1)}, bf16[2,640,128]{2,1,0:T(8,128)(2,1)S(1)}, u32[]{:S(2)}, u32[]{:S(2)}) collective-permute-start(bf16[2,640,128]{2,1,0:T(8,128)(2,1)S(1)} %collective-permute-done.4.refs_5_), channel_id=1, source_target_pairs={{0,32},{16,496},{32,64},{48,16},{64,96},{80,48},{96,128},{112,80},... | collective-permute-start | bytes 983048 | tf_op jit(solution)/shard_map/ppermute | solution.py:136
  80.7 19.3 %copy-start = (bf16[2,640,128]{2,1,0:T(8,128)(2,1)}, bf16[2,640,128]{2,1,0:T(8,128)(2,1)S(1)}, u32[]{:S(2)}) copy-start(bf16[2,640,128]{2,1,0:T(8,128)(2,1)S(1)} %collective-permute-done.5._.refs_6_) | copy-start | bytes 983044
  82.1 10.4 %copy-start.6 = (bf16[2,640,128]{2,1,0:T(8,128)(2,1)S(1)}, bf16[2,640,128]{2,1,0:T(8,128)(2,1)}, u32[]{:S(2)}) copy-start(bf16[2,640,128]{2,1,0:T(8,128)(2,1)} %copy-done.5) | copy-start | bytes 983044
  82.1 42.2 %all-to-all-start.2 = ((bf16[16,16,3200]{2,1,0:T(8,128)(2,1)}), bf16[16,16,3200]{2,1,0:T(8,128)(2,1)S(1)}, u32[]{:S(2)}, u32[]{:S(2)}) async-start(bf16[16,16,3200]{2,1,0:T(8,128)(2,1)} %bitcast.1), calls=%async_computation.2 | async-start | bytes 3276800 | tf_op jit(solution)/shard_map/all_to_all | solution.py:189
  89.7 10.3 %copy-start.10 = (bf16[2,640,128]{2,1,0:T(8,128)(2,1)S(1)}, bf16[2,640,128]{2,1,0:T(8,128)(2,1)}, u32[]{:S(2)}) copy-start(bf16[2,640,128]{2,1,0:T(8,128)(2,1)} %copy-done.9) | copy-start | bytes 983044
  89.7 10.3 %collective-permute-start.7 = (bf16[2,640,128]{2,1,0:T(8,128)(2,1)S(1)}, bf16[2,640,128]{2,1,0:T(8,128)(2,1)S(1)}, u32[]{:S(2)}, u32[]{:S(2)}) collective-permute-start(bf16[2,640,128]{2,1,0:T(8,128)(2,1)S(1)} %collective-permute-done.5._.refs_6_), channel_id=1, source_target_pairs={{0,32},{16,496},{32,64},{48,16},{64,96},{80,48},{96,128},{112,80},... | collective-permute-start | bytes 983048 | tf_op jit(solution)/shard_map/ppermute | solution.py:136
  92.6 23.4 %collective-permute-start.6 = (bf16[6,640,128]{2,1,0:T(8,128)(2,1)S(1)}, bf16[6,640,128]{2,1,0:T(8,128)(2,1)S(1)}, u32[]{:S(2)}, u32[]{:S(2)}) collective-permute-start(bf16[6,640,128]{2,1,0:T(8,128)(2,1)S(1)} %pad_maximum_fusion), channel_id=1, source_target_pairs={{0,16},{16,0},{32,48},{48,32},{64,80},{80,64},{96,112},{112,96},{1... | collective-permute-start | bytes 2949128 | tf_op jit(solution)/shard_map/ppermute | solution.py:146
  100.0 24.3 %copy-start.11 = (bf16[2,640,128]{2,1,0:T(8,128)(2,1)}, bf16[2,640,128]{2,1,0:T(8,128)(2,1)S(1)}, u32[]{:S(2)}) copy-start(bf16[2,640,128]{2,1,0:T(8,128)(2,1)S(1)} %collective-permute-done.7.refs_7_) | copy-start | bytes 983044
  100.1 24.2 %collective-permute-start.8 = (bf16[6,640,128]{2,1,0:T(8,128)(2,1)S(1)}, bf16[6,640,128]{2,1,0:T(8,128)(2,1)}, u32[]{:S(2)}, u32[]{:S(2)}) collective-permute-start(bf16[6,640,128]{2,1,0:T(8,128)(2,1)S(1)} %pad_maximum_fusion.1), channel_id=1, source_target_pairs={{0,16},{16,0},{32,48},{48,32},{64,80},{80,64},{96,112},{112,96},{1... | collective-permute-start | bytes 2949128 | tf_op jit(solution)/shard_map/ppermute | solution.py:146
  102.0 10.2 %collective-permute-start.9 = (bf16[2,640,128]{2,1,0:T(8,128)(2,1)S(1)}, bf16[2,640,128]{2,1,0:T(8,128)(2,1)S(1)}, u32[]{:S(2)}, u32[]{:S(2)}) collective-permute-start(bf16[2,640,128]{2,1,0:T(8,128)(2,1)S(1)} %collective-permute-done.7.refs_7_), channel_id=1, source_target_pairs={{0,32},{16,496},{32,64},{48,16},{64,96},{80,48},{96,128},{112,80},... | collective-permute-start | bytes 983048 | tf_op jit(solution)/shard_map/ppermute | solution.py:136
  112.2 12.1 %copy-start.14 = (bf16[2,640,128]{2,1,0:T(8,128)(2,1)}, bf16[2,640,128]{2,1,0:T(8,128)(2,1)S(1)}, u32[]{:S(2)}) copy-start(bf16[2,640,128]{2,1,0:T(8,128)(2,1)S(1)} %collective-permute-done.9.refs_9_) | copy-start | bytes 983044
  112.2 3.9 %collective-permute-start.10 = (bf16[2,640,128]{2,1,0:T(8,128)(2,1)S(1)}, bf16[2,640,128]{2,1,0:T(8,128)(2,1)S(1)}, u32[]{:S(2)}, u32[]{:S(2)}) collective-permute-start(bf16[2,640,128]{2,1,0:T(8,128)(2,1)S(1)} %collective-permute-done.9.refs_9_), channel_id=1, source_target_pairs={{0,16},{16,0},{32,48},{48,32},{64,80},{80,64},{96,112},{112,96},{1... | collective-permute-start | bytes 983048 | tf_op jit(solution)/shard_map/ppermute | solution.py:146
  114.1 10.2 %collective-permute-start.11 = (bf16[2,640,128]{2,1,0:T(8,128)(2,1)S(1)}, bf16[2,640,128]{2,1,0:T(8,128)(2,1)S(1)}, u32[]{:S(2)}, u32[]{:S(2)}) collective-permute-start(bf16[2,640,128]{2,1,0:T(8,128)(2,1)S(1)} %collective-permute-done.9.refs_9_), channel_id=1, source_target_pairs={{0,32},{16,496},{32,64},{48,16},{64,96},{80,48},{96,128},{112,80},... | collective-permute-start | bytes 983048 | tf_op jit(solution)/shard_map/ppermute | solution.py:136
  116.1 8.2 %copy-start.12 = (bf16[6,640,128]{2,1,0:T(8,128)(2,1)}, bf16[6,640,128]{2,1,0:T(8,128)(2,1)S(1)}, u32[]{:S(2)}) copy-start(bf16[6,640,128]{2,1,0:T(8,128)(2,1)S(1)} %collective-permute-done.6.refs_4_) | copy-start | bytes 2949124
  116.1 8.3 %copy-start.15 = (bf16[2,640,128]{2,1,0:T(8,128)(2,1)}, bf16[2,640,128]{2,1,0:T(8,128)(2,1)S(1)}, u32[]{:S(2)}) copy-start(bf16[2,640,128]{2,1,0:T(8,128)(2,1)S(1)} %collective-permute-done.10.refs_10_) | copy-start | bytes 983044
  124.3 0.8 copy-start.16
  124.3 1.3 copy-start.4

commit v9 on v6

v9 whole, which is shorter than its diff:
```python
import functools

import jax
import jax.numpy as jnp
from jax import lax
from jax.experimental import pallas as pl
from jax.experimental.pallas import tpu as pltpu
from jax.sharding import PartitionSpec as P

LANE = 128
VMEM = pl.BlockSpec(memory_space=pltpu.VMEM)
ANY = pl.BlockSpec(memory_space=pl.ANY)
SMEM = pl.BlockSpec(memory_space=pltpu.SMEM)


def call(body, out_shape, in_specs, flops=0, moved=0, n_out=1, scratch=(), limit=32, out=VMEM):
    return pl.pallas_call(
        body,
        out_shape=out_shape,
        in_specs=in_specs,
        out_specs=out if n_out == 1 else [out] * n_out,
        scratch_shapes=list(scratch),
        compiler_params=pltpu.CompilerParams(vmem_limit_bytes=limit * 1024 * 1024),
        cost_estimate=pl.CostEstimate(flops=flops, bytes_accessed=moved, transcendentals=0),
    )


def first_body(x_ref, in_ref, out_ref, gain_ref, scale_ref, weights_ref, tiles_ref, both_ref):
    both_ref[0] = gain_ref[...]
    both_ref[1] = scale_ref[...]
    part = in_ref.shape[1]
    kept = weights_ref.shape[0] // 2
    fold, chunk = kept // 4, part // 4
    for k, ref in enumerate((in_ref, out_ref)):
        at = k * kept
        weights_ref[at : at + kept, :part] = ref[:kept, :]
        for j in range(4):
            weights_ref[at + j * fold : at + (j + 1) * fold, part : part + chunk] = ref[
                kept:, j * chunk : (j + 1) * chunk
            ]
        edge = LANE - part - chunk
        weights_ref[at : at + kept, part + chunk :] = jnp.zeros((kept, edge), weights_ref.dtype)
    blocks, rows, width = x_ref.shape
    for m in range(tiles_ref.shape[0] // blocks):
        for b in range(blocks):
            if (m + 1) * LANE <= width:
                tiles_ref[m * blocks + b] = x_ref[b, :, m * LANE : (m + 1) * LANE]
            else:
                tiles_ref[m * blocks + b] = jnp.zeros((rows, LANE), tiles_ref.dtype)


def order_body(plan_ref, x_ref, o_ref):
    for p in range(o_ref.shape[0]):
        o_ref[p] = x_ref[plan_ref[p]]


def norm_body(x_ref, both_ref, rows_ref, copies_ref, scale_out_ref):
    blocks, rows, width = rows_ref.shape
    tiles = width // LANE
    for b in range(blocks):
        whole = jnp.concatenate([x_ref[m * blocks + b] for m in range(tiles)], axis=-1)
        rows_ref[b] = whole
        values = whole.astype(jnp.float32)
        mean_square = jnp.sum(values * values, axis=-1, keepdims=True) * (1.0 / width)
        normed = values * lax.rsqrt(mean_square + 1e-06) * both_ref[:1, :]
        normed = normed.astype(jnp.bfloat16)
        for t in range(copies_ref.shape[0]):
            copies_ref[t, b] = normed
    scale_out_ref[...] = both_ref[1:, :]


def spread_body(part, x_ref, o_ref):
    blank = jnp.zeros((x_ref.shape[0], LANE - part), x_ref.dtype)
    for s in range(o_ref.shape[1] // LANE):
        o_ref[:, s * LANE : (s + 1) * LANE] = jnp.concatenate(
            [x_ref[:, s * part : (s + 1) * part], blank], axis=1
        )


def opened(ref, index, at, kept, part):
    fold, chunk = kept // 4, part // 4
    rest = [ref[index, at + j * fold : at + (j + 1) * fold, part : part + chunk] for j in range(4)]
    rest.append(jnp.zeros((fold, LANE - part), ref.dtype))
    return jnp.concatenate([ref[index, at : at + kept, :], jnp.concatenate(rest, axis=1)], axis=0)


def mlp_body(part, units, x_hbm, w_hbm, o_hbm, x_ref, held, o_ref, x_sem, in_sem, out_sem, o_sems):
    sections, both, _ = held.shape
    kept = both // 2
    rows = x_ref.shape[0]
    x_copy = pltpu.make_async_copy(x_hbm, x_ref, x_sem)
    x_copy.start()
    first, second = pl.ds(0, kept), pl.ds(kept, kept)
    in_copy = pltpu.make_async_copy(w_hbm.at[:, first], held.at[:, first], in_sem)
    in_copy.start()
    out_copy = pltpu.make_async_copy(w_hbm.at[:, second], held.at[:, second], out_sem)
    out_copy.start()
    x_copy.wait()
    in_copy.wait()
    total = jnp.zeros((rows, units), jnp.float32)
    for s in range(0, sections, 2):
        pair = [opened(held, s + k, 0, kept, part) for k in range(2)]
        total += lax.dot_general(
            x_ref[:, s * LANE : (s + 2) * LANE],
            jnp.concatenate(pair, axis=1),
            (((1,), (1,)), ((), ())),
            preferred_element_type=jnp.float32,
        )
    hidden = 0.5 * total * (1.0 + lax.erf(total * (0.5**0.5)))
    hidden = hidden.astype(jnp.bfloat16)
    out_copy.wait()
    pairs = [
        jnp.concatenate([opened(held, s + k, kept, kept, part) for k in range(2)], axis=1)
        for s in range(0, sections, 2)
    ]
    size = rows // 2
    copies = []
    for h in range(2):
        own = slice(h * size, (h + 1) * size)
        for j, pair in enumerate(pairs):
            product = jnp.dot(hidden[own], pair, preferred_element_type=jnp.float32)
            product = product.astype(jnp.bfloat16)
            for i in range(2):
                at = (2 * j + i) * part
                o_ref[own, at : at + part] = product[:, i * LANE : i * LANE + part]
        place = pl.ds(h * size, size)
        copy = pltpu.make_async_copy(o_ref.at[place], o_hbm.at[place], o_sems.at[h])
        copy.start()
        copies.append(copy)
    for copy in copies:
        copy.wait()


def sum_body(x_ref, rows_ref, scale_ref, o_ref):
    blocks = rows_ref.shape[0]
    for b in range(blocks):
        branch = x_ref[0, b].astype(jnp.float32)
        for t in range(1, x_ref.shape[0]):
            branch += x_ref[t, b].astype(jnp.float32)
        values = rows_ref[b].astype(jnp.float32)
        o_ref[b] = (values + scale_ref[...] * branch).astype(o_ref.dtype)


def local(sections, groups, patches, plan, norm_gain, proj_in, proj_out, layer_scale):
    blocks, rows, width = patches.shape
    bf16 = jnp.bfloat16
    part, units = proj_in.shape
    kept = units * 4 // 5
    shape = jax.ShapeDtypeStruct((sections * blocks, rows, LANE), bf16)
    weights, tiles, gain_and_scale = call(
        first_body,
        (
            jax.ShapeDtypeStruct((2 * kept, LANE), bf16),
            shape,
            jax.ShapeDtypeStruct((2, width), jnp.float32),
        ),
        [VMEM] * 5,
        n_out=3,
        limit=60,
    )(patches, proj_in.T, proj_out, norm_gain, layer_scale)
    weights = lax.all_gather(weights, "section", axis=0, tiled=False)
    tiles = lax.all_to_all(tiles, "section", 0, 0, tiled=True)
    tiles = call(order_body, shape, [SMEM, VMEM])(plan, tiles)
    tiles = lax.all_to_all(tiles, "section", 0, 0, tiled=True)
    own, copies, scale = call(
        norm_body,
        (
            jax.ShapeDtypeStruct((blocks, rows, width), bf16),
            jax.ShapeDtypeStruct((groups, blocks, rows, width), bf16),
            jax.ShapeDtypeStruct((1, width), jnp.float32),
        ),
        [VMEM, VMEM],
        n_out=3,
    )(tiles, gain_and_scale)

    all_rows = groups * blocks * rows
    normed = lax.all_to_all(copies.reshape(all_rows, width), "tensor", 0, 0, tiled=True)
    spread = call(
        functools.partial(spread_body, part),
        jax.ShapeDtypeStruct((all_rows, sections * LANE), bf16),
        [VMEM],
    )(normed)
    partial_sum = call(
        functools.partial(mlp_body, part, units),
        jax.ShapeDtypeStruct((all_rows, width), bf16),
        [ANY, ANY],
        flops=4 * all_rows * width * units,
        moved=10 * 1024 * 1024,
        scratch=[
            pltpu.VMEM((all_rows, sections * LANE), bf16),
            pltpu.VMEM((sections, 2 * kept, LANE), bf16),
            pltpu.VMEM((all_rows, width), bf16),
            pltpu.SemaphoreType.DMA(()),
            pltpu.SemaphoreType.DMA(()),
            pltpu.SemaphoreType.DMA(()),
            pltpu.SemaphoreType.DMA((2,)),
        ],
        limit=60,
        out=ANY,
    )(spread, weights)
    terms = lax.all_to_all(partial_sum, "tensor", 0, 0, tiled=True)
    return call(
        sum_body,
        jax.ShapeDtypeStruct((blocks, rows, width), bf16),
        [VMEM, VMEM, VMEM],
    )(terms.reshape(groups, blocks, rows, width), own, scale)


def solution(mesh):
    return jax.shard_map(
        functools.partial(local, mesh.shape["section"], mesh.shape["tensor"]),
        mesh=mesh,
        in_specs=(
            P("section", "tensor", None),
            P(),
            P(),
            P("section", "tensor"),
            P("tensor", "section"),
            P(),
        ),
        out_specs=P("section", "tensor", None),
        check_vma=False,
    )
```

time: 144 us -> 138 us (0.958)
  Pallas kernels: 15.6 us -> 11.1 us
  blocking collectives: 113 us -> 110 us
  local copies, waits for them, and re-layouts: 0 us -> 2.75 us
    unnamed x0 -> x6, local copies, waits for them, and re-layouts: none -> 2.75 us
    pallas_call x1, Pallas kernels: 2.41 us -> 0.22 us  [local(): call(norm_body, (jax.ShapeDtypeStruct((blocks, rows, width), bf16), jax.S...]
    all_to_all x1, blocking collectives: 28.7 us -> 26.5 us  [local(): terms = lax.all_to_all(partial_sum, 'tensor', 0, 0, tiled=True)]
    all_to_all x2, blocking collectives: 55.8 us -> 54.2 us  [local(): tiles = lax.all_to_all(tiles, 'section', 0, 0, tiled=True)]
    pallas_call x1, Pallas kernels: 2.37 us -> 0.88 us  [local(): call(sum_body, jax.ShapeDtypeStruct((blocks, rows, width), bf16), [VMEM,...]
    pallas_call x3 -> x4, Pallas kernels: 10.8 us -> 9.99 us  [the longest x1 6.57 us: local(): call(functools.partial(mlp_body, part, units), jax.ShapeDtypeStruct((all_...]
  transfers between devices with their start and end apart: 1 -> 1, of which waited for: 0 -> 0; matrix products, arithmetic and copies ran while one was open for 0% -> 0% of each run, Pallas kernels for 3% -> 1%
where the time goes in v9:
time: 138 us; the launch traced here: 137 us
  blocking collectives  110 us (80%)
  between operations  13.4 us (10%)
  Pallas kernels  11.1 us (8%)
  local copies, waits for them, and re-layouts  2.75 us (2%)
    all_to_all x2, blocking collectives, local(): tiles = lax.all_to_all(tiles, 'section', 0, 0, tiled=True)  54.2 us
    all_to_all x1, blocking collectives, local(): lax.all_to_all(copies.reshape(all_rows, width), 'tensor', 0, 0, tiled=True)  29.3 us
    all_to_all x1, blocking collectives, local(): terms = lax.all_to_all(partial_sum, 'tensor', 0, 0, tiled=True)  26.5 us
    pallas_call x1, Pallas kernels, local(): call(functools.partial(mlp_body, part, units), jax.ShapeDtypeStruct((all_...  6.57 us
  transfers between devices with their start and end apart: 1, of which 0 were waited for; matrix products, arithmetic and copies ran while one was open for 0% of the time, Pallas kernels for 1%

profile of v9, /device:TPU:6, one launch (start us, length us, event | category | flops | bytes accessed | tf_op | source)
XLA Modules:
  0.0 137.3 jit_solution(14479886642855104906)
XLA Ops:
  6.5 0.0 all-gather.3.cloned.1.call-start
  6.5 1.8 %shard_map.64 = (bf16[640,128]{1,0:T(8,128)(2,1)}, bf16[64,8,128]{2,1,0:T(8,128)(2,1)}, f32[2,3200]{1,0:T(2,128)}) custom-call(bf16[2,8,3200]{2,1,0:T(8,128)(2,1)} %x_ref.1, bf16[400,100]{1,0:T(8,128)(2,1)} %bitcast.11, bf16[400,100]{1,0:T(8,128)(2,1)} %out_ref.1, f32[3200]{0:T(1024)} %gain_ref.1, f32[3200]{0:T(1024)} %scale_ref.1), custom_call_target="tpu_custom_call" | custom-call | tf_op jit(solution)/shard_map/pallas_call | solution.py:150
  8.4 0.0 all-gather.3.cloned.1.call-update
  8.4 32.8 %all_to_all.30.x_ref = bf16[64,8,128]{2,1,0:T(8,128)(2,1)S(1)} all-to-all(bf16[64,8,128]{2,1,0:T(8,128)(2,1)} %get-tuple-element.11), channel_id=1, replica_groups=mesh['section'=32,'tensor'=16] {'section'}, dimensions={0} | all-to-all | bytes 262144 | tf_op jit(solution)/shard_map/all_to_all | solution.py:162
  41.2 0.0 copy-start.2
  41.2 0.7 copy-done.2
  41.9 0.6 shard_map.65
  42.5 21.3 %all_to_all.31.x_ref = bf16[64,8,128]{2,1,0:T(8,128)(2,1)S(1)} all-to-all(bf16[64,8,128]{2,1,0:T(8,128)(2,1)S(1)} %shard_map.65), channel_id=1, replica_groups=mesh['section'=32,'tensor'=16] {'section'}, dimensions={0} | all-to-all | bytes 262144 | tf_op jit(solution)/shard_map/all_to_all | solution.py:164
  63.8 0.0 copy-start.1
  63.8 0.7 copy-done.1
  64.6 0.2 shard_map.66
  64.8 29.3 %all_to_all.32 = bf16[16,16,3200]{2,1,0:T(8,128)(2,1)S(1)} all-to-all(bf16[16,16,3200]{2,1,0:T(8,128)(2,1)S(1)} %bitcast.8), channel_id=1, replica_groups=mesh['section'=32,'tensor'=16] {'tensor'}, dimensions={0} | all-to-all | bytes 3276800 | tf_op jit(solution)/shard_map/all_to_all | solution.py:177
  94.1 1.0 shard_map.67.x_hbm
  95.1 0.0 copy-start
  95.1 1.3 copy-done
  96.5 0.0 all-gather.3.cloned.1.call-done
  96.5 6.6 %shard_map.68 = bf16[256,3200]{1,0:T(8,128)(2,1)} custom-call(bf16[256,4096]{1,0:T(8,128)(2,1)} %copy-done, bf16[32,640,128]{2,1,0:T(8,128)(2,1)} %bitcast.10), custom_call_target="tpu_custom_call" | custom-call | flops 1310720000 | bytes 10485760 | tf_op jit(solution)/shard_map/pallas_call | solution.py:183
  103.1 26.5 %all_to_all.33 = bf16[16,16,3200]{2,1,0:T(8,128)(2,1)S(1)} all-to-all(bf16[16,16,3200]{2,1,0:T(8,128)(2,1)} %bitcast.9), channel_id=1, replica_groups=mesh['section'=32,'tensor'=16] {'tensor'}, dimensions={0} | all-to-all | bytes 3276800 | tf_op jit(solution)/shard_map/all_to_all | solution.py:201
  129.6 0.9 shard_map.69
Async XLA Ops:
  6.5 89.9 %all-gather.3.cloned.1.call-start = ((), (), s32[]{:S(2)}) async-start(), calls=%async_computation.4 | async-start | bytes 5406720 | tf_op jit(solution)/shard_map/all_gather | solution.py:161
  41.2 0.7 copy-start.2
  63.8 0.7 copy-start.1
  95.1 1.4 copy-start
Sparse Core Ops, SparseCore 0:
  9.5 84.2 all-gather.2

commit v10 on v9

--- a/solution.py
+++ b/solution.py
@@ -13,12 +13,12 @@
 SMEM = pl.BlockSpec(memory_space=pltpu.SMEM)
 
 
-def call(body, out_shape, in_specs, flops=0, moved=0, n_out=1, scratch=(), limit=32, out=VMEM):
+def call(body, out_shape, in_specs, flops=0, moved=0, n_out=1, scratch=(), limit=32):
     return pl.pallas_call(
         body,
         out_shape=out_shape,
         in_specs=in_specs,
-        out_specs=out if n_out == 1 else [out] * n_out,
+        out_specs=VMEM if n_out == 1 else [VMEM] * n_out,
         scratch_shapes=list(scratch),
         compiler_params=pltpu.CompilerParams(vmem_limit_bytes=limit * 1024 * 1024),
         cost_estimate=pl.CostEstimate(flops=flops, bytes_accessed=moved, transcendentals=0),
@@ -69,14 +69,6 @@
     scale_out_ref[...] = both_ref[1:, :]
 
 
-def spread_body(part, x_ref, o_ref):
-    blank = jnp.zeros((x_ref.shape[0], LANE - part), x_ref.dtype)
-    for s in range(o_ref.shape[1] // LANE):
-        o_ref[:, s * LANE : (s + 1) * LANE] = jnp.concatenate(
-            [x_ref[:, s * part : (s + 1) * part], blank], axis=1
-        )
-
-
 def opened(ref, index, at, kept, part):
     fold, chunk = kept // 4, part // 4
     rest = [ref[index, at + j * fold : at + (j + 1) * fold, part : part + chunk] for j in range(4)]
@@ -84,24 +76,25 @@
     return jnp.concatenate([ref[index, at : at + kept, :], jnp.concatenate(rest, axis=1)], axis=0)
 
 
-def mlp_body(part, units, x_hbm, w_hbm, o_hbm, x_ref, held, o_ref, x_sem, in_sem, out_sem, o_sems):
+def mlp_body(part, units, x_ref, w_hbm, o_ref, spread, held, in_sem, out_sem):
     sections, both, _ = held.shape
     kept = both // 2
-    rows = x_ref.shape[0]
-    x_copy = pltpu.make_async_copy(x_hbm, x_ref, x_sem)
-    x_copy.start()
     first, second = pl.ds(0, kept), pl.ds(kept, kept)
     in_copy = pltpu.make_async_copy(w_hbm.at[:, first], held.at[:, first], in_sem)
     in_copy.start()
     out_copy = pltpu.make_async_copy(w_hbm.at[:, second], held.at[:, second], out_sem)
     out_copy.start()
-    x_copy.wait()
+    blank = jnp.zeros((x_ref.shape[0], LANE - part), x_ref.dtype)
+    for s in range(sections):
+        spread[:, s * LANE : (s + 1) * LANE] = jnp.concatenate(
+            [x_ref[:, s * part : (s + 1) * part], blank], axis=1
+        )
     in_copy.wait()
-    total = jnp.zeros((rows, units), jnp.float32)
+    total = jnp.zeros((x_ref.shape[0], units), jnp.float32)
     for s in range(0, sections, 2):
         pair = [opened(held, s + k, 0, kept, part) for k in range(2)]
         total += lax.dot_general(
-            x_ref[:, s * LANE : (s + 2) * LANE],
+            spread[:, s * LANE : (s + 2) * LANE],
             jnp.concatenate(pair, axis=1),
             (((1,), (1,)), ((), ())),
             preferred_element_type=jnp.float32,
@@ -109,26 +102,14 @@
     hidden = 0.5 * total * (1.0 + lax.erf(total * (0.5**0.5)))
     hidden = hidden.astype(jnp.bfloat16)
     out_copy.wait()
-    pairs = [
-        jnp.concatenate([opened(held, s + k, kept, kept, part) for k in range(2)], axis=1)
-        for s in range(0, sections, 2)
-    ]
-    size = rows // 2
-    copies = []
-    for h in range(2):
-        own = slice(h * size, (h + 1) * size)
-        for j, pair in enumerate(pairs):
-            product = jnp.dot(hidden[own], pair, preferred_element_type=jnp.float32)
-            product = product.astype(jnp.bfloat16)
-            for i in range(2):
-                at = (2 * j + i) * part
-                o_ref[own, at : at + part] = product[:, i * LANE : i * LANE + part]
-        place = pl.ds(h * size, size)
-        copy = pltpu.make_async_copy(o_ref.at[place], o_hbm.at[place], o_sems.at[h])
-        copy.start()
-        copies.append(copy)
-    for copy in copies:
-        copy.wait()
+    for s in range(0, sections, 2):
+        pair = [opened(held, s + k, kept, kept, part) for k in range(2)]
+        product = jnp.dot(
+            hidden, jnp.concatenate(pair, axis=1), preferred_element_type=jnp.float32
+        ).astype(jnp.bfloat16)
+        for i in range(2):
+            at = (s + i) * part
+            o_ref[:, at : at + part] = product[:, i * LANE : i * LANE + part]
 
 
 def sum_body(x_ref, rows_ref, scale_ref, o_ref):
@@ -175,29 +156,20 @@
 
     all_rows = groups * blocks * rows
     normed = lax.all_to_all(copies.reshape(all_rows, width), "tensor", 0, 0, tiled=True)
-    spread = call(
-        functools.partial(spread_body, part),
-        jax.ShapeDtypeStruct((all_rows, sections * LANE), bf16),
-        [VMEM],
-    )(normed)
     partial_sum = call(
         functools.partial(mlp_body, part, units),
         jax.ShapeDtypeStruct((all_rows, width), bf16),
-        [ANY, ANY],
+        [VMEM, ANY],
         flops=4 * all_rows * width * units,
         moved=10 * 1024 * 1024,
         scratch=[
             pltpu.VMEM((all_rows, sections * LANE), bf16),
             pltpu.VMEM((sections, 2 * kept, LANE), bf16),
-            pltpu.VMEM((all_rows, width), bf16),
             pltpu.SemaphoreType.DMA(()),
             pltpu.SemaphoreType.DMA(()),
-            pltpu.SemaphoreType.DMA(()),
-            pltpu.SemaphoreType.DMA((2,)),
         ],
-        limit=60,
-        out=ANY,
-    )(spread, weights)
+        limit=50,
+    )(normed, weights)
     terms = lax.all_to_all(partial_sum, "tensor", 0, 0, tiled=True)
     return call(
         sum_body,

time: 138 us -> 140 us (1.014)
  blocking collectives: 110 us -> 112 us
    all_to_all x1, blocking collectives: 26.5 us -> 28.7 us  [local(): terms = lax.all_to_all(partial_sum, 'tensor', 0, 0, tiled=True)]
where the time goes in v10:
time: 140 us; the launch traced here: 138 us
  blocking collectives  112 us (80%)
  between operations  13.4 us (10%)
  Pallas kernels  11.1 us (8%)
    all_to_all x2, blocking collectives, local(): tiles = lax.all_to_all(tiles, 'section', 0, 0, tiled=True)  54.2 us
    all_to_all x1, blocking collectives, local(): lax.all_to_all(copies.reshape(all_rows, width), 'tensor', 0, 0, tiled=True)  29.3 us
    all_to_all x1, blocking collectives, local(): terms = lax.all_to_all(partial_sum, 'tensor', 0, 0, tiled=True)  28.7 us
    pallas_call x1, Pallas kernels, local(): call(functools.partial(mlp_body, part, units), jax.ShapeDtypeStruct((all_...  7.51 us
  transfers between devices with their start and end apart: 1, of which 0 were waited for; matrix products, arithmetic and copies ran while one was open for 0% of the time, Pallas kernels for 1%

profile of v10, /device:TPU:6, one launch (start us, length us, event | category | flops | bytes accessed | tf_op | source)
XLA Modules:
  0.0 138.1 jit_solution(18429887799063750411)
XLA Ops:
  6.5 0.0 all-gather.3.cloned.1.call-start
  6.5 1.8 %shard_map.64 = (bf16[640,128]{1,0:T(8,128)(2,1)}, bf16[64,8,128]{2,1,0:T(8,128)(2,1)}, f32[2,3200]{1,0:T(2,128)}) custom-call(bf16[2,8,3200]{2,1,0:T(8,128)(2,1)} %x_ref.1, bf16[400,100]{1,0:T(8,128)(2,1)} %bitcast.11, bf16[400,100]{1,0:T(8,128)(2,1)} %out_ref.1, f32[3200]{0:T(1024)} %gain_ref.1, f32[3200]{0:T(1024)} %scale_ref.1), custom_call_target="tpu_custom_call" | custom-call | tf_op jit(solution)/shard_map/pallas_call | solution.py:131
  8.4 0.0 all-gather.3.cloned.1.call-update
  8.4 32.8 %all_to_all.30.x_ref = bf16[64,8,128]{2,1,0:T(8,128)(2,1)S(1)} all-to-all(bf16[64,8,128]{2,1,0:T(8,128)(2,1)} %get-tuple-element.11), channel_id=1, replica_groups=mesh['section'=32,'tensor'=16] {'section'}, dimensions={0} | all-to-all | bytes 262144 | tf_op jit(solution)/shard_map/all_to_all | solution.py:143
  41.2 0.0 copy-start.1
  41.2 0.7 copy-done.1
  41.9 0.6 shard_map.65
  42.5 21.4 %all_to_all.31.x_ref = bf16[64,8,128]{2,1,0:T(8,128)(2,1)S(1)} all-to-all(bf16[64,8,128]{2,1,0:T(8,128)(2,1)S(1)} %shard_map.65), channel_id=1, replica_groups=mesh['section'=32,'tensor'=16] {'section'}, dimensions={0} | all-to-all | bytes 262144 | tf_op jit(solution)/shard_map/all_to_all | solution.py:145
  63.9 0.0 copy-start
  63.9 0.7 copy-done
  64.6 0.2 shard_map.66
  64.8 29.3 %all_to_all.32 = bf16[16,16,3200]{2,1,0:T(8,128)(2,1)S(1)} all-to-all(bf16[16,16,3200]{2,1,0:T(8,128)(2,1)S(1)} %bitcast.9), channel_id=1, replica_groups=mesh['section'=32,'tensor'=16] {'tensor'}, dimensions={0} | all-to-all | bytes 3276800 | tf_op jit(solution)/shard_map/all_to_all | solution.py:158
  94.1 0.0 all-gather.3.cloned.1.call-done
  94.1 7.5 %shard_map.67 = bf16[256,3200]{1,0:T(8,128)(2,1)S(1)} custom-call(bf16[256,3200]{1,0:T(8,128)(2,1)S(1)} %bitcast.7, bf16[32,640,128]{2,1,0:T(8,128)(2,1)} %bitcast.10), custom_call_target="tpu_custom_call" | custom-call | flops 1310720000 | bytes 10485760 | tf_op jit(solution)/shard_map/pallas_call | solution.py:159
  101.7 28.7 %all_to_all.33 = bf16[16,16,3200]{2,1,0:T(8,128)(2,1)S(1)} all-to-all(bf16[16,16,3200]{2,1,0:T(8,128)(2,1)S(1)} %bitcast.8), channel_id=1, replica_groups=mesh['section'=32,'tensor'=16] {'tensor'}, dimensions={0} | all-to-all | bytes 3276800 | tf_op jit(solution)/shard_map/all_to_all | solution.py:173
  130.3 0.9 shard_map.68
Async XLA Ops:
  6.5 87.6 %all-gather.3.cloned.1.call-start = ((), (), s32[]{:S(2)}) async-start(), calls=%async_computation.4 | async-start | bytes 5406720 | tf_op jit(solution)/shard_map/all_gather | solution.py:142
  41.2 0.7 copy-start.1
  63.9 0.7 copy-start
Sparse Core Ops, SparseCore 0:
  9.5 84.3 all-gather.2

commit v11 on v10

--- a/solution.py
+++ b/solution.py
@@ -1,11 +1,12 @@
 import functools
+import math
 
 import jax
 import jax.numpy as jnp
 from jax import lax
 from jax.experimental import pallas as pl
 from jax.experimental.pallas import tpu as pltpu
-from jax.sharding import PartitionSpec as P
+from jax.sharding import Mesh, PartitionSpec as P
 
 LANE = 128
 VMEM = pl.BlockSpec(memory_space=pltpu.VMEM)
@@ -54,7 +55,7 @@
         o_ref[p] = x_ref[plan_ref[p]]
 
 
-def norm_body(x_ref, both_ref, rows_ref, copies_ref, scale_out_ref):
+def norm_body(x_ref, both_ref, rows_ref, normed_ref, scale_out_ref):
     blocks, rows, width = rows_ref.shape
     tiles = width // LANE
     for b in range(blocks):
@@ -63,10 +64,13 @@
         values = whole.astype(jnp.float32)
         mean_square = jnp.sum(values * values, axis=-1, keepdims=True) * (1.0 / width)
         normed = values * lax.rsqrt(mean_square + 1e-06) * both_ref[:1, :]
-        normed = normed.astype(jnp.bfloat16)
-        for t in range(copies_ref.shape[0]):
-            copies_ref[t, b] = normed
+        normed_ref[b] = normed.astype(jnp.bfloat16)
     scale_out_ref[...] = both_ref[1:, :]
+
+
+def copies_body(x_ref, o_ref):
+    for k in range(o_ref.shape[0]):
+        o_ref[k] = x_ref[...]
 
 
 def opened(ref, index, at, kept, part):
@@ -143,11 +147,11 @@
     tiles = lax.all_to_all(tiles, "section", 0, 0, tiled=True)
     tiles = call(order_body, shape, [SMEM, VMEM])(plan, tiles)
     tiles = lax.all_to_all(tiles, "section", 0, 0, tiled=True)
-    own, copies, scale = call(
+    own, normed, scale = call(
         norm_body,
         (
             jax.ShapeDtypeStruct((blocks, rows, width), bf16),
-            jax.ShapeDtypeStruct((groups, blocks, rows, width), bf16),
+            jax.ShapeDtypeStruct((blocks, rows, width), bf16),
             jax.ShapeDtypeStruct((1, width), jnp.float32),
         ),
         [VMEM, VMEM],
@@ -155,7 +159,11 @@
     )(tiles, gain_and_scale)
 
     all_rows = groups * blocks * rows
-    normed = lax.all_to_all(copies.reshape(all_rows, width), "tensor", 0, 0, tiled=True)
+    normed = lax.all_gather(normed.reshape(blocks * rows, width), "x", axis=0, tiled=True)
+    column = normed.shape[0]
+    copies = jax.ShapeDtypeStruct((all_rows // column, column, width), bf16)
+    normed = call(copies_body, copies, [VMEM])(normed)
+    normed = lax.all_to_all(normed.reshape(all_rows, width), "y", 0, 0, tiled=True)
     partial_sum = call(
         functools.partial(mlp_body, part, units),
         jax.ShapeDtypeStruct((all_rows, width), bf16),
@@ -170,7 +178,7 @@
         ],
         limit=50,
     )(normed, weights)
-    terms = lax.all_to_all(partial_sum, "tensor", 0, 0, tiled=True)
+    terms = lax.all_to_all(partial_sum, ("y", "x"), 0, 0, tiled=True)
     return call(
         sum_body,
         jax.ShapeDtypeStruct((blocks, rows, width), bf16),
@@ -179,17 +187,21 @@
 
 
 def solution(mesh):
+    sections, groups = mesh.shape["section"], mesh.shape["tensor"]
+    side = math.isqrt(groups)
+    plane = Mesh(mesh.devices.reshape(sections, groups // side, side), ("section", "x", "y"))
+    tensor = ("x", "y")
     return jax.shard_map(
-        functools.partial(local, mesh.shape["section"], mesh.shape["tensor"]),
-        mesh=mesh,
+        functools.partial(local, sections, groups),
+        mesh=plane,
         in_specs=(
-            P("section", "tensor", None),
+            P("section", tensor, None),
             P(),
             P(),
-            P("section", "tensor"),
-            P("tensor", "section"),
+            P("section", tensor),
+            P(tensor, "section"),
             P(),
         ),
-        out_specs=P("section", "tensor", None),
+        out_specs=P("section", tensor, None),
         check_vma=False,
     )

time: 140 us -> 141 us (level)
  blocking collectives: 112 us -> 114 us
    all_gather x0 -> x1, blocking collectives: none -> 12.9 us  [local(): lax.all_gather(normed.reshape(blocks * rows, width), 'x', axis=0, tiled=T...]
    all_to_all x2, blocking collectives: 58 us -> 46.7 us  [the longest x1 23.6 us: local(): lax.all_to_all(normed.reshape(all_rows, width), 'y', 0, 0, tiled=True)]
where the time goes in v11:
time: 141 us; the launch traced here: 140 us
  blocking collectives  114 us (81%)
  between operations  13.4 us (10%)
  Pallas kernels  11.1 us (8%)
    all_to_all x2, blocking collectives, local(): tiles = lax.all_to_all(tiles, 'section', 0, 0, tiled=True)  54.2 us
    all_to_all x1, blocking collectives, local(): lax.all_to_all(normed.reshape(all_rows, width), 'y', 0, 0, tiled=True)  23.6 us
    all_to_all x1, blocking collectives, local(): terms = lax.all_to_all(partial_sum, ('y', 'x'), 0, 0, tiled=True)  23.1 us
    all_gather x1, blocking collectives, local(): lax.all_gather(normed.reshape(blocks * rows, width), 'x', axis=0, tiled=T...  12.9 us
    pallas_call x1, Pallas kernels, local(): call(functools.partial(mlp_body, part, units), jax.ShapeDtypeStruct((all_...  7.51 us
  transfers between devices with their start and end apart: 1, of which 0 were waited for; matrix products, arithmetic and copies ran while one was open for 0% of the time, Pallas kernels for 1%

profile of v11, /device:TPU:6, one launch (start us, length us, event | category | flops | bytes accessed | tf_op | source)
XLA Modules:
  0.0 139.7 jit_solution(13576177144276847374)
XLA Ops:
  6.5 0.0 all-gather.3.cloned.1.call-start
  6.5 1.8 %shard_map.64 = (bf16[640,128]{1,0:T(8,128)(2,1)}, bf16[64,8,128]{2,1,0:T(8,128)(2,1)}, f32[2,3200]{1,0:T(2,128)}) custom-call(bf16[2,8,3200]{2,1,0:T(8,128)(2,1)} %x_ref.1, bf16[400,100]{1,0:T(8,128)(2,1)} %bitcast.11, bf16[400,100]{1,0:T(8,128)(2,1)} %out_ref.1, f32[3200]{0:T(1024)} %gain_ref.1, f32[3200]{0:T(1024)} %scale_ref.1), custom_call_target="tpu_custom_call" | custom-call | tf_op jit(solution)/shard_map/pallas_call | solution.py:135
  8.4 0.0 all-gather.3.cloned.1.call-update
  8.4 32.8 %all_to_all.27.x_ref = bf16[64,8,128]{2,1,0:T(8,128)(2,1)S(1)} all-to-all(bf16[64,8,128]{2,1,0:T(8,128)(2,1)} %get-tuple-element.11), channel_id=1, replica_groups=mesh['section'=32,'x'=4,'y'=4] {'section'}, dimensions={0} | all-to-all | bytes 262144 | tf_op jit(solution)/shard_map/all_to_all | solution.py:147
  41.2 0.0 copy-start.1
  41.2 0.7 copy-done.1
  41.9 0.6 shard_map.65
  42.5 21.4 %all_to_all.28.x_ref = bf16[64,8,128]{2,1,0:T(8,128)(2,1)S(1)} all-to-all(bf16[64,8,128]{2,1,0:T(8,128)(2,1)S(1)} %shard_map.65), channel_id=1, replica_groups=mesh['section'=32,'x'=4,'y'=4] {'section'}, dimensions={0} | all-to-all | bytes 262144 | tf_op jit(solution)/shard_map/all_to_all | solution.py:149
  63.9 0.0 copy-start
  63.9 0.7 copy-done
  64.6 0.1 shard_map.66
  64.7 12.9 %all_gather.9.x_ref = bf16[64,3200]{1,0:T(8,128)(2,1)S(1)} all-gather(bf16[16,3200]{1,0:T(8,128)(2,1)S(1)} %bitcast.9), channel_id=1, replica_groups=mesh['section'=32,'x'=4,'y'=4] {'x'}, dimensions={0}, use_global_device_ids=true | all-gather | bytes 512000 | tf_op jit(solution)/shard_map/all_gather | solution.py:162
  77.7 0.1 shard_map.67
  77.8 23.6 %all_to_all.29 = bf16[4,64,3200]{2,1,0:T(8,128)(2,1)S(1)} all-to-all(bf16[4,64,3200]{2,1,0:T(8,128)(2,1)S(1)} %shard_map.67), channel_id=1, replica_groups=mesh['section'=32,'x'=4,'y'=4] {'y'}, dimensions={0} | all-to-all | bytes 3276800 | tf_op jit(solution)/shard_map/all_to_all | solution.py:166
  101.4 0.0 all-gather.3.cloned.1.call-done
  101.4 7.5 %shard_map.68 = bf16[256,3200]{1,0:T(8,128)(2,1)S(1)} custom-call(bf16[256,3200]{1,0:T(8,128)(2,1)S(1)} %bitcast.7, bf16[32,640,128]{2,1,0:T(8,128)(2,1)} %bitcast.10), custom_call_target="tpu_custom_call" | custom-call | flops 1310720000 | bytes 10485760 | tf_op jit(solution)/shard_map/pallas_call | solution.py:167
  108.9 23.1 %all_to_all.30 = bf16[16,16,3200]{2,1,0:T(8,128)(2,1)S(1)} all-to-all(bf16[16,16,3200]{2,1,0:T(8,128)(2,1)S(1)} %bitcast.8), channel_id=1, replica_groups=mesh['section'=32,'x'=4,'y'=4] {'y','x'}, dimensions={0} | all-to-all | bytes 3276800 | tf_op jit(solution)/shard_map/all_to_all | solution.py:181
  132.0 0.9 shard_map.69
Async XLA Ops:
  6.5 94.9 %all-gather.3.cloned.1.call-start = ((), (), s32[]{:S(2)}) async-start(), calls=%async_computation.4 | async-start | bytes 5406720 | tf_op jit(solution)/shard_map/all_gather | solution.py:146
  41.2 0.7 copy-start.1
  63.9 0.7 copy-start
Sparse Core Ops, SparseCore 0:
  9.5 84.2 all-gather.2

commit v12 on v11

--- a/solution.py
+++ b/solution.py
@@ -55,7 +55,7 @@
         o_ref[p] = x_ref[plan_ref[p]]
 
 
-def norm_body(x_ref, both_ref, rows_ref, normed_ref, scale_out_ref):
+def norm_body(x_ref, both_ref, rows_ref, copies_ref, scale_out_ref):
     blocks, rows, width = rows_ref.shape
     tiles = width // LANE
     for b in range(blocks):
@@ -64,13 +64,10 @@
         values = whole.astype(jnp.float32)
         mean_square = jnp.sum(values * values, axis=-1, keepdims=True) * (1.0 / width)
         normed = values * lax.rsqrt(mean_square + 1e-06) * both_ref[:1, :]
-        normed_ref[b] = normed.astype(jnp.bfloat16)
+        normed = normed.astype(jnp.bfloat16)
+        for t in range(copies_ref.shape[0]):
+            copies_ref[t, b] = normed
     scale_out_ref[...] = both_ref[1:, :]
-
-
-def copies_body(x_ref, o_ref):
-    for k in range(o_ref.shape[0]):
-        o_ref[k] = x_ref[...]
 
 
 def opened(ref, index, at, kept, part):
@@ -147,11 +144,11 @@
     tiles = lax.all_to_all(tiles, "section", 0, 0, tiled=True)
     tiles = call(order_body, shape, [SMEM, VMEM])(plan, tiles)
     tiles = lax.all_to_all(tiles, "section", 0, 0, tiled=True)
-    own, normed, scale = call(
+    own, copies, scale = call(
         norm_body,
         (
             jax.ShapeDtypeStruct((blocks, rows, width), bf16),
-            jax.ShapeDtypeStruct((blocks, rows, width), bf16),
+            jax.ShapeDtypeStruct((groups, blocks, rows, width), bf16),
             jax.ShapeDtypeStruct((1, width), jnp.float32),
         ),
         [VMEM, VMEM],
@@ -159,11 +156,7 @@
     )(tiles, gain_and_scale)
 
     all_rows = groups * blocks * rows
-    normed = lax.all_gather(normed.reshape(blocks * rows, width), "x", axis=0, tiled=True)
-    column = normed.shape[0]
-    copies = jax.ShapeDtypeStruct((all_rows // column, column, width), bf16)
-    normed = call(copies_body, copies, [VMEM])(normed)
-    normed = lax.all_to_all(normed.reshape(all_rows, width), "y", 0, 0, tiled=True)
+    normed = lax.all_to_all(copies.reshape(all_rows, width), ("y", "x"), 0, 0, tiled=True)
     partial_sum = call(
         functools.partial(mlp_body, part, units),
         jax.ShapeDtypeStruct((all_rows, width), bf16),

time: 141 us -> 140 us (level)
  blocking collectives: 114 us -> 112 us
    all_gather x1 -> x0, blocking collectives: 12.9 us -> none  [local(): lax.all_gather(normed.reshape(blocks * rows, width), 'x', axis=0, tiled=T...]
    all_to_all x1, blocking collectives: 23.1 us -> 28.9 us  [local(): terms = lax.all_to_all(partial_sum, ('y', 'x'), 0, 0, tiled=True)]
    all_to_all x1, blocking collectives: 23.6 us -> 29.2 us  [local(): lax.all_to_all(copies.reshape(all_rows, width), ('y', 'x'), 0, 0, tiled=T...]
where the time goes in v12:
time: 140 us; the launch traced here: 138 us
  blocking collectives  112 us (80%)
  between operations  13.4 us (10%)
  Pallas kernels  11.1 us (8%)
    all_to_all x2, blocking collectives, local(): tiles = lax.all_to_all(tiles, 'section', 0, 0, tiled=True)  54.2 us
    all_to_all x1, blocking collectives, local(): lax.all_to_all(copies.reshape(all_rows, width), ('y', 'x'), 0, 0, tiled=T...  29.2 us
    all_to_all x1, blocking collectives, local(): terms = lax.all_to_all(partial_sum, ('y', 'x'), 0, 0, tiled=True)  28.9 us
    pallas_call x1, Pallas kernels, local(): call(functools.partial(mlp_body, part, units), jax.ShapeDtypeStruct((all_...  7.51 us
  transfers between devices with their start and end apart: 1, of which 0 were waited for; matrix products, arithmetic and copies ran while one was open for 0% of the time, Pallas kernels for 1%

profile of v12, /device:TPU:6, one launch (start us, length us, event | category | flops | bytes accessed | tf_op | source)
XLA Modules:
  0.0 138.2 jit_solution(5202704370804593340)
XLA Ops:
  6.5 0.0 all-gather.3.cloned.1.call-start
  6.5 1.8 %shard_map.64 = (bf16[640,128]{1,0:T(8,128)(2,1)}, bf16[64,8,128]{2,1,0:T(8,128)(2,1)}, f32[2,3200]{1,0:T(2,128)}) custom-call(bf16[2,8,3200]{2,1,0:T(8,128)(2,1)} %x_ref.1, bf16[400,100]{1,0:T(8,128)(2,1)} %bitcast.11, bf16[400,100]{1,0:T(8,128)(2,1)} %out_ref.1, f32[3200]{0:T(1024)} %gain_ref.1, f32[3200]{0:T(1024)} %scale_ref.1), custom_call_target="tpu_custom_call" | custom-call | tf_op jit(solution)/shard_map/pallas_call | solution.py:132
  8.4 0.0 all-gather.3.cloned.1.call-update
  8.4 32.8 %all_to_all.30.x_ref = bf16[64,8,128]{2,1,0:T(8,128)(2,1)S(1)} all-to-all(bf16[64,8,128]{2,1,0:T(8,128)(2,1)} %get-tuple-element.11), channel_id=1, replica_groups=mesh['section'=32,'x'=4,'y'=4] {'section'}, dimensions={0} | all-to-all | bytes 262144 | tf_op jit(solution)/shard_map/all_to_all | solution.py:144
  41.2 0.0 copy-start.1
  41.2 0.7 copy-done.1
  41.9 0.6 shard_map.65
  42.5 21.4 %all_to_all.31.x_ref = bf16[64,8,128]{2,1,0:T(8,128)(2,1)S(1)} all-to-all(bf16[64,8,128]{2,1,0:T(8,128)(2,1)S(1)} %shard_map.65), channel_id=1, replica_groups=mesh['section'=32,'x'=4,'y'=4] {'section'}, dimensions={0} | all-to-all | bytes 262144 | tf_op jit(solution)/shard_map/all_to_all | solution.py:146
  63.9 0.0 copy-start
  63.9 0.7 copy-done
  64.6 0.2 shard_map.66
  64.8 29.2 %all_to_all.32 = bf16[16,16,3200]{2,1,0:T(8,128)(2,1)S(1)} all-to-all(bf16[16,16,3200]{2,1,0:T(8,128)(2,1)S(1)} %bitcast.9), channel_id=1, replica_groups=mesh['section'=32,'x'=4,'y'=4] {'y','x'}, dimensions={0} | all-to-all | bytes 3276800 | tf_op jit(solution)/shard_map/all_to_all | solution.py:159
  94.0 0.0 all-gather.3.cloned.1.call-done
  94.1 7.5 %shard_map.67 = bf16[256,3200]{1,0:T(8,128)(2,1)S(1)} custom-call(bf16[256,3200]{1,0:T(8,128)(2,1)S(1)} %bitcast.7, bf16[32,640,128]{2,1,0:T(8,128)(2,1)} %bitcast.10), custom_call_target="tpu_custom_call" | custom-call | flops 1310720000 | bytes 10485760 | tf_op jit(solution)/shard_map/pallas_call | solution.py:160
  101.6 28.9 %all_to_all.33 = bf16[16,16,3200]{2,1,0:T(8,128)(2,1)S(1)} all-to-all(bf16[16,16,3200]{2,1,0:T(8,128)(2,1)S(1)} %bitcast.8), channel_id=1, replica_groups=mesh['section'=32,'x'=4,'y'=4] {'y','x'}, dimensions={0} | all-to-all | bytes 3276800 | tf_op jit(solution)/shard_map/all_to_all | solution.py:174
  130.4 0.9 shard_map.68
Async XLA Ops:
  6.5 87.5 %all-gather.3.cloned.1.call-start = ((), (), s32[]{:S(2)}) async-start(), calls=%async_computation.4 | async-start | bytes 5406720 | tf_op jit(solution)/shard_map/all_gather | solution.py:143
  41.2 0.7 copy-start.1
  63.9 0.7 copy-start
Sparse Core Ops, SparseCore 0:
  9.5 84.3 all-gather.2

commit v13 on v10

--- a/solution.py
+++ b/solution.py
@@ -122,6 +122,17 @@
         o_ref[b] = (values + scale_ref[...] * branch).astype(o_ref.dtype)
 
 
+def across_plane(x, sections, groups):
+    order = list(range(groups))
+    listed = [
+        [section * groups + t for t in (order if section % 2 == 0 else order[::-1])]
+        for section in range(sections)
+    ]
+    return lax.all_to_all(
+        x, ("section", "tensor"), 0, 0, axis_index_groups=listed, tiled=True
+    )
+
+
 def local(sections, groups, patches, plan, norm_gain, proj_in, proj_out, layer_scale):
     blocks, rows, width = patches.shape
     bf16 = jnp.bfloat16
@@ -155,7 +166,7 @@
     )(tiles, gain_and_scale)
 
     all_rows = groups * blocks * rows
-    normed = lax.all_to_all(copies.reshape(all_rows, width), "tensor", 0, 0, tiled=True)
+    normed = across_plane(copies.reshape(all_rows, width), sections, groups)
     partial_sum = call(
         functools.partial(mlp_body, part, units),
         jax.ShapeDtypeStruct((all_rows, width), bf16),
@@ -170,7 +181,7 @@
         ],
         limit=50,
     )(normed, weights)
-    terms = lax.all_to_all(partial_sum, "tensor", 0, 0, tiled=True)
+    terms = across_plane(partial_sum, sections, groups)
     return call(
         sum_body,
         jax.ShapeDtypeStruct((blocks, rows, width), bf16),

time: 140 us -> 138 us (0.986)
  blocking collectives: 112 us -> 110 us
    all_to_all x2, blocking collectives: 58 us -> 55.7 us  [across_plane(): lax.all_to_all(x, ('section', 'tensor'), 0, 0, axis_index_groups=listed,...]
    all_gather x1, waiting for transfers between devices: 0.01 us -> 1.4 us  [local(): weights = lax.all_gather(weights, 'section', axis=0, tiled=False)]
  transfers between devices with their start and end apart: 1 -> 1, of which waited for: 0 -> 1; matrix products, arithmetic and copies ran while one was open for 0% -> 0% of each run, Pallas kernels for 1% -> 1%
where the time goes in v13:
time: 138 us; the launch traced here: 137 us
  blocking collectives  110 us (80%)
  between operations  13.4 us (10%)
  Pallas kernels  11 us (8%)
  waiting for transfers between devices  1.42 us (1%)
  local copies, waits for them, and re-layouts  1.4 us (1%)
    all_to_all x2, blocking collectives, across_plane(): lax.all_to_all(x, ('section', 'tensor'), 0, 0, axis_index_groups=listed,...  55.7 us
    all_to_all x2, blocking collectives, local(): tiles = lax.all_to_all(tiles, 'section', 0, 0, tiled=True)  54.2 us
    pallas_call x1, Pallas kernels, local(): call(functools.partial(mlp_body, part, units), jax.ShapeDtypeStruct((all_...  7.5 us
  transfers between devices with their start and end apart: 1, of which 1 were waited for; matrix products, arithmetic and copies ran while one was open for 0% of the time, Pallas kernels for 1%

profile of v13, /device:TPU:6, one launch (start us, length us, event | category | flops | bytes accessed | tf_op | source)
XLA Modules:
  0.0 137.2 jit_solution(11296994214327543763)
XLA Ops:
  6.5 0.0 all-gather.3.cloned.1.call-start
  6.5 1.8 %shard_map.64 = (bf16[640,128]{1,0:T(8,128)(2,1)}, bf16[64,8,128]{2,1,0:T(8,128)(2,1)}, f32[2,3200]{1,0:T(2,128)}) custom-call(bf16[2,8,3200]{2,1,0:T(8,128)(2,1)} %x_ref.1, bf16[400,100]{1,0:T(8,128)(2,1)} %bitcast.11, bf16[400,100]{1,0:T(8,128)(2,1)} %out_ref.1, f32[3200]{0:T(1024)} %gain_ref.1, f32[3200]{0:T(1024)} %scale_ref.1), custom_call_target="tpu_custom_call" | custom-call | tf_op jit(solution)/shard_map/pallas_call | solution.py:142
  8.4 0.0 all-gather.3.cloned.1.call-update
  8.4 32.8 %all_to_all.30.x_ref = bf16[64,8,128]{2,1,0:T(8,128)(2,1)S(1)} all-to-all(bf16[64,8,128]{2,1,0:T(8,128)(2,1)} %get-tuple-element.11), channel_id=1, replica_groups=mesh['section'=32,'tensor'=16] {'section'}, dimensions={0} | all-to-all | bytes 262144 | tf_op jit(solution)/shard_map/all_to_all | solution.py:154
  41.2 0.0 copy-start.1
  41.2 0.7 copy-done.1
  41.9 0.6 shard_map.65
  42.5 21.4 %all_to_all.31.x_ref = bf16[64,8,128]{2,1,0:T(8,128)(2,1)S(1)} all-to-all(bf16[64,8,128]{2,1,0:T(8,128)(2,1)S(1)} %shard_map.65), channel_id=1, replica_groups=mesh['section'=32,'tensor'=16] {'section'}, dimensions={0} | all-to-all | bytes 262144 | tf_op jit(solution)/shard_map/all_to_all | solution.py:156
  63.9 0.0 copy-start
  63.9 0.7 copy-done
  64.6 0.2 shard_map.66
  64.8 27.6 %all_to_all.32 = bf16[16,16,3200]{2,1,0:T(8,128)(2,1)S(1)} all-to-all(bf16[16,16,3200]{2,1,0:T(8,128)(2,1)S(1)} %bitcast.9), channel_id=1, replica_groups={{0,1,2,3,4,5,6,7,8,9,10,11,12,13,14,15},{31,30,29,28,27,26,25,24,23,22,..., dimensions={0} | all-to-all | bytes 3276800 | tf_op jit(solution)/shard_map/all_to_all | solution.py:131
  92.4 1.4 %all-gather.3.cloned.1.call-done = bf16[20480,128]{1,0:T(8,128)(2,1)} async-done(((bf16[640,128]{1,0:T(8,128)(2,1)}), bf16[20480,128]{1,0:T(8,128)(2,1)}) %all-gather.3.cloned.1.call-update) | async-done | bytes 5242896 | tf_op jit(solution)/shard_map/all_gather | solution.py:153
  93.8 7.5 %shard_map.67 = bf16[256,3200]{1,0:T(8,128)(2,1)S(1)} custom-call(bf16[256,3200]{1,0:T(8,128)(2,1)S(1)} %bitcast.7, bf16[32,640,128]{2,1,0:T(8,128)(2,1)} %bitcast.10), custom_call_target="tpu_custom_call" | custom-call | flops 1310720000 | bytes 10485760 | tf_op jit(solution)/shard_map/pallas_call | solution.py:170
  101.3 28.1 %all_to_all.33 = bf16[16,16,3200]{2,1,0:T(8,128)(2,1)S(1)} all-to-all(bf16[16,16,3200]{2,1,0:T(8,128)(2,1)S(1)} %bitcast.8), channel_id=1, replica_groups={{0,1,2,3,4,5,6,7,8,9,10,11,12,13,14,15},{31,30,29,28,27,26,25,24,23,22,..., dimensions={0} | all-to-all | bytes 3276800 | tf_op jit(solution)/shard_map/all_to_all | solution.py:131
  129.5 0.9 shard_map.68
Async XLA Ops:
  6.5 87.3 %all-gather.3.cloned.1.call-start = ((), (), s32[]{:S(2)}) async-start(), calls=%async_computation.4 | async-start | bytes 5406720 | tf_op jit(solution)/shard_map/all_gather | solution.py:153
  41.2 0.7 copy-start.1
  63.9 0.7 copy-start
Sparse Core Ops, SparseCore 0:
  9.5 84.3 all-gather.2

commit v14 on v9

--- a/solution.py
+++ b/solution.py
@@ -141,6 +141,17 @@
         o_ref[b] = (values + scale_ref[...] * branch).astype(o_ref.dtype)
 
 
+def across_plane(x, sections, groups):
+    order = list(range(groups))
+    listed = [
+        [section * groups + t for t in (order if section % 2 == 0 else order[::-1])]
+        for section in range(sections)
+    ]
+    return lax.all_to_all(
+        x, ("section", "tensor"), 0, 0, axis_index_groups=listed, tiled=True
+    )
+
+
 def local(sections, groups, patches, plan, norm_gain, proj_in, proj_out, layer_scale):
     blocks, rows, width = patches.shape
     bf16 = jnp.bfloat16
@@ -174,7 +185,7 @@
     )(tiles, gain_and_scale)
 
     all_rows = groups * blocks * rows
-    normed = lax.all_to_all(copies.reshape(all_rows, width), "tensor", 0, 0, tiled=True)
+    normed = across_plane(copies.reshape(all_rows, width), sections, groups)
     spread = call(
         functools.partial(spread_body, part),
         jax.ShapeDtypeStruct((all_rows, sections * LANE), bf16),
@@ -198,7 +209,7 @@
         limit=60,
         out=ANY,
     )(spread, weights)
-    terms = lax.all_to_all(partial_sum, "tensor", 0, 0, tiled=True)
+    terms = across_plane(partial_sum, sections, groups)
     return call(
         sum_body,
         jax.ShapeDtypeStruct((blocks, rows, width), bf16),

time: 138 us -> 137 us (level)
  no operation moved by 1% of the time
where the time goes in v14:
time: 137 us
  blocking collectives  109 us (80%)
  between operations  13.4 us (10%)
  Pallas kernels  11.1 us (8%)
  local copies, waits for them, and re-layouts  2.75 us (2%)
    all_to_all x2, blocking collectives, across_plane(): lax.all_to_all(x, ('section', 'tensor'), 0, 0, axis_index_groups=listed,...  55.2 us
    all_to_all x2, blocking collectives, local(): tiles = lax.all_to_all(tiles, 'section', 0, 0, tiled=True)  54.2 us
    pallas_call x1, Pallas kernels, local(): call(functools.partial(mlp_body, part, units), jax.ShapeDtypeStruct((all_...  6.56 us
    unnamed x6, local copies, waits for them, and re-layouts  2.75 us
  transfers between devices with their start and end apart: 1, of which 0 were waited for; matrix products, arithmetic and copies ran while one was open for 0% of the time, Pallas kernels for 1%

profile of v14, /device:TPU:6, one launch (start us, length us, event | category | flops | bytes accessed | tf_op | source)
XLA Modules:
  0.0 136.7 jit_solution(15060840846084167206)
XLA Ops:
  6.5 0.0 all-gather.3.cloned.1.call-start
  6.5 1.8 %shard_map.64 = (bf16[640,128]{1,0:T(8,128)(2,1)}, bf16[64,8,128]{2,1,0:T(8,128)(2,1)}, f32[2,3200]{1,0:T(2,128)}) custom-call(bf16[2,8,3200]{2,1,0:T(8,128)(2,1)} %x_ref.1, bf16[400,100]{1,0:T(8,128)(2,1)} %bitcast.11, bf16[400,100]{1,0:T(8,128)(2,1)} %out_ref.1, f32[3200]{0:T(1024)} %gain_ref.1, f32[3200]{0:T(1024)} %scale_ref.1), custom_call_target="tpu_custom_call" | custom-call | tf_op jit(solution)/shard_map/pallas_call | solution.py:161
  8.4 0.0 all-gather.3.cloned.1.call-update
  8.4 32.8 %all_to_all.30.x_ref = bf16[64,8,128]{2,1,0:T(8,128)(2,1)S(1)} all-to-all(bf16[64,8,128]{2,1,0:T(8,128)(2,1)} %get-tuple-element.11), channel_id=1, replica_groups=mesh['section'=32,'tensor'=16] {'section'}, dimensions={0} | all-to-all | bytes 262144 | tf_op jit(solution)/shard_map/all_to_all | solution.py:173
  41.2 0.0 copy-start.2
  41.2 0.7 copy-done.2
  41.9 0.6 shard_map.65
  42.5 21.3 %all_to_all.31.x_ref = bf16[64,8,128]{2,1,0:T(8,128)(2,1)S(1)} all-to-all(bf16[64,8,128]{2,1,0:T(8,128)(2,1)S(1)} %shard_map.65), channel_id=1, replica_groups=mesh['section'=32,'tensor'=16] {'section'}, dimensions={0} | all-to-all | bytes 262144 | tf_op jit(solution)/shard_map/all_to_all | solution.py:175
  63.8 0.0 copy-start.1
  63.8 0.7 copy-done.1
  64.6 0.2 shard_map.66
  64.8 27.8 %all_to_all.32 = bf16[16,16,3200]{2,1,0:T(8,128)(2,1)S(1)} all-to-all(bf16[16,16,3200]{2,1,0:T(8,128)(2,1)S(1)} %bitcast.8), channel_id=1, replica_groups={{0,1,2,3,4,5,6,7,8,9,10,11,12,13,14,15},{31,30,29,28,27,26,25,24,23,22,..., dimensions={0} | all-to-all | bytes 3276800 | tf_op jit(solution)/shard_map/all_to_all | solution.py:150
  92.6 1.0 shard_map.67.x_hbm
  93.6 0.0 copy-start
  93.6 1.3 copy-done
  95.0 0.0 all-gather.3.cloned.1.call-done
  95.0 6.6 %shard_map.68 = bf16[256,3200]{1,0:T(8,128)(2,1)} custom-call(bf16[256,4096]{1,0:T(8,128)(2,1)} %copy-done, bf16[32,640,128]{2,1,0:T(8,128)(2,1)} %bitcast.10), custom_call_target="tpu_custom_call" | custom-call | flops 1310720000 | bytes 10485760 | tf_op jit(solution)/shard_map/pallas_call | solution.py:194
  101.6 27.4 %all_to_all.33 = bf16[16,16,3200]{2,1,0:T(8,128)(2,1)S(1)} all-to-all(bf16[16,16,3200]{2,1,0:T(8,128)(2,1)} %bitcast.9), channel_id=1, replica_groups={{0,1,2,3,4,5,6,7,8,9,10,11,12,13,14,15},{31,30,29,28,27,26,25,24,23,22,..., dimensions={0} | all-to-all | bytes 3276800 | tf_op jit(solution)/shard_map/all_to_all | solution.py:150
  129.0 0.9 shard_map.69
Async XLA Ops:
  6.5 88.4 %all-gather.3.cloned.1.call-start = ((), (), s32[]{:S(2)}) async-start(), calls=%async_computation.4 | async-start | bytes 5406720 | tf_op jit(solution)/shard_map/all_gather | solution.py:172
  41.2 0.7 copy-start.2
  63.8 0.7 copy-start.1
  93.6 1.4 copy-start
Sparse Core Ops, SparseCore 0:
  9.5 84.2 all-gather.2

commit v15 on v13

--- a/solution.py
+++ b/solution.py
@@ -69,6 +69,14 @@
     scale_out_ref[...] = both_ref[1:, :]
 
 
+def spread_body(part, x_ref, o_ref):
+    blank = jnp.zeros((x_ref.shape[0], LANE - part), x_ref.dtype)
+    for s in range(o_ref.shape[1] // LANE):
+        o_ref[:, s * LANE : (s + 1) * LANE] = jnp.concatenate(
+            [x_ref[:, s * part : (s + 1) * part], blank], axis=1
+        )
+
+
 def opened(ref, index, at, kept, part):
     fold, chunk = kept // 4, part // 4
     rest = [ref[index, at + j * fold : at + (j + 1) * fold, part : part + chunk] for j in range(4)]
@@ -76,7 +84,7 @@
     return jnp.concatenate([ref[index, at : at + kept, :], jnp.concatenate(rest, axis=1)], axis=0)
 
 
-def mlp_body(part, units, x_ref, w_hbm, o_ref, spread, held, in_sem, out_sem):
+def mlp_body(part, units, x_ref, w_hbm, o_ref, held, in_sem, out_sem):
     sections, both, _ = held.shape
     kept = both // 2
     first, second = pl.ds(0, kept), pl.ds(kept, kept)
@@ -84,17 +92,12 @@
     in_copy.start()
     out_copy = pltpu.make_async_copy(w_hbm.at[:, second], held.at[:, second], out_sem)
     out_copy.start()
-    blank = jnp.zeros((x_ref.shape[0], LANE - part), x_ref.dtype)
-    for s in range(sections):
-        spread[:, s * LANE : (s + 1) * LANE] = jnp.concatenate(
-            [x_ref[:, s * part : (s + 1) * part], blank], axis=1
-        )
     in_copy.wait()
     total = jnp.zeros((x_ref.shape[0], units), jnp.float32)
     for s in range(0, sections, 2):
         pair = [opened(held, s + k, 0, kept, part) for k in range(2)]
         total += lax.dot_general(
-            spread[:, s * LANE : (s + 2) * LANE],
+            x_ref[:, s * LANE : (s + 2) * LANE],
             jnp.concatenate(pair, axis=1),
             (((1,), (1,)), ((), ())),
             preferred_element_type=jnp.float32,
@@ -167,6 +170,11 @@
 
     all_rows = groups * blocks * rows
     normed = across_plane(copies.reshape(all_rows, width), sections, groups)
+    spread = call(
+        functools.partial(spread_body, part),
+        jax.ShapeDtypeStruct((all_rows, sections * LANE), bf16),
+        [VMEM],
+    )(normed)
     partial_sum = call(
         functools.partial(mlp_body, part, units),
         jax.ShapeDtypeStruct((all_rows, width), bf16),
@@ -174,13 +182,12 @@
         flops=4 * all_rows * width * units,
         moved=10 * 1024 * 1024,
         scratch=[
-            pltpu.VMEM((all_rows, sections * LANE), bf16),
             pltpu.VMEM((sections, 2 * kept, LANE), bf16),
             pltpu.SemaphoreType.DMA(()),
             pltpu.SemaphoreType.DMA(()),
         ],
         limit=50,
-    )(normed, weights)
+    )(spread, weights)
     terms = across_plane(partial_sum, sections, groups)
     return call(
         sum_body,

time: 138 us -> 137 us (level)
  no operation moved by 1% of the time
where the time goes in v15:
time: 137 us
  blocking collectives  110 us (80%)
  between operations  13.4 us (10%)
  Pallas kernels  11.8 us (9%)
  local copies, waits for them, and re-layouts  1.4 us (1%)
    all_to_all x2, blocking collectives, across_plane(): lax.all_to_all(x, ('section', 'tensor'), 0, 0, axis_index_groups=listed,...  55.7 us
    all_to_all x2, blocking collectives, local(): tiles = lax.all_to_all(tiles, 'section', 0, 0, tiled=True)  54.2 us
    pallas_call x1, Pallas kernels, local(): call(functools.partial(mlp_body, part, units), jax.ShapeDtypeStruct((all_...  7.2 us
  transfers between devices with their start and end apart: 1, of which 1 were waited for; matrix products, arithmetic and copies ran while one was open for 0% of the time, Pallas kernels for 1%

profile of v15, /device:TPU:6, one launch (start us, length us, event | category | flops | bytes accessed | tf_op | source)
XLA Modules:
  0.0 136.9 jit_solution(12733166482280476037)
XLA Ops:
  6.5 0.0 all-gather.3.cloned.1.call-start
  6.5 1.8 %shard_map.64 = (bf16[640,128]{1,0:T(8,128)(2,1)}, bf16[64,8,128]{2,1,0:T(8,128)(2,1)}, f32[2,3200]{1,0:T(2,128)}) custom-call(bf16[2,8,3200]{2,1,0:T(8,128)(2,1)} %x_ref.1, bf16[400,100]{1,0:T(8,128)(2,1)} %bitcast.11, bf16[400,100]{1,0:T(8,128)(2,1)} %out_ref.1, f32[3200]{0:T(1024)} %gain_ref.1, f32[3200]{0:T(1024)} %scale_ref.1), custom_call_target="tpu_custom_call" | custom-call | tf_op jit(solution)/shard_map/pallas_call | solution.py:145
  8.4 0.0 all-gather.3.cloned.1.call-update
  8.4 32.8 %all_to_all.30.x_ref = bf16[64,8,128]{2,1,0:T(8,128)(2,1)S(1)} all-to-all(bf16[64,8,128]{2,1,0:T(8,128)(2,1)} %get-tuple-element.11), channel_id=1, replica_groups=mesh['section'=32,'tensor'=16] {'section'}, dimensions={0} | all-to-all | bytes 262144 | tf_op jit(solution)/shard_map/all_to_all | solution.py:157
  41.2 0.0 copy-start.1
  41.2 0.7 copy-done.1
  41.9 0.6 shard_map.65
  42.5 21.4 %all_to_all.31.x_ref = bf16[64,8,128]{2,1,0:T(8,128)(2,1)S(1)} all-to-all(bf16[64,8,128]{2,1,0:T(8,128)(2,1)S(1)} %shard_map.65), channel_id=1, replica_groups=mesh['section'=32,'tensor'=16] {'section'}, dimensions={0} | all-to-all | bytes 262144 | tf_op jit(solution)/shard_map/all_to_all | solution.py:159
  63.9 0.0 copy-start
  63.9 0.7 copy-done
  64.6 0.2 shard_map.66
  64.8 27.6 %all_to_all.32 = bf16[16,16,3200]{2,1,0:T(8,128)(2,1)S(1)} all-to-all(bf16[16,16,3200]{2,1,0:T(8,128)(2,1)S(1)} %bitcast.9), channel_id=1, replica_groups={{0,1,2,3,4,5,6,7,8,9,10,11,12,13,14,15},{31,30,29,28,27,26,25,24,23,22,..., dimensions={0} | all-to-all | bytes 3276800 | tf_op jit(solution)/shard_map/all_to_all | solution.py:134
  92.4 1.0 shard_map.67.x_ref
  93.4 0.4 all-gather.3.cloned.1.call-done
  93.8 7.2 %shard_map.68 = bf16[256,3200]{1,0:T(8,128)(2,1)S(1)} custom-call(bf16[256,4096]{1,0:T(8,128)(2,1)S(1)} %shard_map.67.x_ref, bf16[32,640,128]{2,1,0:T(8,128)(2,1)} %bitcast.10), custom_call_target="tpu_custom_call" | custom-call | flops 1310720000 | bytes 10485760 | tf_op jit(solution)/shard_map/pallas_call | solution.py:178
  101.0 28.1 %all_to_all.33 = bf16[16,16,3200]{2,1,0:T(8,128)(2,1)S(1)} all-to-all(bf16[16,16,3200]{2,1,0:T(8,128)(2,1)S(1)} %bitcast.8), channel_id=1, replica_groups={{0,1,2,3,4,5,6,7,8,9,10,11,12,13,14,15},{31,30,29,28,27,26,25,24,23,22,..., dimensions={0} | all-to-all | bytes 3276800 | tf_op jit(solution)/shard_map/all_to_all | solution.py:134
  129.1 0.9 shard_map.69
Async XLA Ops:
  6.5 87.3 %all-gather.3.cloned.1.call-start = ((), (), s32[]{:S(2)}) async-start(), calls=%async_computation.4 | async-start | bytes 5406720 | tf_op jit(solution)/shard_map/all_gather | solution.py:156
  41.2 0.7 copy-start.1
  63.9 0.7 copy-start
Sparse Core Ops, SparseCore 0:
  9.5 84.3 all-gather.2
